TPU v7x, 32 devices: a whole 2x2x4 slice. The times are simulated.
32 devices in a mesh: gx: 4 (over y, core), gy: 4 (over z), gz: 2 (over x).
Axes of the slice: x: 2, y: 2, z: 4, core: 2. Of those that a mesh axis runs over, the one named last changes fastest.
Arguments:
- mode_shapes: bfloat16 [3, 16, 16, 32, 256], P(None, None, 'gx', 'gy', 'gz'), may hold values from -4 to 4
- stress_field: float32 [6, 16, 32, 256], P(None, 'gx', 'gy', 'gz'), may hold values from -6 to 6
- displacement: float32 [3, 16, 32, 256], P(None, 'gx', 'gy', 'gz'), may hold values from -6 to 6
- material: int32 [16, 32, 256], P('gx', 'gy', 'gz'), may hold values from 0 to 7
- fixed_nodes: int32 [16, 32, 256], P('gx', 'gy', 'gz'), may hold values 0 or 1
- eigenvalues: float32 [16], replicated, may hold values from 0.5 to 4
- mode_weight: float32 [16], replicated, may hold values from 0.2 to 1
Outputs:
- mode_sens: float32 [16, 16, 32, 256], P(None, 'gx', 'gy', 'gz')
- adjoint_term: float32 [16, 32, 256], P('gx', 'gy', 'gz')
All inputs are finite; a program needn't handle non-finite values. No bound on the sum of `fixed_nodes` on one device may be relied on, other than what follows from the above.
Results may differ from a plain program's by a relative error of at most 0.00035.
Values may be sent and summed in bfloat16 or wider, within the bound.
No kernel may reach another device: no remote copies, remote signals or barrier semaphores. Data moves between devices by JAX's collectives and lax.ppermute only.
A program may use at most 64 MiB of HBM per device.

v0:
```python
import math

import jax
import jax.numpy as jnp
import numpy as np
from jax import lax
from jax.sharding import PartitionSpec as P

LEVELS = 8


corner_list = [(a, b, c) for a in (0, 1) for b in (0, 1) for c in (0, 1)]


def shifted(block, axis, distance):
    devices = range(lax.axis_size(axis))
    route = [(i - distance, i) for i in devices if i - distance in devices]
    return lax.ppermute(block, axis, route)


def shape_value(side, point):
    return point if side else 1.0 - point


def shape_slope(side):
    return 1.0 if side else -1.0


def strain_matrix(point_x, point_y, point_z):
    deriv = np.zeros((3, 8))
    for node, (a, b, c) in enumerate(corner_list):
        value_x = shape_value(a, point_x)
        value_y = shape_value(b, point_y)
        value_z = shape_value(c, point_z)
        deriv[0, node] = shape_slope(a) * value_y * value_z
        deriv[1, node] = value_x * shape_slope(b) * value_z
        deriv[2, node] = value_x * value_y * shape_slope(c)
    matrix = np.zeros((6, 24))
    for node in range(8):
        column = 3 * node
        matrix[0, column] = deriv[0, node]
        matrix[1, column + 1] = deriv[1, node]
        matrix[2, column + 2] = deriv[2, node]
        matrix[3, column + 1] = deriv[2, node]
        matrix[3, column + 2] = deriv[1, node]
        matrix[4, column] = deriv[2, node]
        matrix[4, column + 2] = deriv[0, node]
        matrix[5, column] = deriv[1, node]
        matrix[5, column + 1] = deriv[0, node]
    return (matrix, deriv)


def tables():
    poisson = 0.45
    lame_first = poisson / ((1.0 + poisson) * (1.0 - 2.0 * poisson))
    lame_second = 0.5 / (1.0 + poisson)
    elastic = np.zeros((6, 6))
    elastic[:3, :3] = lame_first
    for axis_k in range(3):
        elastic[axis_k, axis_k] += 2.0 * lame_second
        elastic[axis_k + 3, axis_k + 3] = lame_second
    offset = 0.5 / math.sqrt(3.0)
    points = [0.5 - offset, 0.5 + offset]
    pairs = [(0, 0), (1, 1), (2, 2), (1, 2), (0, 2), (0, 1)]
    stiffness = np.zeros((24, 24))
    geometric = np.zeros((6, 24, 24))
    for point_x in points:
        for point_y in points:
            for point_z in points:
                matrix, deriv = strain_matrix(point_x, point_y, point_z)
                stiffness += 0.125 * matrix.T @ elastic @ matrix
                for comp, (first, second) in enumerate(pairs):
                    outer = np.outer(deriv[first], deriv[second])
                    if first != second:
                        outer = outer + outer.T
                    geometric[comp] += 0.125 * np.kron(outer, np.eye(3))
    center, unused = strain_matrix(0.5, 0.5, 0.5)
    coupling = elastic @ center
    return (
        jnp.asarray(stiffness, jnp.float32),
        jnp.asarray(geometric, jnp.float32),
        jnp.asarray(coupling, jnp.float32),
    )


def element_block(node_slab, cell_data, eigenvalues, mode_weight, k_base, g_base, coupling):
    highest = lax.Precision.HIGHEST
    mode_count = node_slab.shape[1]
    count_y = cell_data.shape[1]
    count_z = cell_data.shape[2]
    total = count_y * count_z
    width = -(-total // 128) * 128
    pieces = [node_slab[:, :, a, b : b + count_y, c : c + count_z] for a, b, c in corner_list]
    dofs = jnp.stack(pieces, 0).reshape(24, mode_count, total)
    big_table = jnp.concatenate([k_base[None], g_base], 0).reshape(168, 24)
    products = jnp.einsum("rs,sme->rme", big_table, dofs, precision=highest).reshape(
        7, 24, mode_count, width
    )
    forms = jnp.sum(products * dofs[None], 1)
    energy = forms[0]
    quad = forms[1:]
    flat_cells = cell_data.reshape(9, total)
    projected = jnp.einsum("ce,cme->me", flat_cells[:6], quad, precision=highest)
    sensitivity = flat_cells[7] * energy - eigenvalues[:, None] * flat_cells[8] * projected
    coefficient = jnp.einsum("m,cme->ce", mode_weight * eigenvalues, quad, precision=highest)
    forces = -flat_cells[6] * jnp.dot(coupling.T, coefficient, precision=highest)
    return (sensitivity.reshape(mode_count, count_y, count_z), forces.reshape(24, count_y, count_z))


def element_term(node_slab, slope_layer, k_base):
    count_y = slope_layer.shape[0]
    count_z = slope_layer.shape[1]
    pieces = jnp.stack(
        [node_slab[:, a, b : b + count_y, c : c + count_z] for a, b, c in corner_list], 0
    )
    load_dofs = pieces[:, :3].reshape(24, count_y * count_z)
    disp_dofs = pieces[:, 3:].reshape(24, count_y * count_z)
    product = jnp.dot(k_base, disp_dofs, precision=lax.Precision.HIGHEST)
    return slope_layer * jnp.sum(load_dofs * product, 0).reshape(count_y, count_z)


def assemble(forces):
    assembled = None
    for corner, (a, b, c) in enumerate(corner_list):
        portion = jnp.transpose(forces[:, 3 * corner : 3 * corner + 3], (1, 0, 2, 3))
        portion = jnp.pad(portion, ((0, 0), (a, 1 - a), (b, 1 - b), (c, 1 - c)))
        assembled = portion if assembled is None else assembled + portion
    return assembled


def body(mode_shapes, stress_field, displacement, material, fixed_nodes, eigenvalues, mode_weight):
    k_base, g_base, coupling = tables()
    count_x, count_y, count_z = material.shape
    density = (material.astype(jnp.float32) + 1.0) / LEVELS
    young_mod = 0.001 + density**3
    slope_mod = 3.0 * density**2
    ratio_mod = slope_mod / young_mod
    cell_data = jnp.concatenate(
        [stress_field, young_mod[None], slope_mod[None], ratio_mod[None]], 0
    )
    free_mask = 1.0 - fixed_nodes.astype(jnp.float32)
    whole_load = None
    upper = mode_shapes
    upper = jnp.concatenate([upper, shifted(upper[:, :, :1], "gx", -1)], 2)
    upper = jnp.concatenate([upper, shifted(upper[:, :, :, :1], "gy", -1)], 3)
    upper = jnp.concatenate([upper, shifted(upper[:, :, :, :, :1], "gz", -1)], 4)

    def layer_own(index):
        node_slab = lax.dynamic_slice_in_dim(upper, index, 2, 2).astype(jnp.float32)
        cells_now = lax.dynamic_index_in_dim(cell_data, index, 1, keepdims=False)
        return element_block(
            node_slab, cells_now, eigenvalues, mode_weight, k_base, g_base, coupling
        )

    sensitivity, forces = lax.map(layer_own, jnp.arange(count_x))
    mode_sens = jnp.transpose(sensitivity, (1, 0, 2, 3))
    partial_value = assemble(forces)
    incoming = shifted(partial_value[:, :, :, count_z:], "gz", 1)
    partial_value = jnp.concatenate(
        [partial_value[:, :, :, :1] + incoming, partial_value[:, :, :, 1:count_z]], 3
    )
    incoming = shifted(partial_value[:, :, count_y:], "gy", 1)
    partial_value = jnp.concatenate(
        [partial_value[:, :, :1] + incoming, partial_value[:, :, 1:count_y]], 2
    )
    incoming = shifted(partial_value[:, count_x:], "gx", 1)
    load = jnp.concatenate([partial_value[:, :1] + incoming, partial_value[:, 1:count_x]], 1)
    load = load * free_mask
    stacked = jnp.concatenate([load, displacement], 0)
    stacked = jnp.concatenate([stacked, shifted(stacked[:, :1], "gx", -1)], 1)
    stacked = jnp.concatenate([stacked, shifted(stacked[:, :, :1], "gy", -1)], 2)
    stacked = jnp.concatenate([stacked, shifted(stacked[:, :, :, :1], "gz", -1)], 3)
    whole_load = stacked

    def term_at(index):
        node_slab = lax.dynamic_slice_in_dim(whole_load, index, 2, 1)
        slope_layer = lax.dynamic_index_in_dim(slope_mod, index, 0, keepdims=False)
        return element_term(node_slab, slope_layer, k_base)

    adjoint_term = lax.map(term_at, jnp.arange(count_x))
    return (mode_sens, adjoint_term)


def solution(mesh):
    return jax.shard_map(
        body,
        mesh=mesh,
        in_specs=(
            P(None, None, "gx", "gy", "gz"),
            P(None, "gx", "gy", "gz"),
            P(None, "gx", "gy", "gz"),
            P("gx", "gy", "gz"),
            P("gx", "gy", "gz"),
            P(),
            P(),
        ),
        out_specs=(P(None, "gx", "gy", "gz"), P("gx", "gy", "gz")),
        check_vma=False,
    )
```

profile of v0, /device:TPU:0, one launch (start us, length us, event | category | flops | bytes accessed | tf_op | source)
XLA Modules:
  0.0 171.5 jit_solution(7530559346815399489)
XLA Ops:
  0.6 0.9 slice.175
  1.6 1.3 collective-permute-start
  2.9 0.7 multiply_multiply_fusion
  3.6 0.7 mul.101
  4.3 1.0 constant_dynamic-update-slice_fusion.1
  5.5 1.3 collective-permute-start.1
  6.8 4.4 %copy.33 = bf16[3,16,5,8,128]{1,0,4,3,2:T(4,128)(2,1)} copy(bf16[3,16,5,8,128]{4,3,2,1,0:T(8,128)(2,1)S(1)} %constant_dynamic-update-slice_fusion) | data formatting | bytes 983040 | tf_op jit(solution)/shard_map/concatenate | solution.py:144
  11.2 1.4 collective-permute-done.1
  12.6 0.3 copy.34
  13.0 1.0 fusion.35
  13.9 1.4 collective-permute-start.2
  15.5 7.3 %pad_maximum_fusion = bf16[3,16,5,9,128]{1,0,4,3,2:T(4,128)(2,1)} fusion(bf16[3,16,5,1,128]{1,0,4,3,2:T(4,128)(2,1)S(1)} %copy.34, bf16[3,16,5,8,128]{1,0,4,3,2:T(4,128)(2,1)S(1)} %copy-done), kind=kLoop, calls=%fused_computation.66 | loop fusion | flops 276480 | bytes 1105920 | tf_op jit(solution)/shard_map/concatenate | solution.py:145
  22.7 6.8 %copy.35 = bf16[3,16,5,9,128]{4,1,3,2,0:T(8,128)(2,1)S(1)} copy(bf16[3,16,5,9,128]{1,0,4,3,2:T(4,128)(2,1)} %pad_maximum_fusion) | data formatting | bytes 1105920 | tf_op jit(solution)/shard_map/concatenate | solution.py:145
  29.5 0.9 copy.36
  30.4 1.3 pad_maximum_fusion.1
  31.7 83.8 %while.28 = (s32[]{:T(128)}, f32[4,16,8,128]{3,2,0,1:T(8,128)}, f32[4,24,8,128]{3,2,1,0:T(8,128)}, s32[4]{0:T(128)S(1)}, f32[9,4,8,128]{3,2,1,0:T(8,128)S(1)}, /...) while((s32[]{:T(128)}, f32[4,16,8,128]{3,2,0,1:T(8,128)}, ...), condition=%wide.region_2.3_spmd.clone.clone, body=%wide.region_0.2_spmd.sunk.clone.clone.sunk | while | flops 801445760 | bytes 20248736 | solution.py:155
  31.7 0.6 dynamic_slice.51
  34.0 1.1 constant_dynamic-slice_fusion.2
  36.3 1.4 reshape.69
  37.7 11.1 %fusion.107 = f32[7,16,1024]{2,0,1:T(8,128)S(1)} fusion(f32[24,16,1024]{2,0,1:T(8,128)S(1)} %reshape.68, f32[7,24,24,1]{2,1,0,3:T(8,128)S(1)} %get-tuple-element.433, f32[24,16,1024,1]{2,0,1,3:T(8,128)} %reshape.69), kind=kOutput, calls=%fused_computation.24.clone.1 | convolution fusion | flops 798113792 | bytes 3620608 | tf_op jit(solution)/shard_map/while/body/eval_jaxpr/rs,sme->rme/dot_general | solution.py:96
  49.0 0.6 fusion.111
  50.7 0.3 fusion.112
  51.0 0.6 bitcast_dynamic-update-slice_fusion.2
  52.0 0.6 fusion.110
  52.7 0.6 dynamic_slice.51
  54.9 1.1 constant_dynamic-slice_fusion.2
  57.3 1.4 reshape.69
  58.7 11.1 %fusion.107 = f32[7,16,1024]{2,0,1:T(8,128)S(1)} fusion(f32[24,16,1024]{2,0,1:T(8,128)S(1)} %reshape.68, f32[7,24,24,1]{2,1,0,3:T(8,128)S(1)} %get-tuple-element.433, f32[24,16,1024,1]{2,0,1,3:T(8,128)} %reshape.69), kind=kOutput, calls=%fused_computation.24.clone.1 | convolution fusion | flops 798113792 | bytes 3620608 | tf_op jit(solution)/shard_map/while/body/eval_jaxpr/rs,sme->rme/dot_general | solution.py:96
  69.9 0.6 fusion.111
  71.9 0.7 bitcast_dynamic-update-slice_fusion.2
  73.0 0.6 fusion.110
  73.6 0.6 dynamic_slice.51
  75.9 1.1 constant_dynamic-slice_fusion.2
  78.2 1.4 reshape.69
  79.6 11.1 %fusion.107 = f32[7,16,1024]{2,0,1:T(8,128)S(1)} fusion(f32[24,16,1024]{2,0,1:T(8,128)S(1)} %reshape.68, f32[7,24,24,1]{2,1,0,3:T(8,128)S(1)} %get-tuple-element.433, f32[24,16,1024,1]{2,0,1,3:T(8,128)} %reshape.69), kind=kOutput, calls=%fused_computation.24.clone.1 | convolution fusion | flops 798113792 | bytes 3620608 | tf_op jit(solution)/shard_map/while/body/eval_jaxpr/rs,sme->rme/dot_general | solution.py:96
  90.8 0.6 fusion.111
  92.9 0.6 bitcast_dynamic-update-slice_fusion.2
  93.9 0.6 fusion.110
  94.5 0.6 dynamic_slice.51
  96.8 1.1 constant_dynamic-slice_fusion.2
  99.1 1.4 reshape.69
  100.5 11.1 %fusion.107 = f32[7,16,1024]{2,0,1:T(8,128)S(1)} fusion(f32[24,16,1024]{2,0,1:T(8,128)S(1)} %reshape.68, f32[7,24,24,1]{2,1,0,3:T(8,128)S(1)} %get-tuple-element.433, f32[24,16,1024,1]{2,0,1,3:T(8,128)} %reshape.69), kind=kOutput, calls=%fused_computation.24.clone.1 | convolution fusion | flops 798113792 | bytes 3620608 | tf_op jit(solution)/shard_map/while/body/eval_jaxpr/rs,sme->rme/dot_general | solution.py:96
  111.8 0.6 fusion.111
  113.8 0.6 bitcast_dynamic-update-slice_fusion.2
  114.8 0.6 fusion.110
  115.5 1.0 slice_bitcast_fusion.15
  116.8 4.5 %collective-permute-start.3 = (f32[3,5,9,1]{3,2,0,1:T(8,128)S(1)}, f32[3,5,9,1]{3,2,0,1:T(8,128)S(1)}, u32[]{:S(2)}, u32[]{:S(2)}) collective-permute-start(f32[3,5,9,1]{3,2,0,1:T(8,128)S(1)} %slice.279), channel_id=1, source_target_pairs={{0,1},{2,3},{4,5},{6,7},{8,9},{10,11},{12,13},{14,15},{16,17},{18,... | collective-permute-start | bytes 1628 | tf_op jit(solution)/shard_map/ppermute | solution.py:18
  121.3 2.7 %collective-permute-done.3 = f32[3,5,9,1]{3,2,0,1:T(8,128)S(1)} collective-permute-done((f32[3,5,9,1]{3,2,0,1:T(8,128)S(1)}, f32[3,5,9,1]{3,2,0,1:T(8,128)S(1)}, u32[]{:S(2)}, u32[]{:S(2)}) %collective-permute-start.3) | collective-permute-done | bytes 572 | tf_op jit(solution)/shard_map/ppermute | solution.py:18
  124.2 4.1 %collective-permute-start.4 = (f32[3,5,1,128]{3,2,0,1:T(1,128)S(1)}, f32[3,5,1,128]{3,2,0,1:T(1,128)S(1)}, u32[]{:S(2)}, u32[]{:S(2)}) collective-permute-start(f32[3,5,1,128]{3,2,0,1:T(1,128)S(1)} %pad_maximum_fusion.10), channel_id=1, source_target_pairs={{0,2},{2,4},{4,6},{1,3},{3,5},{5,7},{8,10},{10,12},{12,14},{9,11},... | collective-permute-start | bytes 23048 | tf_op jit(solution)/shard_map/ppermute | solution.py:18
  128.3 1.3 collective-permute-done.4
  129.8 2.1 %collective-permute-start.5 = (f32[3,1,8,128]{3,2,0,1:T(8,128)S(1)}, f32[3,1,8,128]{3,2,0,1:T(8,128)S(1)}, u32[]{:S(2)}, u32[]{:S(2)}) collective-permute-start(f32[3,1,8,128]{3,2,0,1:T(8,128)S(1)} %slice.282), channel_id=1, source_target_pairs={{0,8},{8,16},{16,24},{1,9},{9,17},{17,25},{2,10},{10,18},{18,26},{... | collective-permute-start | bytes 36872 | tf_op jit(solution)/shard_map/ppermute | solution.py:18
  132.0 0.8 collective-permute-done.5
  132.8 1.3 collective-permute-start.6
  134.1 3.7 %collective-permute-done.6 = f32[6,1,8,128]{3,2,0,1:T(8,128)S(1)} collective-permute-done((f32[6,1,8,128]{3,2,0,1:T(8,128)S(1)}, f32[6,1,8,128]{3,2,0,1:T(8,128)S(1)}, u32[]{:S(2)}, u32[]{:S(2)}) %collective-permute-start.6) | collective-permute-done | bytes 24608 | tf_op jit(solution)/shard_map/ppermute | solution.py:18
  137.8 1.3 collective-permute-start.7
  139.1 4.6 %collective-permute-done.7 = f32[6,5,1,128]{3,2,0,1:T(1,128)S(1)} collective-permute-done((f32[6,5,1,128]{3,2,0,1:T(1,128)S(1)}, f32[6,5,1,128]{3,2,0,1:T(1,128)S(1)}, u32[]{:S(2)}, u32[]{:S(2)}) %collective-permute-start.7) | collective-permute-done | bytes 15392 | tf_op jit(solution)/shard_map/ppermute | solution.py:18
  143.7 1.3 collective-permute-start.8
  145.0 8.0 %collective-permute-done.8 = f32[6,5,9,1]{3,2,0,1:T(8,128)S(1)} collective-permute-done((f32[6,5,9,1]{3,2,0,1:T(8,128)S(1)}, f32[6,5,9,1]{3,2,0,1:T(8,128)S(1)}, u32[]{:S(2)}, u32[]{:S(2)}) %collective-permute-start.8) | collective-permute-done | bytes 1112 | tf_op jit(solution)/shard_map/ppermute | solution.py:18
  153.1 17.8 %while.27 = (s32[]{:T(128)}, f32[4,8,128]{2,1,0:T(8,128)S(1)}, s32[4]{0:T(128)S(1)}, f32[4,8,128]{2,1,0:T(8,128)S(1)}, f32[6,5,9,129]{3,2,0,1:T(8,128)S(1)}, /*i...) while((s32[]{:T(128)}, f32[4,8,128]{2,1,0:T(8,128)S(1)}, ...), condition=%wide.region_5.6_spmd.clone, body=%wide.region_3.5_spmd.sunk.clone.sunk | while | flops 7127049 | bytes 1001996 | solution.py:180
  153.1 0.6 dynamic_slice.49
  157.5 0.6 dynamic_slice.49
  162.0 0.6 dynamic_slice.49
  166.4 0.6 dynamic_slice.49
  170.9 0.6 copy-done.7
  (171 shorter events, 10.9 us)
Async XLA Ops:
  0.6 6.1 %copy-start.4 = (f32[6,4,8,128]{3,2,1,0:T(8,128)S(1)}, f32[6,4,8,128]{3,2,1,0:T(8,128)}, u32[]{:S(2)}) copy-start(f32[6,4,8,128]{3,2,1,0:T(8,128)} %param.15) | copy-start | bytes 294916
  1.6 3.7 %collective-permute-start = (bf16[3,16,1,8,128]{4,3,2,1,0:T(8,128)(2,1)S(1)}, bf16[3,16,1,8,128]{4,3,2,1,0:T(8,128)(2,1)S(1)}, u32[]{:S(2)}, u32[]{:S(2)}) collective-permute-start(bf16[3,16,1,8,128]{4,3,2,1,0:T(8,128)(2,1)S(1)} %slice.175), channel_id=1, source_target_pairs={{8,0},{16,8},{24,16},{9,1},{17,9},{25,17},{10,2},{18,10},{26,18},{... | collective-permute-start | bytes 294920 | tf_op jit(solution)/shard_map/ppermute | solution.py:18
  5.5 7.1 %collective-permute-start.1 = (bf16[3,16,5,1,128]{4,1,3,2,0:T(8,128)(2,1)S(1)}, bf16[3,16,5,1,128]{4,1,3,2,0:T(8,128)(2,1)S(1)}, u32[]{:S(2)}, u32[]{:S(2)}) collective-permute-start(bf16[3,16,5,1,128]{4,1,3,2,0:T(8,128)(2,1)S(1)} %copy.54), channel_id=1, source_target_pairs={{2,0},{4,2},{6,4},{3,1},{5,3},{7,5},{10,8},{12,10},{14,12},{11,9},... | collective-permute-start | bytes 184328 | tf_op jit(solution)/shard_map/ppermute | solution.py:18
  12.9 2.5 %copy-start = (bf16[3,16,5,8,128]{1,0,4,3,2:T(4,128)(2,1)S(1)}, bf16[3,16,5,8,128]{1,0,4,3,2:T(4,128)(2,1)}, u32[]{:S(2)}) copy-start(bf16[3,16,5,8,128]{1,0,4,3,2:T(4,128)(2,1)} %copy.33) | copy-start | bytes 1474564
  13.9 15.6 %collective-permute-start.2 = (bf16[3,16,5,9,1]{1,0,4,3,2:T(4,128)(2,1)S(1)}, bf16[3,16,5,9,1]{1,0,4,3,2:T(4,128)(2,1)S(1)}, u32[]{:S(2)}, u32[]{:S(2)}) collective-permute-start(bf16[3,16,5,9,1]{1,0,4,3,2:T(4,128)(2,1)S(1)} %fusion.35), channel_id=1, source_target_pairs={{1,0},{3,2},{5,4},{7,6},{9,8},{11,10},{13,12},{15,14},{17,16},{19,... | collective-permute-start | bytes 12968 | tf_op jit(solution)/shard_map/ppermute | solution.py:18
  29.5 2.2 %copy-start.3 = (f32[6,24]{1,0:T(8,128)S(1)}, f32[6,24]{1,0:T(8,128)}, u32[]{:S(2)}) copy-start(f32[6,24]{1,0:T(8,128)} %constant.73.clone..sunk.3) | copy-start | bytes 1732
  29.5 2.2 %copy-start.6 = (f32[16]{0:T(128)S(1)}, f32[16]{0:T(128)}, u32[]{:S(2)}) copy-start(f32[16]{0:T(128)} %param.19) | copy-start | bytes 196
  29.5 2.2 %copy-start.8 = (f32[7,24,24,1]{2,1,0,3:T(8,128)S(1)}, f32[7,24,24,1]{2,1,0,3:T(8,128)}, u32[]{:S(2)}) copy-start(f32[7,24,24,1]{2,1,0,3:T(8,128)} %constant.249) | copy-start | bytes 48388
  115.5 16.5 %copy-start.5 = (s32[4,8,128]{2,1,0:T(8,128)S(1)}, s32[4,8,128]{2,1,0:T(8,128)}, u32[]{:S(2)}) copy-start(s32[4,8,128]{2,1,0:T(8,128)} %param.18) | copy-start | bytes 49156
  115.5 17.3 %copy-start.1 = (f32[3,4,8,128]{3,2,1,0:T(8,128)S(1)}, f32[3,4,8,128]{3,2,1,0:T(8,128)}, u32[]{:S(2)}) copy-start(f32[3,4,8,128]{3,2,1,0:T(8,128)} %param.16) | copy-start | bytes 147460
  116.8 36.3 %copy-start.2 = (f32[24,24]{1,0:T(8,128)S(1)}, f32[24,24]{1,0:T(8,128)}, u32[]{:S(2)}) copy-start(f32[24,24]{1,0:T(8,128)} %constant.71.clone..sunk.2) | copy-start | bytes 6916
  116.8 7.3 %collective-permute-start.3 = (f32[3,5,9,1]{3,2,0,1:T(8,128)S(1)}, f32[3,5,9,1]{3,2,0,1:T(8,128)S(1)}, u32[]{:S(2)}, u32[]{:S(2)}) collective-permute-start(f32[3,5,9,1]{3,2,0,1:T(8,128)S(1)} %slice.279), channel_id=1, source_target_pairs={{0,1},{2,3},{4,5},{6,7},{8,9},{10,11},{12,13},{14,15},{16,17},{18,... | collective-permute-start | bytes 1628 | tf_op jit(solution)/shard_map/ppermute | solution.py:18
  124.2 5.4 %collective-permute-start.4 = (f32[3,5,1,128]{3,2,0,1:T(1,128)S(1)}, f32[3,5,1,128]{3,2,0,1:T(1,128)S(1)}, u32[]{:S(2)}, u32[]{:S(2)}) collective-permute-start(f32[3,5,1,128]{3,2,0,1:T(1,128)S(1)} %pad_maximum_fusion.10), channel_id=1, source_target_pairs={{0,2},{2,4},{4,6},{1,3},{3,5},{5,7},{8,10},{10,12},{12,14},{9,11},... | collective-permute-start | bytes 23048 | tf_op jit(solution)/shard_map/ppermute | solution.py:18
  129.8 3.0 %collective-permute-start.5 = (f32[3,1,8,128]{3,2,0,1:T(8,128)S(1)}, f32[3,1,8,128]{3,2,0,1:T(8,128)S(1)}, u32[]{:S(2)}, u32[]{:S(2)}) collective-permute-start(f32[3,1,8,128]{3,2,0,1:T(8,128)S(1)} %slice.282), channel_id=1, source_target_pairs={{0,8},{8,16},{16,24},{1,9},{9,17},{17,25},{2,10},{10,18},{18,26},{... | collective-permute-start | bytes 36872 | tf_op jit(solution)/shard_map/ppermute | solution.py:18
  132.8 5.0 %collective-permute-start.6 = (f32[6,1,8,128]{3,2,0,1:T(8,128)S(1)}, f32[6,1,8,128]{3,2,0,1:T(8,128)S(1)}, u32[]{:S(2)}, u32[]{:S(2)}) collective-permute-start(f32[6,1,8,128]{3,2,0,1:T(8,128)S(1)} %pad_maximum_fusion.7), channel_id=1, source_target_pairs={{8,0},{16,8},{24,16},{9,1},{17,9},{25,17},{10,2},{18,10},{26,18},{... | collective-permute-start | bytes 73736 | tf_op jit(solution)/shard_map/ppermute | solution.py:18
  137.8 5.9 %collective-permute-start.7 = (f32[6,5,1,128]{3,2,0,1:T(1,128)S(1)}, f32[6,5,1,128]{3,2,0,1:T(1,128)S(1)}, u32[]{:S(2)}, u32[]{:S(2)}) collective-permute-start(f32[6,5,1,128]{3,2,0,1:T(1,128)S(1)} %pad_maximum_fusion.8), channel_id=1, source_target_pairs={{2,0},{4,2},{6,4},{3,1},{5,3},{7,5},{10,8},{12,10},{14,12},{11,9},... | collective-permute-start | bytes 46088 | tf_op jit(solution)/shard_map/ppermute | solution.py:18
  143.7 9.3 %collective-permute-start.8 = (f32[6,5,9,1]{3,2,0,1:T(8,128)S(1)}, f32[6,5,9,1]{3,2,0,1:T(8,128)S(1)}, u32[]{:S(2)}, u32[]{:S(2)}) collective-permute-start(f32[6,5,9,1]{3,2,0,1:T(8,128)S(1)} %pad_maximum_fusion.3), channel_id=1, source_target_pairs={{1,0},{3,2},{5,4},{7,6},{9,8},{11,10},{13,12},{15,14},{17,16},{19,... | collective-permute-start | bytes 3248 | tf_op jit(solution)/shard_map/ppermute | solution.py:18
  170.9 0.6 copy-start.7
where the time goes:
time: 174 us; the launch traced here: 171 us
  matrix products  48.8 us (28%)
  local copies, waits for them, and re-layouts  42.3 us (24%)
  loops' own time  24.7 us (14%)
  waiting for transfers between devices  22.5 us (13%)
  starting transfers between devices  18.5 us (11%)
  other arithmetic  13.6 us (8%)
    dot_general x4, matrix products, element_block(): jnp.einsum('rs,sme->rme', big_table, dofs, precision=highest)  44.6 us
    ppermute x9, waiting for transfers between devices, shifted(): return lax.ppermute(block, axis, route)  22.5 us
    ppermute x9, starting transfers between devices, shifted(): return lax.ppermute(block, axis, route)  18.5 us
    another operation x1, loops' own time, body(): adjoint_term = lax.map(term_at, jnp.arange(count_x))  12.7 us
    another operation x1, loops' own time, body(): sensitivity, forces = lax.map(layer_own, jnp.arange(count_x))  12 us
    concatenate x2, other arithmetic, body(): upper = jnp.concatenate([upper, shifted(upper[:, :, :, :1], 'gy', -1)], 3)  8.22 us
    concatenate x1, local copies, waits for them, and re-layouts, body(): upper = jnp.concatenate([upper, shifted(upper[:, :, :, :1], 'gy', -1)], 3)  6.79 us
    reshape x8, local copies, waits for them, and re-layouts, element_block(): dofs = jnp.stack(pieces, 0).reshape(24, mode_count, total)  6.54 us
  transfers between devices with their start and end apart: 9, of which 7 were waited for; matrix products, arithmetic and copies ran while one was open for 12% of the time, Pallas kernels for 0%

commit v1 on v0

v1 whole, which is shorter than its diff:
```python
import functools
import math

import jax
import jax.numpy as jnp
from jax import lax
from jax.experimental import pallas as pl
from jax.experimental.pallas import tpu as pltpu
from jax.sharding import PartitionSpec as P

LEVELS = 8
POISSON = 0.45
LAM = POISSON / ((1.0 + POISSON) * (1.0 - 2.0 * POISSON))
MU = 0.5 / (1.0 + POISSON)
R3 = 1.0 / math.sqrt(3.0)
F32 = jnp.float32
BF16 = jnp.bfloat16
MODES = 16
GROUPS = 4
LANES = 128


def lane_iota(shape=(MODES, LANES)):
    return lax.broadcasted_iota(jnp.int32, shape, len(shape) - 1)


def row_iota(shape):
    return lax.broadcasted_iota(jnp.int32, shape, 0)


def roll(value, shift, axis=1):
    size = value.shape[axis]
    if isinstance(shift, int):
        shift = shift % size
        if shift == 0:
            return value
    return pltpu.roll(value, shift, axis)


def place(axis):
    me = lax.axis_index(axis)
    size = lax.axis_size(axis)
    even = lax.rem(me, 2) == 0
    return even, me > 0, me < size - 1


def pack_kernel(dims, modes, material, fixed, disp, tiles, x1, x2, edge, ex1, ex2, raw):
    nx, ny = dims
    span = MODES * nx * ny
    part = nx * ny
    for c in range(3):
        raw[c * span : (c + 1) * span, :] = modes[c].astype(F32).reshape(span, LANES)
    base = 3 * span

    def channel(index, value):
        raw[base + index * part : base + (index + 1) * part, :] = value.reshape(part, LANES)

    channel(0, material[...].astype(F32) + 1.0)
    channel(1, 1.0 - fixed[...].astype(F32))
    for c in range(3):
        value = disp[c]
        head = value.astype(BF16).astype(F32)
        channel(2 + c, head)
        channel(5 + c, value - head)
    raw[base + 8 * part : base + 16 * part, :] = jnp.zeros((8 * part, LANES), F32)
    lane = lane_iota()

    @pl.loop(0, GROUPS * nx)
    def _(step):
        c = step // nx
        x = lax.rem(step, nx)
        row = c * span + x * ny
        ends = jnp.zeros((MODES, LANES), F32)
        for y in range(ny):
            value = raw[pl.ds(row + y, MODES, stride=part), :]
            tiles[c, x, y] = value.astype(BF16)
            ends = jnp.where((lane >= 3 * y) & (lane < 3 * y + 3), roll(value, 3 * y + 1), ends)
        edge[c, x] = ends.astype(BF16)

    even, _, _ = place("gx")
    for out, out_edge, upward in ((x1, ex1, even), (x2, ex2, jnp.logical_not(even))):
        for s in range(2):
            layer = jnp.where(upward, nx - 1, s)
            for c in range(GROUPS):
                out[c, s] = tiles[c, layer]
                out_edge[c, s] = edge[c, layer]


def pick(parity, lower, upper, first, second, use_lower, use_upper, none_lower, none_upper):
    odd = jnp.logical_not(parity)
    pl.when(jnp.logical_and(lower, parity))(lambda: use_lower(second))
    pl.when(jnp.logical_and(lower, odd))(lambda: use_lower(first))
    pl.when(jnp.logical_and(upper, parity))(lambda: use_upper(first))
    pl.when(jnp.logical_and(upper, odd))(lambda: use_upper(second))
    pl.when(jnp.logical_not(lower))(none_lower)
    pl.when(jnp.logical_not(upper))(none_upper)


def merge_kernel(dims, zcount, *refs):
    nx, ny = dims
    tiles, r1, r2 = refs[:3]
    rz = refs[3 : 3 + zcount]
    rz1 = refs[3 + zcount : 3 + 2 * zcount]
    rz2 = refs[3 + 2 * zcount : 3 + 3 * zcount]
    full, rim, y1, y2 = refs[3 + 3 * zcount :]
    xe, xlo, xup = place("gx")
    ze, zlo, zup = place("gz")
    ye, _, _ = place("gy")
    full[:, 1 : nx + 1] = tiles[...]

    def lower(ref):
        full[:, 0:1] = ref[:, 0:1]

    def upper(ref):
        full[:, nx + 1 : nx + 3] = ref[...]

    def no_lower():
        full[:, 0:1] = jnp.zeros_like(full[:, 0:1])

    def no_upper():
        full[:, nx + 1 : nx + 3] = jnp.zeros_like(full[:, nx + 1 : nx + 3])

    pick(xe, xlo, xup, r1, r2, lower, upper, no_lower, no_upper)

    lane = lane_iota()
    phase = lax.rem(lane, 3)
    even_f = ze.astype(F32)
    lo_f = zlo.astype(F32)
    up_f = zup.astype(F32)

    def merged(blocks):
        if len(blocks) == 1:
            first = blocks[0].astype(F32)
            return first * jnp.where(phase == 0, lo_f, up_f)
        first, second = (b.astype(F32) for b in blocks)
        low = (second * even_f + first * (1.0 - even_f)) * lo_f
        high = (first * even_f + second * (1.0 - even_f)) * up_f
        return jnp.where(phase == 0, low, high)

    for c in range(GROUPS):
        for x in range(nx):
            rim[c, x + 1] = merged([r[c, x] for r in rz])

        def rim_lower(refs, c=c):
            rim[c, 0] = merged([r[c, 0] for r in refs])

        def rim_upper(refs, c=c):
            for s in range(2):
                rim[c, nx + 1 + s] = merged([r[c, s] for r in refs])

        def rim_no_lower(c=c):
            rim[c, 0] = jnp.zeros((MODES, LANES), F32)

        def rim_no_upper(c=c):
            for s in range(2):
                rim[c, nx + 1 + s] = jnp.zeros((MODES, LANES), F32)

        pick(xe, xlo, xup, rz1, rz2, rim_lower, rim_upper, rim_no_lower, rim_no_upper)

    width = nx + 3
    for out, upward in ((y1, ye), (y2, jnp.logical_not(ye))):
        rows = [jnp.where(upward, ny - 1, s) for s in range(2)]
        for c in range(GROUPS):
            ends = jnp.zeros((MODES, LANES), F32)
            for x in range(width):
                for s in range(2):
                    out[(c * width + x) * 2 + s] = full[c, x, rows[s]]
                    start = 16 * x + 3 * s
                    turned = roll(rim[c, x], lax.rem(start + LANES - 3 * rows[s], LANES))
                    ends = jnp.where((lane >= start) & (lane < start + 3), turned, ends)
            out[GROUPS * width * 2 + c] = ends.astype(BF16)


def cross_xy(a, b):
    return a[0] * b[1] + a[4] * b[5]


def cross_xz(a, b):
    return a[0] * b[2] + a[3] * b[5]


def cross_yz(a, b):
    return a[1] * b[2] + a[3] * b[4]


def squares(a):
    f, g, h, t = a[3] * a[3], a[4] * a[4], a[5] * a[5], a[6] * a[6]
    ft = f + t
    return (a[0] * a[0] + (ft + g), a[1] * a[1] + (ft + h), a[2] * a[2] + ((g + t) + h))


def combos(now, after):
    return (
        now[1] + after[1],
        after[0] - now[0],
        now[2] + after[2],
        (after[1] - now[1]) * R3,
        (now[3] + after[3]) * R3,
        (after[2] - now[2]) * R3,
        (after[3] - now[3]) * (1.0 / 3.0),
    )


def forms(parts, with_energy):
    own = [squares(p) for p in parts]
    quad = [own[0][i] + own[1][i] + own[2][i] for i in range(3)]
    for f in (cross_yz, cross_xz, cross_xy):
        quad.append(f(parts[0], parts[0]) + f(parts[1], parts[1]) + f(parts[2], parts[2]))
    if not with_energy:
        return quad, None
    x, y, z = parts
    energy = (
        MU * (quad[0] + quad[1] + quad[2])
        + (LAM + MU) * (own[0][0] + own[1][1] + own[2][2])
        + (2.0 * LAM) * (cross_xy(x, y) + cross_xz(x, z) + cross_yz(y, z))
        + (2.0 * MU) * (cross_xy(y, x) + cross_xz(z, x) + cross_yz(z, y))
    )
    return quad, energy


def bilinear(l, d):
    total = None
    diagonal = None
    for p in range(3):
        prod = [l[p][i] * d[p][i] for i in range(7)]
        ft = prod[3] + prod[6]
        three = (
            prod[0] + (ft + prod[4]),
            prod[1] + (ft + prod[5]),
            prod[2] + ((prod[4] + prod[6]) + prod[5]),
        )
        whole = three[0] + three[1] + three[2]
        total = whole if total is None else total + whole
        diagonal = three[p] if diagonal is None else diagonal + three[p]
    lx, ly, lz = l
    dx, dy, dz = d
    mixed = (
        (cross_xy(lx, dy) + cross_xy(dx, ly))
        + (cross_xz(lx, dz) + cross_xz(dx, lz))
        + (cross_yz(ly, dz) + cross_yz(dy, lz))
    )
    shear = (
        (cross_xy(dy, lx) + cross_xy(ly, dx))
        + (cross_xz(dz, lx) + cross_xz(lz, dx))
        + (cross_yz(dz, ly) + cross_yz(lz, dy))
    )
    return MU * total + (LAM + MU) * diagonal + LAM * mixed + MU * shear


def fold_rows(values):
    row = row_iota((8, LANES))
    top = row < 4
    step = [
        jnp.where(top, values[k], values[k + 4]) + roll(jnp.where(top, values[k + 4], values[k]), 4, 0)
        for k in range(4)
    ]
    top = lax.rem(row, 4) < 2
    step = [
        jnp.where(top, step[k] + roll(step[k], 6, 0), step[k + 2] + roll(step[k + 2], 2, 0)) for k in range(2)
    ]
    return jnp.where(lax.rem(row, 2) == 0, step[0] + roll(step[0], 7, 0), step[1] + roll(step[1], 1, 0))


def final_kernel(dims, full, rim, r1, r2, stress, eig, weight, sens, adjoint, yrim, zrim, sz, dz, part, w, zt, aux, cell, shear, load, stage):
    nx, ny = dims
    width = nx + 3
    tall = ny + 3
    lane = lane_iota()
    ye, ylo, yup = place("gy")

    count = GROUPS * width

    def lower(ref):
        for i in range(count):
            yrim[i, 0] = ref[2 * i]
        for c in range(GROUPS):
            yrim[count + c, 0] = ref[2 * count + c]

    def upper(ref):
        for i in range(count):
            yrim[i, 1] = ref[2 * i]
            yrim[i, 2] = ref[2 * i + 1]
        for c in range(GROUPS):
            yrim[count + c, 1] = ref[2 * count + c]

    def no_lower():
        yrim[:, 0] = jnp.zeros_like(yrim[:, 0])

    def no_upper():
        yrim[:, 1] = jnp.zeros_like(yrim[:, 1])
        yrim[:, 2] = jnp.zeros_like(yrim[:, 2])

    pick(ye, ylo, yup, r1, r2, lower, upper, no_lower, no_upper)

    @pl.loop(0, width)
    def _(x):
        for c in range(GROUPS):
            ends = roll(rim[c, x], 3)
            ends = jnp.where(lane < 3, roll(yrim[count + c, 0].astype(F32), lax.rem(2 * LANES - 16 * x, LANES)), ends)
            far = 3 * (ny + 1)
            ends = jnp.where(
                lane >= far, roll(yrim[count + c, 1].astype(F32), lax.rem(2 * LANES + far - 16 * x, LANES)), ends
            )
            for y in range(tall):
                if y == 0:
                    value = yrim[c * width + x, 0]
                elif y <= ny:
                    value = full[c, x, y - 1]
                else:
                    value = yrim[c * width + x, y - ny]
                value = value.astype(F32)
                start = 3 * tall + y
                if c < 3:
                    after = roll(value, LANES - 1)
                    after = jnp.where(lane == LANES - 1, roll(ends, LANES - 1 - (3 * y + 1)), after)
                    sz[c, x, y] = value + after
                    dz[c, x, y] = after - value
                else:
                    aux[pl.ds((x * 16 + y) * 16, 16), :] = value
                ends = jnp.where(lane == start, roll(value, start), ends)
            zrim[c, x] = ends

    def field(channel, x, first, rows):
        return aux[pl.ds((x * 16 + first) * 16 + channel, rows, stride=16), :]

    for c in range(GROUPS):
        stacked = zrim[c].reshape(width * 16, LANES)
        stacked = jnp.concatenate([stacked, jnp.zeros((LANES - width * 16, LANES), F32)], 0)
        zt[c] = stacked.T

    mode_row = lax.broadcasted_iota(jnp.int32, (MODES, LANES), 0)
    mode_lane = lax.rem(lax.broadcasted_iota(jnp.int32, (16, LANES), 1), MODES)
    eig_rows = jnp.zeros((MODES, LANES), F32)
    coef_rows = jnp.zeros((MODES, LANES), F32)
    coef_lanes = jnp.zeros((16, LANES), F32)
    for m in range(MODES):
        product = eig[m] * weight[m]
        eig_rows = jnp.where(mode_row == m, eig[m], eig_rows)
        coef_rows = jnp.where(mode_row == m, product, coef_rows)
        coef_lanes = jnp.where(mode_lane == m, product, coef_lanes)

    for x in range(nx):
        level = field(0, x + 1, 1, ny)
        density = level * (1.0 / LEVELS)
        young = 0.001 + density * density * density
        slope = 3.0 * density * density
        ratio = slope / young
        cell[6, x] = slope * (1.0 / 16.0)
        for c in range(6):
            cell[c, x] = stress[c, x] * ratio * (-1.0 / 16.0 if c < 3 else -1.0 / 8.0)

    def row_parts(x, y, h):
        found = []
        for c in range(3):
            s0 = sz[c, x, y, pl.ds(8 * h, 8), :]
            s1 = sz[c, x + 1, y, pl.ds(8 * h, 8), :]
            d0 = dz[c, x, y, pl.ds(8 * h, 8), :]
            d1 = dz[c, x + 1, y, pl.ds(8 * h, 8), :]
            found.append((s0 + s1, s1 - s0, d0 + d1, d1 - d0))
        return found

    def sweep(x, inside):
        for h in range(2):
            coef = coef_rows[8 * h : 8 * h + 8]
            now = row_parts(x, 0, h)
            for y in range(ny + 2):
                after = row_parts(x, y + 1, h)
                own = inside and 0 < y <= ny
                quad, energy = forms([combos(now[c], after[c]) for c in range(3)], own)
                if own:
                    fields = [cell[i, x - 1, pl.ds(y - 1, 1), :] for i in range(7)]
                    terms = [fields[i] * quad[i] for i in range(6)]
                    total = ((terms[0] + terms[1]) + (terms[2] + terms[3])) + (terms[4] + terms[5])
                    value = fields[6] * energy + eig_rows[8 * h : 8 * h + 8] * total
                    sens[pl.ds(8 * h * nx * ny + (x - 1) * ny + y - 1, 8, stride=nx * ny), :] = value
                for i in range(6):
                    if h == 0:
                        part[i, y] = coef * quad[i]
                    else:
                        part[i, y] += coef * quad[i]
                now = after
        for i in range(6):
            w[i, x, 0:8, 0:LANES] = fold_rows([part[i, y] for y in range(8)])
            for y in range(8, ny + 2):
                w[i, x, y : y + 1, 0:LANES] = jnp.sum(part[i, y], axis=0, keepdims=True)

    @pl.loop(1, nx + 1)
    def _(x):
        sweep(x, True)

    @pl.loop(0, 2)
    def _(i):
        sweep(i * (nx + 1), False)

    def end_nodes(c, kind, y):
        if kind == 3:
            return zt[c, pl.ds(3 * tall + y, 16), :]
        return zt[c, pl.ds(3 * y + kind, 16, stride=3), :]

    def end_parts(low, high, y):
        found = []
        for c in range(3):
            first, second = end_nodes(c, low, y), end_nodes(c, high, y)
            s, d = first + second, second - first
            s_next, d_next = roll(s, LANES - 16), roll(d, LANES - 16)
            found.append((s + s_next, s_next - s, d + d_next, d_next - d))
        return found

    sides = []
    for low, high in ((0, 3), (1, 2)):
        now, after = end_parts(low, high, 0), end_parts(low, high, 1)
        quad, _ = forms([combos(now[c], after[c]) for c in range(3)], False)
        summed = []
        for value in quad:
            value = value * coef_lanes
            for shift in (1, 2, 4, 8):
                value = value + roll(value, LANES - shift)
            summed.append(value)
        sides.append(summed)
    for i in range(6):
        both = jnp.where(lax.rem(lane, 16) == 0, sides[1][i], roll(sides[0][i], LANES - 1))
        for x in range(nx + 2):
            w[i, x, 0:16, LANES:] = roll(both, LANES - 16 * x)

    def end_field(channel, x, first, with_low):
        value = roll(zt[3, pl.ds(3 * first + 1, 16, stride=3), :], LANES - (16 * x + channel))
        if not with_low:
            return value
        low = roll(zt[3, pl.ds(3 * first, 16, stride=3), :], LANES - 1 - (16 * x + channel))
        return jnp.where(lane == 0, value, jnp.where(lane == LANES - 1, low, 0.0))

    def z_back(main, end):
        turned, turned_end = roll(main, 1), roll(end, 1)
        return jnp.where(lane == 0, turned_end, turned), jnp.where(lane == 0, turned, turned_end)

    first_rows = [None] * 6
    for x in range(nx + 2):
        level = (field(0, x, 0, 16), end_field(0, x, 0, True))
        scaled = []
        for t in range(2):
            density = level[t] * (1.0 / LEVELS)
            young = 0.001 + density * density * density
            young = jnp.where(level[t] > 0.0, young, 0.0) * (1.0 / 64.0)
            value = [w[i, x, 0:16, LANES * t : LANES * (t + 1)] * young for i in range(6)]
            trace = LAM * (value[0] + value[1] + value[2])
            scaled.append(
                [trace + (2.0 * MU) * value[i] for i in range(3)] + [(2.0 * MU) * value[i] for i in range(3, 6)]
            )
        sums, diffs = [], []
        for i in range(6):
            main, end = scaled[0][i], scaled[1][i]
            back_main, back_end = z_back(main, end)
            sums.append((main + back_main, end + back_end))
            diffs.append((main - back_main, end - back_end))
        xx, yy, zz, yz, xz, xy = range(6)
        for slot, source in enumerate((sums[xx], sums[xy], diffs[xz], sums[yy], diffs[yz], sums[xz], sums[yz], diffs[zz])):
            for t in range(2):
                shear[slot, t, 0:16] = source[t]
        rows = []
        for t in range(2):
            low = [shear[slot, t, 0:16] for slot in range(8)]
            high = [shear[slot, t, 1:17] for slot in range(8)]
            plus = lambda k: low[k] + high[k]
            minus = lambda k: high[k] - low[k]
            rows.append(
                [
                    plus(0),
                    minus(1) + plus(2),
                    plus(1),
                    minus(3) + plus(4),
                    plus(5),
                    minus(6) + plus(7),
                ]
            )
        if x > 0:
            node = x - 1
            for t in range(2):
                free = field(1, x, 1, 16) if t == 0 else end_field(1, x, 1, False)
                for p in range(3):
                    value = (rows[t][2 * p] - first_rows[t][2 * p]) + (rows[t][2 * p + 1] + first_rows[t][2 * p + 1])
                    load[p, node, t] = value * free
                    if t == 0:
                        shift = field(2 + p, x, 1, 16) + field(5 + p, x, 1, 16)
                    else:
                        shift = end_field(2 + p, x, 1, False) + end_field(5 + p, x, 1, False)
                    load[3 + p, node, t] = shift
        first_rows = rows

    def node_layer(x):
        found = []
        for f in range(6):
            main, end = load[f, x, 0], load[f, x, 1]
            after = jnp.where(lane == LANES - 1, roll(end, LANES - 1), roll(main, LANES - 1))
            s, d = main + after, after - main
            stage[0, 0:16] = s
            stage[1, 0:16] = d
            s_next, d_next = stage[0, 1:9], stage[1, 1:9]
            s, d = s[0:8], d[0:8]
            found.append((s + s_next, s_next - s, d + d_next, d_next - d))
        return found

    def layer_combos(now, after):
        return (
            after[0] - now[0],
            now[1] + after[1],
            now[2] + after[2],
            (after[1] - now[1]) * R3,
            (after[2] - now[2]) * R3,
            (now[3] + after[3]) * R3,
            (after[3] - now[3]) * (1.0 / 3.0),
        )

    now = node_layer(0)
    for x in range(nx):
        after = node_layer(x + 1)
        parts = [layer_combos(now[f], after[f]) for f in range(6)]
        adjoint[x] = cell[6, x] * bilinear(parts[:3], parts[3:])
        now = after


def partner(index, size, kind):
    other = index ^ 1 if kind == 1 else ((index + 1) ^ 1) - 1
    return other if 0 <= other < size else None


def swap(block, axes, kinds, fill):
    sizes = [lax.axis_size(a) for a in axes]
    route = []
    for i in range(sizes[0]):
        for j in range(sizes[1]):
            ends = [p if k == 0 else partner(p, n, k) for p, n, k in zip((i, j), sizes, kinds, strict=True)]
            if ends[0] is None:
                ends = [i, partner(j, sizes[1], 1)] if fill else None
            elif ends[1] is None:
                ends = [partner(i, sizes[0], 1) if kinds[0] == 0 else ends[0], j] if fill else None
            if ends is not None:
                route.append((i * sizes[1] + j, ends[0] * sizes[1] + ends[1]))
    return lax.ppermute(block, axes, route)


def vmem(n):
    return [pl.BlockSpec(memory_space=pltpu.VMEM)] * n


def body(mode_shapes, stress_field, displacement, material, fixed_nodes, eigenvalues, mode_weight):
    nx, ny, nz = material.shape
    dims = (nx, ny)
    width = nx + 3
    tall = ny + 3
    sds = jax.ShapeDtypeStruct
    tile = (MODES, LANES)
    tiles, x1, x2, edge, ex1, ex2 = pl.pallas_call(
        functools.partial(pack_kernel, dims),
        out_shape=(
            sds((GROUPS, nx, ny) + tile, BF16),
            sds((GROUPS, 2, ny) + tile, BF16),
            sds((GROUPS, 2, ny) + tile, BF16),
            sds((GROUPS, nx) + tile, BF16),
            sds((GROUPS, 2) + tile, BF16),
            sds((GROUPS, 2) + tile, BF16),
        ),
        in_specs=vmem(4),
        out_specs=tuple(vmem(6)),
        scratch_shapes=[pltpu.VMEM((GROUPS * MODES * nx * ny, LANES), F32)],
        compiler_params=pltpu.CompilerParams(vmem_limit_bytes=8 << 20),
        name="pack",
    )(mode_shapes, material, fixed_nodes, displacement)

    xz = ("gx", "gz")
    zkinds = (1,) if lax.axis_size("gz") == 2 else (1, 2)
    r1 = swap(x1, xz, (1, 0), True)
    r2 = swap(x2, xz, (2, 0), True)
    rz = [swap(edge, xz, (0, k), True) for k in zkinds]
    rz1 = [swap(ex1, xz, (1, k), True) for k in zkinds]
    rz2 = [swap(ex2, xz, (2, k), True) for k in zkinds]
    count = GROUPS * width * 2 + GROUPS
    full, rim, y1, y2 = pl.pallas_call(
        functools.partial(merge_kernel, dims, len(zkinds)),
        out_shape=(
            sds((GROUPS, width, ny) + tile, BF16),
            sds((GROUPS, width) + tile, F32),
            sds((count,) + tile, BF16),
            sds((count,) + tile, BF16),
        ),
        in_specs=vmem(3 + 3 * len(zkinds)),
        out_specs=tuple(vmem(4)),
        compiler_params=pltpu.CompilerParams(vmem_limit_bytes=8 << 20),
        name="merge",
    )(tiles, r1, r2, *rz, *rz1, *rz2)

    yz = ("gy", "gz")
    ry1 = swap(y1, yz, (1, 0), True)
    ry2 = swap(y2, yz, (2, 0), True)
    sens, adjoint = pl.pallas_call(
        functools.partial(final_kernel, dims),
        out_shape=(sds((MODES * nx * ny, LANES), F32), sds((nx, ny, LANES), F32)),
        in_specs=vmem(5) + [pl.BlockSpec(memory_space=pltpu.SMEM)] * 2,
        out_specs=tuple(vmem(2)),
        scratch_shapes=[
            pltpu.VMEM((GROUPS * width + GROUPS, 3) + tile, BF16),
            pltpu.VMEM((GROUPS, width) + tile, F32),
            pltpu.VMEM((3, width, tall) + tile, F32),
            pltpu.VMEM((3, width, tall) + tile, F32),
            pltpu.VMEM((6, ny + 2, 8, LANES), F32),
            pltpu.VMEM((6, nx + 2, 16, 2 * LANES), F32),
            pltpu.VMEM((GROUPS, LANES, LANES), F32),
            pltpu.VMEM(((width + 1) * 16 * 16, LANES), F32),
            pltpu.VMEM((7, nx, ny, LANES), F32),
            pltpu.VMEM((8, 2, 24, LANES), F32),
            pltpu.VMEM((6, nx + 1, 2, 16, LANES), F32),
            pltpu.VMEM((2, 24, LANES), F32),
        ],
        compiler_params=pltpu.CompilerParams(vmem_limit_bytes=32 << 20),
        name="finish",
    )(full, rim, ry1, ry2, stress_field, eigenvalues, mode_weight)
    return sens.reshape(MODES, nx, ny, nz), adjoint


def solution(mesh):
    return jax.shard_map(
        body,
        mesh=mesh,
        in_specs=(
            P(None, None, "gx", "gy", "gz"),
            P(None, "gx", "gy", "gz"),
            P(None, "gx", "gy", "gz"),
            P("gx", "gy", "gz"),
            P("gx", "gy", "gz"),
            P(),
            P(),
        ),
        out_specs=(P(None, "gx", "gy", "gz"), P("gx", "gy", "gz")),
        check_vma=False,
    )
```

time: 174 us -> 38.5 us (0.22); the launches traced: 171 us -> 38.2 us
  matrix products: 48.8 us -> 0 us
  local copies, waits for them, and re-layouts: 42.3 us -> 3.89 us
  loops' own time: 24.7 us -> 0 us
  Pallas kernels: 0 us -> 14.1 us
  other arithmetic: 13.6 us -> 0 us
  waiting for transfers between devices: 22.5 us -> 9.75 us
  starting transfers between devices: 18.5 us -> 9.73 us
    dot_general x16 -> x0, matrix products: 48.8 us -> none  [the longest x4 44.6 us: element_block(): jnp.einsum('rs,sme->rme', big_table, dofs, precision=highest)]
    another operation x2 -> x0, loops' own time: 24.7 us -> none  [the longest x1 12.7 us: body(): adjoint_term = lax.map(term_at, jnp.arange(count_x))]
    pallas_call x0 -> x3, Pallas kernels: none -> 14.1 us  [the longest x1 11.8 us: body(): pl.pallas_call(functools.partial(final_kernel, dims), out_shape=(sds((MOD...]
    ppermute x9 -> x7, waiting for transfers between devices: 22.5 us -> 9.75 us  [swap(): return lax.ppermute(block, axes, route)]
    concatenate x3 -> x0, local copies, waits for them, and re-layouts: 11.2 us -> none  [the longest x1 6.79 us: body(): upper = jnp.concatenate([upper, shifted(upper[:, :, :, :1], 'gy', -1)], 3)]
    concatenate x9 -> x0, other arithmetic: 9.67 us -> none  [the longest x2 8.22 us: body(): upper = jnp.concatenate([upper, shifted(upper[:, :, :, :1], 'gy', -1)], 3)]
    dynamic_slice x12 -> x0, local copies, waits for them, and re-layouts: 9.09 us -> none  [the longest x8 4.89 us: body(): sensitivity, forces = lax.map(layer_own, jnp.arange(count_x))]
    ppermute x9 -> x7, starting transfers between devices: 18.5 us -> 9.73 us  [swap(): return lax.ppermute(block, axes, route)]
  transfers between devices with their start and end apart: 9 -> 7, of which waited for: 7 -> 4; matrix products, arithmetic and copies ran while one was open for 12% -> 0% of each run, Pallas kernels for 0% -> 0%
where the time goes in v1:
time: 38.5 us; the launch traced here: 38.2 us
  Pallas kernels  14.1 us (37%)
  waiting for transfers between devices  9.75 us (25%)
  starting transfers between devices  9.73 us (25%)
  local copies, waits for them, and re-layouts  3.89 us (10%)
  between operations  0.67 us (2%)
    pallas_call x1, Pallas kernels, body(): pl.pallas_call(functools.partial(final_kernel, dims), out_shape=(sds((MOD...  11.8 us
    ppermute x7, waiting for transfers between devices, swap(): return lax.ppermute(block, axes, route)  9.75 us
    ppermute x7, starting transfers between devices, swap(): return lax.ppermute(block, axes, route)  9.73 us
    unnamed x14, local copies, waits for them, and re-layouts  3.89 us
    pallas_call x1, Pallas kernels, body(): pl.pallas_call(functools.partial(pack_kernel, dims), out_shape=(sds((GROU...  1.94 us
  transfers between devices with their start and end apart: 7, of which 4 were waited for; matrix products, arithmetic and copies ran while one was open for 0% of the time, Pallas kernels for 0%

profile of v1, /device:TPU:0, one launch (start us, length us, event | category | flops | bytes accessed | tf_op | source)
XLA Modules:
  0.0 38.2 jit_solution(8360653601889986108)
XLA Ops:
  0.6 0.0 copy-start
  0.6 1.0 %copy-done = bf16[3,16,4,8,128]{4,3,2,1,0:T(8,128)(2,1)S(1)} copy-done((bf16[3,16,4,8,128]{4,3,2,1,0:T(8,128)(2,1)S(1)}, bf16[3,16,4,8,128]{4,3,2,1,0:T(8,128)(2,1)}, u32[]{:S(2)}) %copy-start) | copy-done | bytes 393240
  1.6 0.0 copy-start.2
  1.6 0.8 %copy-done.2 = f32[3,4,8,128]{3,2,1,0:T(8,128)S(1)} copy-done((f32[3,4,8,128]{3,2,1,0:T(8,128)S(1)}, f32[3,4,8,128]{3,2,1,0:T(8,128)}, u32[]{:S(2)}) %copy-start.2) | copy-done | bytes 49176
  2.4 0.0 copy-start.3
  2.4 0.7 %copy-done.3 = s32[4,8,128]{2,1,0:T(8,128)S(1)} copy-done((s32[4,8,128]{2,1,0:T(8,128)S(1)}, s32[4,8,128]{2,1,0:T(8,128)}, u32[]{:S(2)}) %copy-start.3) | copy-done | bytes 16408
  3.1 0.0 copy-start.4
  3.1 0.7 %copy-done.4 = s32[4,8,128]{2,1,0:T(8,128)S(1)} copy-done((s32[4,8,128]{2,1,0:T(8,128)S(1)}, s32[4,8,128]{2,1,0:T(8,128)}, u32[]{:S(2)}) %copy-start.4) | copy-done | bytes 16408
  3.9 1.9 %pack.1 = (bf16[4,4,8,16,128]{4,3,2,1,0:T(8,128)(2,1)S(1)}, bf16[4,2,8,16,128]{4,3,2,1,0:T(8,128)(2,1)S(1)}, bf16[4,2,8,16,128]{4,3,2,1,0:T(8,128)(2,1)S(1)}, bf...) custom-call(bf16[3,16,4,8,128]{4,3,2,1,0:T(8,128)(2,1)S(1)} %copy-done, ...), custom_call_target="tpu_custom_call" | custom-call | tf_op jit(solution)/shard_map/pack/pallas_call | solution.py:552
  5.8 0.5 %collective-permute-start = (bf16[4,2,8,16,128]{4,3,2,1,0:T(8,128)(2,1)S(1)}, bf16[4,2,8,16,128]{4,3,2,1,0:T(8,128)(2,1)S(1)}, u32[]{:S(2)}, u32[]{:S(2)}) collective-permute-start(bf16[4,2,8,16,128]{4,3,2,1,0:T(8,128)(2,1)S(1)} %get-tuple-element.15), channel_id=1, source_target_pairs={{0,8},{1,9},{8,0},{9,1},{16,24},{17,25},{24,16},{25,17},{2,10},{3,... | collective-permute-start | bytes 786440 | tf_op jit(solution)/shard_map/ppermute | solution.py:538
  6.3 2.6 %collective-permute-start.1 = (bf16[4,2,8,16,128]{4,3,2,1,0:T(8,128)(2,1)S(1)}, bf16[4,2,8,16,128]{4,3,2,1,0:T(8,128)(2,1)S(1)}, u32[]{:S(2)}, u32[]{:S(2)}) collective-permute-start(bf16[4,2,8,16,128]{4,3,2,1,0:T(8,128)(2,1)S(1)} %get-tuple-element.16), channel_id=1, source_target_pairs={{0,1},{1,0},{8,16},{9,17},{16,8},{17,9},{24,25},{25,24},{2,3},{3,2... | collective-permute-start | bytes 786440 | tf_op jit(solution)/shard_map/ppermute | solution.py:538
  8.9 0.1 collective-permute-start.2
  9.0 1.4 %collective-permute-start.3 = (bf16[4,2,16,128]{3,2,1,0:T(8,128)(2,1)S(1)}, bf16[4,2,16,128]{3,2,1,0:T(8,128)(2,1)S(1)}, u32[]{:S(2)}, u32[]{:S(2)}) collective-permute-start(bf16[4,2,16,128]{3,2,1,0:T(8,128)(2,1)S(1)} %get-tuple-element.18), channel_id=1, source_target_pairs={{0,9},{1,8},{8,1},{9,0},{16,25},{17,24},{24,17},{25,16},{2,11},{3,... | collective-permute-start | bytes 98312 | tf_op jit(solution)/shard_map/ppermute | solution.py:538
  10.4 1.5 %collective-permute-start.4 = (bf16[4,2,16,128]{3,2,1,0:T(8,128)(2,1)S(1)}, bf16[4,2,16,128]{3,2,1,0:T(8,128)(2,1)S(1)}, u32[]{:S(2)}, u32[]{:S(2)}) collective-permute-start(bf16[4,2,16,128]{3,2,1,0:T(8,128)(2,1)S(1)} %get-tuple-element.19), channel_id=1, source_target_pairs={{0,1},{1,0},{8,17},{9,16},{16,9},{17,8},{24,25},{25,24},{2,3},{3,2... | collective-permute-start | bytes 98312 | tf_op jit(solution)/shard_map/ppermute | solution.py:538
  11.9 3.4 %collective-permute-done.3.refs_4_ = bf16[4,2,16,128]{3,2,1,0:T(8,128)(2,1)S(1)} collective-permute-done((bf16[4,2,16,128]{3,2,1,0:T(8,128)(2,1)S(1)}, bf16[4,2,16,128]{3,2,1,0:T(8,128)(2,1)S(1)}, u32[]{:S(2)}, u32[]{:S(2)}) %collective-permute-start.3) | collective-permute-done | bytes 32800 | tf_op jit(solution)/shard_map/ppermute | solution.py:538
  15.2 0.8 %collective-permute-done.4.refs_5_ = bf16[4,2,16,128]{3,2,1,0:T(8,128)(2,1)S(1)} collective-permute-done((bf16[4,2,16,128]{3,2,1,0:T(8,128)(2,1)S(1)}, bf16[4,2,16,128]{3,2,1,0:T(8,128)(2,1)S(1)}, u32[]{:S(2)}, u32[]{:S(2)}) %collective-permute-start.4) | collective-permute-done | bytes 32800 | tf_op jit(solution)/shard_map/ppermute | solution.py:538
  16.0 0.0 collective-permute-done.2.refs_3_
  16.0 0.0 collective-permute-done.refs_1_
  16.1 0.0 collective-permute-done.1.refs_2_
  16.1 0.0 copy-start.1
  16.1 0.4 %merge.1 = (bf16[4,7,8,16,128]{4,3,2,1,0:T(8,128)(2,1)S(1)}, f32[4,7,16,128]{3,2,1,0:T(8,128)S(1)}, bf16[60,16,128]{2,1,0:T(8,128)(2,1)S(1)}, bf16[60,16,128]{2,1,0:T(8,128)(2,1)S(1)}) custom-call(bf16[4,4,8,16,128]{4,3,2,1,0:T(8,128)(2,1)S(1)} %get-tuple-element.14.refs_0_, bf16[4,2,8,16,128]{4,3,2,1,0:T(8,128)(2,1)S(1)} %collective-permute-done.refs_1_, ...), custom_call_target="tpu_custom_call" | custom-call | tf_op jit(solution)/shard_map/merge/pallas_call | solution.py:577
  16.5 2.2 %collective-permute-start.5 = (bf16[60,16,128]{2,1,0:T(8,128)(2,1)S(1)}, bf16[60,16,128]{2,1,0:T(8,128)(2,1)S(1)}, u32[]{:S(2)}, u32[]{:S(2)}) collective-permute-start(bf16[60,16,128]{2,1,0:T(8,128)(2,1)S(1)} %get-tuple-element.22), channel_id=1, source_target_pairs={{0,2},{1,3},{2,0},{3,1},{4,6},{5,7},{6,4},{7,5},{8,10},{9,11},{10,... | collective-permute-start | bytes 737288 | tf_op jit(solution)/shard_map/ppermute | solution.py:538
  18.6 1.5 %collective-permute-start.6 = (bf16[60,16,128]{2,1,0:T(8,128)(2,1)S(1)}, bf16[60,16,128]{2,1,0:T(8,128)(2,1)S(1)}, u32[]{:S(2)}, u32[]{:S(2)}) collective-permute-start(bf16[60,16,128]{2,1,0:T(8,128)(2,1)S(1)} %get-tuple-element.23), channel_id=1, source_target_pairs={{0,1},{1,0},{2,4},{3,5},{4,2},{5,3},{6,7},{7,6},{8,9},{9,8},{10,12... | collective-permute-start | bytes 737288 | tf_op jit(solution)/shard_map/ppermute | solution.py:538
  20.1 4.1 %collective-permute-done.5.r1 = bf16[60,16,128]{2,1,0:T(8,128)(2,1)S(1)} collective-permute-done((bf16[60,16,128]{2,1,0:T(8,128)(2,1)S(1)}, bf16[60,16,128]{2,1,0:T(8,128)(2,1)S(1)}, u32[]{:S(2)}, u32[]{:S(2)}) %collective-permute-start.5) | collective-permute-done | bytes 245792 | tf_op jit(solution)/shard_map/ppermute | solution.py:538
  24.2 1.5 %collective-permute-done.6.r2 = bf16[60,16,128]{2,1,0:T(8,128)(2,1)S(1)} collective-permute-done((bf16[60,16,128]{2,1,0:T(8,128)(2,1)S(1)}, bf16[60,16,128]{2,1,0:T(8,128)(2,1)S(1)}, u32[]{:S(2)}, u32[]{:S(2)}) %collective-permute-start.6) | collective-permute-done | bytes 245792 | tf_op jit(solution)/shard_map/ppermute | solution.py:538
  25.7 0.0 copy-start.5
  25.7 0.0 copy-start.6
  25.7 0.0 copy-done.1
  25.7 0.6 %copy-done.5 = f32[16]{0:T(128)S(1)} copy-done((f32[16]{0:T(128)S(1)}, f32[16]{0:T(128)}, u32[]{:S(2)}) %copy-start.5) | copy-done | bytes 88
  26.4 0.0 copy-done.6
  26.4 11.8 %finish.1 = (f32[512,128]{1,0:T(8,128)}, f32[4,8,128]{2,1,0:T(8,128)}) custom-call(bf16[4,7,8,16,128]{4,3,2,1,0:T(8,128)(2,1)S(1)} %get-tuple-element.20.full, f32[4,7,16,128]{3,2,1,0:T(8,128)S(1)} %get-tuple-element.21.rim, bf16[60,16,128]{2,1,0:T(8,128)(2,1)S(1)} %collective-permute-done.5.r1, bf16[60,16,128]{2,1,0:T(8,128)(2,1)S(1)} %collective-permute-done.6.r2, ...), custom_call_target="tpu_custom_call" | custom-call | tf_op jit(solution)/shard_map/finish/pallas_call | solution.py:594
Async XLA Ops:
  0.6 1.0 %copy-start = (bf16[3,16,4,8,128]{4,3,2,1,0:T(8,128)(2,1)S(1)}, bf16[3,16,4,8,128]{4,3,2,1,0:T(8,128)(2,1)}, u32[]{:S(2)}) copy-start(bf16[3,16,4,8,128]{4,3,2,1,0:T(8,128)(2,1)} %modes.1) | copy-start | bytes 1179652
  1.6 0.8 %copy-start.2 = (f32[3,4,8,128]{3,2,1,0:T(8,128)S(1)}, f32[3,4,8,128]{3,2,1,0:T(8,128)}, u32[]{:S(2)}) copy-start(f32[3,4,8,128]{3,2,1,0:T(8,128)} %disp.1) | copy-start | bytes 147460
  2.4 0.7 %copy-start.3 = (s32[4,8,128]{2,1,0:T(8,128)S(1)}, s32[4,8,128]{2,1,0:T(8,128)}, u32[]{:S(2)}) copy-start(s32[4,8,128]{2,1,0:T(8,128)} %material.1) | copy-start | bytes 49156
  3.1 0.7 %copy-start.4 = (s32[4,8,128]{2,1,0:T(8,128)S(1)}, s32[4,8,128]{2,1,0:T(8,128)}, u32[]{:S(2)}) copy-start(s32[4,8,128]{2,1,0:T(8,128)} %fixed.1) | copy-start | bytes 49156
  5.8 10.2 %collective-permute-start = (bf16[4,2,8,16,128]{4,3,2,1,0:T(8,128)(2,1)S(1)}, bf16[4,2,8,16,128]{4,3,2,1,0:T(8,128)(2,1)S(1)}, u32[]{:S(2)}, u32[]{:S(2)}) collective-permute-start(bf16[4,2,8,16,128]{4,3,2,1,0:T(8,128)(2,1)S(1)} %get-tuple-element.15), channel_id=1, source_target_pairs={{0,8},{1,9},{8,0},{9,1},{16,24},{17,25},{24,16},{25,17},{2,10},{3,... | collective-permute-start | bytes 786440 | tf_op jit(solution)/shard_map/ppermute | solution.py:538
  6.3 9.7 %collective-permute-start.1 = (bf16[4,2,8,16,128]{4,3,2,1,0:T(8,128)(2,1)S(1)}, bf16[4,2,8,16,128]{4,3,2,1,0:T(8,128)(2,1)S(1)}, u32[]{:S(2)}, u32[]{:S(2)}) collective-permute-start(bf16[4,2,8,16,128]{4,3,2,1,0:T(8,128)(2,1)S(1)} %get-tuple-element.16), channel_id=1, source_target_pairs={{0,1},{1,0},{8,16},{9,17},{16,8},{17,9},{24,25},{25,24},{2,3},{3,2... | collective-permute-start | bytes 786440 | tf_op jit(solution)/shard_map/ppermute | solution.py:538
  8.9 7.2 %collective-permute-start.2 = (bf16[4,4,16,128]{3,2,1,0:T(8,128)(2,1)S(1)}, bf16[4,4,16,128]{3,2,1,0:T(8,128)(2,1)S(1)}, u32[]{:S(2)}, u32[]{:S(2)}) collective-permute-start(bf16[4,4,16,128]{3,2,1,0:T(8,128)(2,1)S(1)} %get-tuple-element.17), channel_id=1, source_target_pairs={{0,1},{1,0},{8,9},{9,8},{16,17},{17,16},{24,25},{25,24},{2,3},{3,2... | collective-permute-start | bytes 196616 | tf_op jit(solution)/shard_map/ppermute | solution.py:538
  9.0 6.3 %collective-permute-start.3 = (bf16[4,2,16,128]{3,2,1,0:T(8,128)(2,1)S(1)}, bf16[4,2,16,128]{3,2,1,0:T(8,128)(2,1)S(1)}, u32[]{:S(2)}, u32[]{:S(2)}) collective-permute-start(bf16[4,2,16,128]{3,2,1,0:T(8,128)(2,1)S(1)} %get-tuple-element.18), channel_id=1, source_target_pairs={{0,9},{1,8},{8,1},{9,0},{16,25},{17,24},{24,17},{25,16},{2,11},{3,... | collective-permute-start | bytes 98312 | tf_op jit(solution)/shard_map/ppermute | solution.py:538
  10.4 5.7 %collective-permute-start.4 = (bf16[4,2,16,128]{3,2,1,0:T(8,128)(2,1)S(1)}, bf16[4,2,16,128]{3,2,1,0:T(8,128)(2,1)S(1)}, u32[]{:S(2)}, u32[]{:S(2)}) collective-permute-start(bf16[4,2,16,128]{3,2,1,0:T(8,128)(2,1)S(1)} %get-tuple-element.19), channel_id=1, source_target_pairs={{0,1},{1,0},{8,17},{9,16},{16,9},{17,8},{24,25},{25,24},{2,3},{3,2... | collective-permute-start | bytes 98312 | tf_op jit(solution)/shard_map/ppermute | solution.py:538
  16.1 9.7 %copy-start.1 = (f32[6,4,8,128]{3,2,1,0:T(8,128)S(1)}, f32[6,4,8,128]{3,2,1,0:T(8,128)}, u32[]{:S(2)}) copy-start(f32[6,4,8,128]{3,2,1,0:T(8,128)} %stress.1) | copy-start | bytes 294916
  16.5 7.8 %collective-permute-start.5 = (bf16[60,16,128]{2,1,0:T(8,128)(2,1)S(1)}, bf16[60,16,128]{2,1,0:T(8,128)(2,1)S(1)}, u32[]{:S(2)}, u32[]{:S(2)}) collective-permute-start(bf16[60,16,128]{2,1,0:T(8,128)(2,1)S(1)} %get-tuple-element.22), channel_id=1, source_target_pairs={{0,2},{1,3},{2,0},{3,1},{4,6},{5,7},{6,4},{7,5},{8,10},{9,11},{10,... | collective-permute-start | bytes 737288 | tf_op jit(solution)/shard_map/ppermute | solution.py:538
  18.6 7.1 %collective-permute-start.6 = (bf16[60,16,128]{2,1,0:T(8,128)(2,1)S(1)}, bf16[60,16,128]{2,1,0:T(8,128)(2,1)S(1)}, u32[]{:S(2)}, u32[]{:S(2)}) collective-permute-start(bf16[60,16,128]{2,1,0:T(8,128)(2,1)S(1)} %get-tuple-element.23), channel_id=1, source_target_pairs={{0,1},{1,0},{2,4},{3,5},{4,2},{5,3},{6,7},{7,6},{8,9},{9,8},{10,12... | collective-permute-start | bytes 737288 | tf_op jit(solution)/shard_map/ppermute | solution.py:538
  25.7 0.7 %copy-start.5 = (f32[16]{0:T(128)S(1)}, f32[16]{0:T(128)}, u32[]{:S(2)}) copy-start(f32[16]{0:T(128)} %eig.1) | copy-start | bytes 196
  25.7 0.7 %copy-start.6 = (f32[16]{0:T(128)S(1)}, f32[16]{0:T(128)}, u32[]{:S(2)}) copy-start(f32[16]{0:T(128)} %weight.1) | copy-start | bytes 196

commit v2 on v1

v2 whole, which is shorter than its diff:
```python
import functools
import math

import jax
import jax.numpy as jnp
from jax import lax
from jax.experimental import pallas as pl
from jax.experimental.pallas import tpu as pltpu
from jax.sharding import PartitionSpec as P

LEVELS = 8
POISSON = 0.45
LAM = POISSON / ((1.0 + POISSON) * (1.0 - 2.0 * POISSON))
MU = 0.5 / (1.0 + POISSON)
R3 = 1.0 / math.sqrt(3.0)
F32 = jnp.float32
BF16 = jnp.bfloat16
MODES = 16
GROUPS = 4
LANES = 128


def lane_iota(shape=(MODES, LANES)):
    return lax.broadcasted_iota(jnp.int32, shape, len(shape) - 1)


def row_iota(shape):
    return lax.broadcasted_iota(jnp.int32, shape, 0)


def roll(value, shift, axis=1):
    size = value.shape[axis]
    if isinstance(shift, int):
        shift = shift % size
        if shift == 0:
            return value
    return pltpu.roll(value, shift, axis)


def place(axis):
    me = lax.axis_index(axis)
    size = lax.axis_size(axis)
    even = lax.rem(me, 2) == 0
    return even, me > 0, me < size - 1


HALF = 8
PITCH = 40


def pair_up(first, second):
    return jnp.concatenate([first[:HALF].astype(F32), second[:HALF].astype(F32)], 0).astype(BF16)


def pack_kernel(dims, modes_in, material_in, fixed_in, disp_in, tiles, x1, x2, edge, ex1, ex2, modes, material, fixed, disp, raw, sems):
    nx, ny = dims
    copies = [
        pltpu.make_async_copy(src, dst, sems.at[i])
        for i, (src, dst) in enumerate(
            [(modes_in.at[c], modes.at[c]) for c in range(3)]
            + [(material_in, material), (fixed_in, fixed), (disp_in, disp)]
        )
    ]
    for copy in copies:
        copy.start()
    part = nx * ny

    def store(c, m, value):
        start = (c * MODES + m) * PITCH
        raw[start : start + part, :] = value.reshape(part, LANES)

    def spread(c):
        @pl.loop(0, nx)
        def _(x):
            for y in range(ny):
                value = raw[pl.ds(c * MODES * PITCH + x * ny + y, MODES, stride=PITCH), :]
                tiles[c, x, y] = value.astype(BF16)

    for c in range(3):
        copies[c].wait()
        for m in range(MODES):
            store(c, m, modes[c, m].astype(F32))
        spread(c)
    for copy in copies[3:]:
        copy.wait()
    store(3, 0, material[...].astype(F32) + 1.0)
    store(3, 1, 1.0 - fixed[...].astype(F32))
    for c in range(3):
        value = disp[c]
        first = value.astype(BF16).astype(F32)
        store(3, 2 + c, first)
        store(3, 5 + c, value - first)
    for m in range(HALF, MODES):
        store(3, m, jnp.zeros((part, LANES), F32))
    spread(3)

    col = lane_iota((LANES, LANES))
    kind = lax.rem(col, 3)
    wanted = row_iota((LANES, LANES)) == jnp.where(kind == 0, LANES - 1, kind - 1)
    ends = None
    for y in range(ny):
        chosen = jnp.where(wanted & (col >= 3 * y) & (col < 3 * y + 3), 1.0, 0.0).astype(BF16)
        block = tiles[:, :, y].reshape(GROUPS * nx * MODES, LANES)
        term = jnp.dot(block, chosen, preferred_element_type=F32)
        ends = term if ends is None else ends + term
    ends = ends.reshape(GROUPS, nx, MODES, LANES)
    pieces = LANES // nx
    even, _, _ = place("gx")
    last = [ends[c, nx - 1] for c in range(GROUPS)]
    for c in range(GROUPS):
        total = ends[c, 0]
        for x in range(1, nx):
            total = total + roll(ends[c, x], pieces * x)
        edge[c] = total.astype(BF16)
    for out, out_edge, upward in ((x1, ex1, even), (x2, ex2, jnp.logical_not(even))):
        flag = upward.astype(F32)
        for s in range(2):
            layer = jnp.where(upward, nx - 1, s)
            for c in range(3):
                for y in range(ny):
                    out[(c * 2 + s) * ny + y] = tiles[c, layer, y]
        layer = jnp.where(upward, nx - 1, 0)
        for y in range(0, ny, 2):
            out[6 * ny + y // 2] = pair_up(tiles[3, layer, y], tiles[3, layer, y + 1])
        for c in range(GROUPS):
            below = ends[c, 0] + roll(ends[c, 1], pieces)
            out_edge[c] = (last[c] * flag + below * (1.0 - flag)).astype(BF16)


def pick(parity, lower, upper, first, second, use_lower, use_upper, none_lower, none_upper):
    odd = jnp.logical_not(parity)
    pl.when(jnp.logical_and(lower, parity))(lambda: use_lower(second))
    pl.when(jnp.logical_and(lower, odd))(lambda: use_lower(first))
    pl.when(jnp.logical_and(upper, parity))(lambda: use_upper(first))
    pl.when(jnp.logical_and(upper, odd))(lambda: use_upper(second))
    pl.when(jnp.logical_not(lower))(none_lower)
    pl.when(jnp.logical_not(upper))(none_upper)


def merge_kernel(dims, zcount, *refs):
    nx, ny = dims
    tiles, r1, r2 = refs[:3]
    rz = refs[3 : 3 + zcount]
    rz1 = refs[3 + zcount : 3 + 2 * zcount]
    rz2 = refs[3 + 2 * zcount : 3 + 3 * zcount]
    rim, y1, y2, rows_aux = refs[3 + 3 * zcount :]
    xe, xlo, xup = place("gx")
    ze, zlo, zup = place("gz")
    ye, _, _ = place("gy")
    width = nx + 3
    pieces = LANES // nx
    lane = lane_iota()
    phase = lax.rem(lane, 3)
    kept = lane < 3 * ny
    even_f = ze.astype(F32)
    low_mask = jnp.where(kept & (phase == 0), zlo.astype(F32), 0.0)
    high_mask = jnp.where(kept & (phase != 0), zup.astype(F32), 0.0)
    whole = low_mask + high_mask

    def merged(blocks, slot):
        turned = [roll(b.astype(F32), LANES - pieces * slot) for b in blocks]
        if len(turned) == 1:
            return turned[0] * whole
        first, second = turned
        low = second * even_f + first * (1.0 - even_f)
        high = first * even_f + second * (1.0 - even_f)
        return low * low_mask + high * high_mask

    for c in range(GROUPS):
        for x in range(nx):
            rim[c, x + 1] = merged([r[c] for r in rz], x)

        def rim_lower(refs, c=c):
            rim[c, 0] = merged([r[c] for r in refs], 0)

        def rim_upper(refs, c=c):
            for s in range(2):
                rim[c, nx + 1 + s] = merged([r[c] for r in refs], s)

        def rim_no_lower(c=c):
            rim[c, 0] = jnp.zeros((MODES, LANES), F32)

        def rim_no_upper(c=c):
            for s in range(2):
                rim[c, nx + 1 + s] = jnp.zeros((MODES, LANES), F32)

        pick(xe, xlo, xup, rz1, rz2, rim_lower, rim_upper, rim_no_lower, rim_no_upper)

    blank = jnp.zeros((MODES, LANES), BF16)
    blank_half = jnp.zeros((HALF, LANES), F32)

    def half_of(ref, row):
        pairs = ref[6 * ny + row // 2].astype(F32)
        odd = lax.rem(row, 2).astype(F32)
        return pairs[:HALF] * (1.0 - odd) + pairs[HALF:] * odd

    for out, upward in ((y1, ye), (y2, jnp.logical_not(ye))):
        rows = [jnp.where(upward, ny - 1, s) for s in range(2)]
        for c in range(3):
            for s in range(2):
                for x in range(nx):
                    out[(c * width + x + 1) * 2 + s] = tiles[c, x, rows[s]]
        for x in range(nx):
            rows_aux[x + 1] = tiles[3, x, rows[0]][:HALF].astype(F32)

        def lower(ref, out=out, rows=rows):
            for c in range(3):
                for s in range(2):
                    out[c * width * 2 + s] = ref[c * 2 * ny + rows[s]]
            rows_aux[0] = half_of(ref, rows[0])

        def upper(ref, out=out, rows=rows):
            for c in range(3):
                for t in range(2):
                    for s in range(2):
                        out[(c * width + nx + 1 + t) * 2 + s] = ref[(c * 2 + t) * ny + rows[s]]
            rows_aux[nx + 1] = half_of(ref, rows[0])

        def no_lower(out=out):
            for c in range(3):
                for s in range(2):
                    out[c * width * 2 + s] = blank
            rows_aux[0] = blank_half

        def no_upper(out=out):
            for c in range(3):
                for i in range(4):
                    out[(c * width + nx + 1) * 2 + i] = blank
            rows_aux[nx + 1] = blank_half

        pick(xe, xlo, xup, r1, r2, lower, upper, no_lower, no_upper)
        base = 6 * width
        for x in range(0, nx + 2, 2):
            out[base + x // 2] = jnp.concatenate([rows_aux[x], rows_aux[x + 1]], 0).astype(BF16)
        base += (nx + 2) // 2
        for c in range(GROUPS):
            ends = jnp.zeros((MODES, LANES), F32)
            for x in range(width):
                start = 16 * x
                turned = roll(rim[c, x], lax.rem(start + LANES - 3 * rows[0], LANES))
                ends = jnp.where((lane >= start) & (lane < start + 6), turned, ends)
            out[base + c] = ends.astype(BF16)


def cross_xy(a, b):
    return a[0] * b[1] + a[4] * b[5]


def cross_xz(a, b):
    return a[0] * b[2] + a[3] * b[5]


def cross_yz(a, b):
    return a[1] * b[2] + a[3] * b[4]


def squares(a):
    f, g, h, t = a[3] * a[3], a[4] * a[4], a[5] * a[5], a[6] * a[6]
    ft = f + t
    return (a[0] * a[0] + (ft + g), a[1] * a[1] + (ft + h), a[2] * a[2] + ((g + t) + h))


def combos(now, after):
    return (
        now[1] + after[1],
        after[0] - now[0],
        now[2] + after[2],
        (after[1] - now[1]) * R3,
        (now[3] + after[3]) * R3,
        (after[2] - now[2]) * R3,
        (after[3] - now[3]) * (1.0 / 3.0),
    )


def forms(parts, with_energy):
    own = [squares(p) for p in parts]
    quad = [own[0][i] + own[1][i] + own[2][i] for i in range(3)]
    for f in (cross_yz, cross_xz, cross_xy):
        quad.append(f(parts[0], parts[0]) + f(parts[1], parts[1]) + f(parts[2], parts[2]))
    if not with_energy:
        return quad, None
    x, y, z = parts
    energy = (
        MU * (quad[0] + quad[1] + quad[2])
        + (LAM + MU) * (own[0][0] + own[1][1] + own[2][2])
        + (2.0 * LAM) * (cross_xy(x, y) + cross_xz(x, z) + cross_yz(y, z))
        + (2.0 * MU) * (cross_xy(y, x) + cross_xz(z, x) + cross_yz(z, y))
    )
    return quad, energy


def bilinear(l, d):
    total = None
    diagonal = None
    for p in range(3):
        prod = [l[p][i] * d[p][i] for i in range(7)]
        ft = prod[3] + prod[6]
        three = (
            prod[0] + (ft + prod[4]),
            prod[1] + (ft + prod[5]),
            prod[2] + ((prod[4] + prod[6]) + prod[5]),
        )
        whole = three[0] + three[1] + three[2]
        total = whole if total is None else total + whole
        diagonal = three[p] if diagonal is None else diagonal + three[p]
    lx, ly, lz = l
    dx, dy, dz = d
    mixed = (
        (cross_xy(lx, dy) + cross_xy(dx, ly))
        + (cross_xz(lx, dz) + cross_xz(dx, lz))
        + (cross_yz(ly, dz) + cross_yz(dy, lz))
    )
    shear = (
        (cross_xy(dy, lx) + cross_xy(ly, dx))
        + (cross_xz(dz, lx) + cross_xz(lz, dx))
        + (cross_yz(dz, ly) + cross_yz(lz, dy))
    )
    return MU * total + (LAM + MU) * diagonal + LAM * mixed + MU * shear


def fold_rows(values):
    row = row_iota((8, LANES))
    top = row < 4
    step = [
        jnp.where(top, values[k], values[k + 4]) + roll(jnp.where(top, values[k + 4], values[k]), 4, 0)
        for k in range(4)
    ]
    top = lax.rem(row, 4) < 2
    step = [
        jnp.where(top, step[k] + roll(step[k], 6, 0), step[k + 2] + roll(step[k + 2], 2, 0)) for k in range(2)
    ]
    return jnp.where(lax.rem(row, 2) == 0, step[0] + roll(step[0], 7, 0), step[1] + roll(step[1], 1, 0))


def z_table(kind):
    row = row_iota((2 * LANES, 2 * LANES))
    col = lane_iota((2 * LANES, 2 * LANES))
    z = jnp.where(col < LANES, col, col - LANES)
    own = jnp.where(row == z, jnp.where(col < LANES, 1.0, -1.0), 0.0)
    after = jnp.where((row == z + 1) & (row < LANES), 1.0, 0.0)
    rim = jnp.where((z == LANES - 1) & (row == LANES + kind), 1.0, 0.0)
    return (own + after + rim).astype(BF16)


def first_column(lane_to):
    return jnp.where((row_iota((LANES, LANES)) == 0) & (lane_iota((LANES, LANES)) == lane_to), 1.0, 0.0).astype(BF16)


def rows_along_z(block, rim, kind, sz, dz, at):
    both = jnp.dot(jnp.concatenate([block, rim], 1), z_table(kind), preferred_element_type=F32)
    sz[at] = both[:, :LANES].reshape(sz.shape[1:])
    dz[at] = both[:, LANES:].reshape(dz.shape[1:])


def x_parts(sz, dz, y, x, h):
    found = []
    for c in range(3):
        s0 = sz[y, c, x, pl.ds(8 * h, 8), :]
        s1 = sz[y, c, x + 1, pl.ds(8 * h, 8), :]
        d0 = dz[y, c, x, pl.ds(8 * h, 8), :]
        d1 = dz[y, c, x + 1, pl.ds(8 * h, 8), :]
        found.append((s0 + s1, s1 - s0, d0 + d1, d1 - d0))
    return found


def mode_value(quad, energy, fields, eig_rows):
    terms = [fields[i] * quad[i] for i in range(6)]
    total = ((terms[0] + terms[1]) + (terms[2] + terms[3])) + (terms[4] + terms[5])
    return fields[6] * energy + eig_rows * total


FIELDS = 5


def inner_kernel(dims, tiles, r1, r2, rim, stress, eig, weight, sens, wmain, field, cell, zr, scale, full, sz, dz, part, aux):
    nx, ny = dims
    width = nx + 3
    tall = ny + 3
    lane = lane_iota()
    xe, xlo, xup = place("gx")

    full[:, 1 : nx + 1] = tiles[0:3]
    for x in range(nx):
        for y in range(ny):
            aux[((x + 1) * ny + y) * HALF : ((x + 1) * ny + y + 1) * HALF, :] = tiles[3, x, y][:HALF].astype(F32)

    def halves(ref, x):
        for i in range(ny // 2):
            start = (x * ny + 2 * i) * HALF
            aux[start : start + 2 * HALF, :] = ref[6 * ny + i].astype(F32)

    def lower(ref):
        for c in range(3):
            for y in range(ny):
                full[c, 0, y] = ref[c * 2 * ny + y]
        halves(ref, 0)

    def upper(ref):
        for c in range(3):
            for s in range(2):
                for y in range(ny):
                    full[c, nx + 1 + s, y] = ref[(c * 2 + s) * ny + y]
        halves(ref, nx + 1)

    def no_lower():
        full[:, 0:1] = jnp.zeros((3, 1, ny, MODES, LANES), BF16)
        aux[0 : ny * HALF, :] = jnp.zeros((ny * HALF, LANES), F32)

    def no_upper():
        full[:, nx + 1 : nx + 3] = jnp.zeros((3, 2, ny, MODES, LANES), BF16)
        aux[(nx + 1) * ny * HALF : (nx + 2) * ny * HALF, :] = jnp.zeros((ny * HALF, LANES), F32)

    pick(xe, xlo, xup, r1, r2, lower, upper, no_lower, no_upper)

    count = 3 * width * MODES
    ends = rim[0:3].reshape(count, LANES).astype(BF16)
    column = None
    for y in range(ny):
        block = full[:, :, y].reshape(count, LANES)
        rows_along_z(block, ends, 3 * y + 1, sz, dz, y)
        term = jnp.dot(block, first_column(3 * tall + y + 1), preferred_element_type=F32)
        column = term if column is None else column + term
    column = column.reshape(3, width, MODES, LANES)
    for c in range(GROUPS):
        for x in range(width):
            turned = roll(rim[c, x], 3)
            zr[c, x] = turned + column[c, x] if c < 3 else turned

    for x in range(nx + 2):
        def channel(k):
            return aux[pl.ds(x * ny * HALF + k, ny, stride=HALF), :]

        field[0, x] = channel(0)
        field[1, x] = channel(1)
        for c in range(3):
            field[2 + c, x] = channel(2 + c) + channel(5 + c)

    mode_row = row_iota((MODES, LANES))
    mode_lane = lax.rem(lane, MODES)
    eig_rows = jnp.zeros((MODES, LANES), F32)
    coef_rows = jnp.zeros((MODES, LANES), F32)
    coef_lanes = jnp.zeros((MODES, LANES), F32)
    for m in range(MODES):
        product = eig[m] * weight[m]
        eig_rows = jnp.where(mode_row == m, eig[m], eig_rows)
        coef_rows = jnp.where(mode_row == m, product, coef_rows)
        coef_lanes = jnp.where(mode_lane == m, product, coef_lanes)
    scale[0], scale[1], scale[2] = eig_rows, coef_rows, coef_lanes

    for x in range(nx):
        density = field[0, x + 1] * (1.0 / LEVELS)
        young = 0.001 + density * density * density
        slope = 3.0 * density * density
        ratio = slope / young
        cell[6, x] = slope * (1.0 / 16.0)
        for c in range(6):
            cell[c, x] = stress[c, x] * ratio * (-1.0 / 16.0 if c < 3 else -1.0 / 8.0)

    def sweep(x, inside):
        for h in range(2):
            coef = scale[1, 8 * h : 8 * h + 8]
            eig_half = scale[0, 8 * h : 8 * h + 8]
            now = x_parts(sz, dz, 0, x, h)
            for y in range(ny - 1):
                after = x_parts(sz, dz, y + 1, x, h)
                quad, energy = forms([combos(now[c], after[c]) for c in range(3)], inside)
                if inside:
                    fields = [cell[i, x - 1, pl.ds(y, 1), :] for i in range(7)]
                    start = 8 * h * nx * ny + (x - 1) * ny + y
                    sens[pl.ds(start, 8, stride=nx * ny), :] = mode_value(quad, energy, fields, eig_half)
                for i in range(6):
                    if h == 0:
                        part[i, y] = coef * quad[i]
                    else:
                        part[i, y] += coef * quad[i]
                now = after
        blank = jnp.zeros((8, LANES), F32)
        for i in range(6):
            wmain[i, x] = fold_rows([blank] + [part[i, y] for y in range(ny - 1)])

    @pl.loop(1, nx + 1)
    def _(x):
        sweep(x, True)

    @pl.loop(0, 2)
    def _(i):
        sweep(i * (nx + 1), False)


def final_kernel(dims, y1, y2, r1, r2, rim, wmain, field_in, cell, zr, scale, sens_in, sens, adjoint, rows, rows_aux, rows_end, sz, dz, sum_z, w, zt, field, shear, load, stage, last, sems):
    del sens_in
    nx, ny = dims
    width = nx + 3
    tall = ny + 3
    lane = lane_iota()
    ye, ylo, yup = place("gy")

    def copy_rows(to, ref, slot):
        for i in range(3 * width):
            rows[to, i] = ref[2 * i + slot]

    aux_base = 6 * width
    end_base = aux_base + (nx + 2) // 2

    def copy_aux(to, ref):
        for i in range((nx + 2) // 2):
            rows_aux[to, i] = ref[aux_base + i].astype(F32)
        for c in range(GROUPS):
            rows_end[to, c] = ref[end_base + c].astype(F32)

    def lower(ref):
        copy_rows(0, ref, 0)
        copy_aux(0, ref)

    def upper(ref):
        copy_rows(3, ref, 0)
        copy_rows(4, ref, 1)
        copy_aux(1, ref)

    def no_lower():
        rows[0] = jnp.zeros_like(rows[0])
        rows_aux[0] = jnp.zeros_like(rows_aux[0])
        rows_end[0] = jnp.zeros_like(rows_end[0])

    def no_upper():
        rows[3:5] = jnp.zeros_like(rows[3:5])
        rows_aux[1] = jnp.zeros_like(rows_aux[1])
        rows_end[1] = jnp.zeros_like(rows_end[1])

    pick(ye, ylo, yup, r1, r2, lower, upper, no_lower, no_upper)

    @pl.when(ye)
    def _():
        copy_rows(2, y1, 0)
        copy_rows(1, y2, 0)

    @pl.when(jnp.logical_not(ye))
    def _():
        copy_rows(2, y2, 0)
        copy_rows(1, y1, 0)

    far = 3 * (ny + 1)
    count = 3 * width * MODES
    at = (0, 1, ny, ny + 1, ny + 2)
    column = None
    for i in (0, 3, 4):
        term = jnp.dot(rows[i].reshape(count, LANES), first_column(3 * tall + at[i]), preferred_element_type=F32)
        column = term if column is None else column + term
    column = column.reshape(3, width, MODES, LANES)
    full_rim = []
    for c in range(GROUPS):
        layers = []
        for x in range(width):
            ends = jnp.where(lane < 3, roll(rows_end[0, c], LANES - 16 * x), zr[c, x])
            ends = jnp.where((lane >= far) & (lane < far + 6), roll(rows_end[1, c], far - 16 * x), ends)
            if c < 3:
                ends = ends + column[c, x]
            layers.append(ends)
        layers.append(jnp.zeros((LANES - width * MODES, LANES), F32))
        stacked = jnp.concatenate(layers, 0)
        full_rim.append(stacked[: width * MODES])
        zt[c] = stacked.T
    ends = jnp.concatenate(full_rim[:3], 0).astype(BF16)
    for i in range(5):
        rows_along_z(rows[i].reshape(count, LANES), ends, 3 * at[i] + 1, sz, dz, i)

    w[:, :, 0:8, 0:LANES] = wmain[...]

    def sweep(x, inside):
        for h in range(2):
            coef = scale[1, 8 * h : 8 * h + 8]
            now = None
            for i, (first, own) in enumerate(((0, False), (2, inside), (3, False))):
                if i < 2:
                    now = x_parts(sz, dz, first, x, h)
                after = x_parts(sz, dz, first + 1, x, h)
                quad, energy = forms([combos(now[c], after[c]) for c in range(3)], own)
                if own:
                    fields = [cell[k, x - 1, ny - 1 : ny, :] for k in range(7)]
                    last[x - 1, pl.ds(8 * h, 8), :] = mode_value(quad, energy, fields, scale[0, 8 * h : 8 * h + 8])
                for k in range(6):
                    if h == 0:
                        sum_z[k, i] = coef * quad[k]
                    else:
                        total = jnp.sum(sum_z[k, i] + coef * quad[k], axis=0, keepdims=True)
                        row = (0, ny, ny + 1)[i]
                        w[k, x, row : row + 1, 0:LANES] = total
                now = after

    @pl.loop(1, nx + 1)
    def _(x):
        sweep(x, True)

    @pl.loop(0, 2)
    def _(i):
        sweep(i * (nx + 1), False)

    copies = [pltpu.make_async_copy(last.at[x], sens.at[:, x, ny - 1], sems.at[x]) for x in range(nx)]
    for copy in copies:
        copy.start()

    for x in range(nx + 2):
        for k in range(FIELDS):
            field[k, x, 1 : ny + 1] = field_in[k, x]
        for side, row in ((0, 0), (1, ny + 1)):
            pair = rows_aux[side, x // 2][(x % 2) * HALF : (x % 2 + 1) * HALF]
            field[0, x, row : row + 1] = pair[0:1]
            field[1, x, row : row + 1] = pair[1:2]
            for c in range(3):
                field[2 + c, x, row : row + 1] = pair[2 + c : 3 + c] + pair[5 + c : 6 + c]

    def end_nodes(c, kind, y):
        if kind == 3:
            return zt[c, pl.ds(3 * tall + y, 16), :]
        return zt[c, pl.ds(3 * y + kind, 16, stride=3), :]

    def end_parts(low, high, y):
        found = []
        for c in range(3):
            first, second = end_nodes(c, low, y), end_nodes(c, high, y)
            s, d = first + second, second - first
            s_next, d_next = roll(s, LANES - 16), roll(d, LANES - 16)
            found.append((s + s_next, s_next - s, d + d_next, d_next - d))
        return found

    sides = []
    for low, high in ((0, 3), (1, 2)):
        now, after = end_parts(low, high, 0), end_parts(low, high, 1)
        quad, _ = forms([combos(now[c], after[c]) for c in range(3)], False)
        summed = []
        for value in quad:
            value = value * scale[2]
            for shift in (1, 2, 4, 8):
                value = value + roll(value, LANES - shift)
            summed.append(value)
        sides.append(summed)
    for i in range(6):
        both = jnp.where(lax.rem(lane, 16) == 0, sides[1][i], roll(sides[0][i], LANES - 1))
        for x in range(nx + 2):
            w[i, x, 0:16, LANES:] = roll(both, LANES - 16 * x)

    def end_field(channel, x, first, with_low):
        value = roll(zt[3, pl.ds(3 * first + 1, 16, stride=3), :], LANES - (16 * x + channel))
        if not with_low:
            return value
        low = roll(zt[3, pl.ds(3 * first, 16, stride=3), :], LANES - 1 - (16 * x + channel))
        return jnp.where(lane == 0, value, jnp.where(lane == LANES - 1, low, 0.0))

    def z_back(main, end):
        turned, turned_end = roll(main, 1), roll(end, 1)
        return jnp.where(lane == 0, turned_end, turned), jnp.where(lane == 0, turned, turned_end)

    first_rows = None
    for x in range(nx + 2):
        level = (field[0, x, 0:16], end_field(0, x, 0, True))
        scaled = []
        for t in range(2):
            density = level[t] * (1.0 / LEVELS)
            young = 0.001 + density * density * density
            young = jnp.where(level[t] > 0.0, young, 0.0) * (1.0 / 64.0)
            value = [w[i, x, 0:16, LANES * t : LANES * (t + 1)] * young for i in range(6)]
            trace = LAM * (value[0] + value[1] + value[2])
            scaled.append(
                [trace + (2.0 * MU) * value[i] for i in range(3)] + [(2.0 * MU) * value[i] for i in range(3, 6)]
            )
        sums, diffs = [], []
        for i in range(6):
            main, end = scaled[0][i], scaled[1][i]
            back_main, back_end = z_back(main, end)
            sums.append((main + back_main, end + back_end))
            diffs.append((main - back_main, end - back_end))
        xx, yy, zz, yz, xz, xy = range(6)
        order = (sums[xx], sums[xy], diffs[xz], sums[yy], diffs[yz], sums[xz], sums[yz], diffs[zz])
        for slot, source in enumerate(order):
            for t in range(2):
                shear[slot, t, 0:16] = source[t]
        found = []
        for t in range(2):
            low = [shear[slot, t, 0:16] for slot in range(8)]
            high = [shear[slot, t, 1:17] for slot in range(8)]
            plus = [low[k] + high[k] for k in range(8)]
            minus = [high[k] - low[k] for k in range(8)]
            found.append([plus[0], minus[1] + plus[2], plus[1], minus[3] + plus[4], plus[5], minus[6] + plus[7]])
        if x > 0:
            node = x - 1
            for t in range(2):
                free = field[1, x, 1:17] if t == 0 else end_field(1, x, 1, False)
                for p in range(3):
                    value = (found[t][2 * p] - first_rows[t][2 * p]) + (
                        found[t][2 * p + 1] + first_rows[t][2 * p + 1]
                    )
                    load[p, node, t] = value * free
                    if t == 0:
                        shift = field[2 + p, x, 1:17]
                    else:
                        shift = end_field(2 + p, x, 1, False) + end_field(5 + p, x, 1, False)
                    load[3 + p, node, t] = shift
        first_rows = found

    def node_layer(x):
        found = []
        for f in range(6):
            main, end = load[f, x, 0], load[f, x, 1]
            after = jnp.where(lane == LANES - 1, roll(end, LANES - 1), roll(main, LANES - 1))
            s, d = main + after, after - main
            stage[0, 0:16] = s
            stage[1, 0:16] = d
            s_next, d_next = stage[0, 1:9], stage[1, 1:9]
            s, d = s[0:8], d[0:8]
            found.append((s + s_next, s_next - s, d + d_next, d_next - d))
        return found

    def layer_combos(now, after):
        return (
            after[0] - now[0],
            now[1] + after[1],
            now[2] + after[2],
            (after[1] - now[1]) * R3,
            (after[2] - now[2]) * R3,
            (now[3] + after[3]) * R3,
            (after[3] - now[3]) * (1.0 / 3.0),
        )

    now = node_layer(0)
    for x in range(nx):
        after = node_layer(x + 1)
        parts = [layer_combos(now[f], after[f]) for f in range(6)]
        adjoint[x] = cell[6, x] * bilinear(parts[:3], parts[3:])
        now = after
    for copy in copies:
        copy.wait()


def partner(index, size, kind):
    other = index ^ 1 if kind == 1 else ((index + 1) ^ 1) - 1
    return other if 0 <= other < size else None


def swap(block, axes, kinds, fill):
    sizes = [lax.axis_size(a) for a in axes]
    route = []
    for i in range(sizes[0]):
        for j in range(sizes[1]):
            ends = [p if k == 0 else partner(p, n, k) for p, n, k in zip((i, j), sizes, kinds, strict=True)]
            if ends[0] is None:
                ends = [i, partner(j, sizes[1], 1)] if fill else None
            elif ends[1] is None:
                ends = [partner(i, sizes[0], 1) if kinds[0] == 0 else ends[0], j] if fill else None
            if ends is not None:
                route.append((i * sizes[1] + j, ends[0] * sizes[1] + ends[1]))
    return lax.ppermute(block, axes, route)


def vmem(n):
    return [pl.BlockSpec(memory_space=pltpu.VMEM)] * n


def vmem(n):
    return [pl.BlockSpec(memory_space=pltpu.VMEM)] * n


def anywhere(n):
    return [pl.BlockSpec(memory_space=pl.ANY)] * n


def body(mode_shapes, stress_field, displacement, material, fixed_nodes, eigenvalues, mode_weight):
    nx, ny, nz = material.shape
    dims = (nx, ny)
    width = nx + 3
    sds = jax.ShapeDtypeStruct
    tile = (MODES, LANES)
    layer = 6 * ny + ny // 2
    tiles, x1, x2, edge, ex1, ex2 = pl.pallas_call(
        functools.partial(pack_kernel, dims),
        out_shape=(
            sds((GROUPS, nx, ny) + tile, BF16),
            sds((layer,) + tile, BF16),
            sds((layer,) + tile, BF16),
            sds((GROUPS,) + tile, BF16),
            sds((GROUPS,) + tile, BF16),
            sds((GROUPS,) + tile, BF16),
        ),
        in_specs=anywhere(4),
        out_specs=tuple(vmem(6)),
        scratch_shapes=[
            pltpu.VMEM(mode_shapes.shape, BF16),
            pltpu.VMEM(material.shape, material.dtype),
            pltpu.VMEM(fixed_nodes.shape, fixed_nodes.dtype),
            pltpu.VMEM(displacement.shape, F32),
            pltpu.VMEM((GROUPS * MODES * PITCH, LANES), F32),
            pltpu.SemaphoreType.DMA((6,)),
        ],
        compiler_params=pltpu.CompilerParams(vmem_limit_bytes=8 << 20),
        name="pack",
    )(*(pltpu.with_memory_space_constraint(a, pltpu.HBM) for a in (mode_shapes, material, fixed_nodes, displacement)))

    xz = ("gx", "gz")
    zkinds = (1,) if lax.axis_size("gz") == 2 else (1, 2)
    r2 = swap(x2, xz, (2, 0), True)
    r1 = swap(x1, xz, (1, 0), True)
    rz = [swap(edge, xz, (0, k), True) for k in zkinds]
    rz1 = [swap(ex1, xz, (1, k), True) for k in zkinds]
    rz2 = [swap(ex2, xz, (2, k), True) for k in zkinds]
    count = 6 * width + (nx + 2) // 2 + GROUPS
    rim, y1, y2 = pl.pallas_call(
        functools.partial(merge_kernel, dims, len(zkinds)),
        out_shape=(sds((GROUPS, width) + tile, F32), sds((count,) + tile, BF16), sds((count,) + tile, BF16)),
        in_specs=vmem(3 + 3 * len(zkinds)),
        out_specs=tuple(vmem(3)),
        scratch_shapes=[pltpu.VMEM((nx + 2, HALF, LANES), F32)],
        compiler_params=pltpu.CompilerParams(vmem_limit_bytes=8 << 20),
        name="merge",
    )(tiles, r1, r2, *rz, *rz1, *rz2)

    yz = ("gy", "gz")
    ry1 = swap(y1, yz, (1, 0), True)
    ry2 = swap(y2, yz, (2, 0), True)
    sens, wmain, field, cell, zr, scale = pl.pallas_call(
        functools.partial(inner_kernel, dims),
        out_shape=(
            sds((MODES * nx * ny, LANES), F32),
            sds((6, nx + 2, 8, LANES), F32),
            sds((FIELDS, nx + 2, ny, LANES), F32),
            sds((7, nx, ny, LANES), F32),
            sds((GROUPS, width) + tile, F32),
            sds((3,) + tile, F32),
        ),
        in_specs=vmem(5) + [pl.BlockSpec(memory_space=pltpu.SMEM)] * 2,
        out_specs=tuple(vmem(6)),
        scratch_shapes=[
            pltpu.VMEM((3, width, ny) + tile, BF16),
            pltpu.VMEM((ny, 3, width) + tile, F32),
            pltpu.VMEM((ny, 3, width) + tile, F32),
            pltpu.VMEM((6, ny - 1, 8, LANES), F32),
            pltpu.VMEM(((nx + 2) * ny * HALF, LANES), F32),
        ],
        compiler_params=pltpu.CompilerParams(vmem_limit_bytes=24 << 20),
        cost_estimate=pl.CostEstimate(flops=20_000_000, bytes_accessed=12_000_000, transcendentals=0),
        name="inner",
    )(tiles, r1, r2, rim, stress_field, eigenvalues, mode_weight)
    sens, adjoint = pl.pallas_call(
        functools.partial(final_kernel, dims),
        out_shape=(sds((MODES, nx, ny, LANES), F32), sds((nx, ny, LANES), F32)),
        in_specs=vmem(10) + anywhere(1),
        out_specs=(pl.BlockSpec(memory_space=pl.ANY), pl.BlockSpec(memory_space=pltpu.VMEM)),
        input_output_aliases={10: 0},
        scratch_shapes=[
            pltpu.VMEM((5, 3 * width) + tile, BF16),
            pltpu.VMEM((2, (nx + 2) // 2) + tile, F32),
            pltpu.VMEM((2, GROUPS) + tile, F32),
            pltpu.VMEM((5, 3, width) + tile, F32),
            pltpu.VMEM((5, 3, width) + tile, F32),
            pltpu.VMEM((6, 3, 8, LANES), F32),
            pltpu.VMEM((6, nx + 2, 16, 2 * LANES), F32),
            pltpu.VMEM((GROUPS, LANES, LANES), F32),
            pltpu.VMEM((FIELDS, nx + 2, 24, LANES), F32),
            pltpu.VMEM((8, 2, 24, LANES), F32),
            pltpu.VMEM((6, nx + 1, 2, 16, LANES), F32),
            pltpu.VMEM((2, 24, LANES), F32),
            pltpu.VMEM((nx,) + tile, F32),
            pltpu.SemaphoreType.DMA((nx,)),
        ],
        compiler_params=pltpu.CompilerParams(vmem_limit_bytes=24 << 20),
        name="finish",
    )(y1, y2, ry1, ry2, rim, wmain, field, cell, zr, scale, sens.reshape(MODES, nx, ny, nz))
    return sens, adjoint


def solution(mesh):
    return jax.shard_map(
        body,
        mesh=mesh,
        in_specs=(
            P(None, None, "gx", "gy", "gz"),
            P(None, "gx", "gy", "gz"),
            P(None, "gx", "gy", "gz"),
            P("gx", "gy", "gz"),
            P("gx", "gy", "gz"),
            P(),
            P(),
        ),
        out_specs=(P(None, "gx", "gy", "gz"), P("gx", "gy", "gz")),
        check_vma=False,
    )
```

time: 38.5 us -> 24.6 us (0.64)
  waiting for transfers between devices: 9.75 us -> 4.08 us
  local copies, waits for them, and re-layouts: 3.89 us -> 0.01 us
  Pallas kernels: 14.1 us -> 10.3 us
    pallas_call x1, Pallas kernels: 11.8 us -> 3.71 us  [body(): pl.pallas_call(functools.partial(final_kernel, dims), out_shape=(sds((MOD...]
    ppermute x7, waiting for transfers between devices: 9.75 us -> 4.08 us  [swap(): return lax.ppermute(block, axes, route)]
    pallas_call x0 -> x1, Pallas kernels: none -> 4.1 us  [body(): pl.pallas_call(functools.partial(inner_kernel, dims), out_shape=(sds((MOD...]
    unnamed x14 -> x6, local copies, waits for them, and re-layouts: 3.89 us -> 0.01 us
    pallas_call x1, Pallas kernels: 0.4 us -> 0.85 us  [body(): pl.pallas_call(functools.partial(merge_kernel, dims, len(zkinds)), out_sh...]
  transfers between devices with their start and end apart: 7 -> 7, of which waited for: 4 -> 4; matrix products, arithmetic and copies ran while one was open for 0% -> 0% of each run, Pallas kernels for 0% -> 17%
where the time goes in v2:
time: 24.6 us; the launch traced here: 24.4 us
  Pallas kernels  10.3 us (42%)
  starting transfers between devices  9.37 us (38%)
  waiting for transfers between devices  4.08 us (17%)
  between operations  0.66 us (3%)
    ppermute x7, starting transfers between devices, swap(): return lax.ppermute(block, axes, route)  9.37 us
    pallas_call x1, Pallas kernels, body(): pl.pallas_call(functools.partial(inner_kernel, dims), out_shape=(sds((MOD...  4.1 us
    ppermute x7, waiting for transfers between devices, swap(): return lax.ppermute(block, axes, route)  4.08 us
    pallas_call x1, Pallas kernels, body(): pl.pallas_call(functools.partial(final_kernel, dims), out_shape=(sds((MOD...  3.71 us
    pallas_call x1, Pallas kernels, body(): pl.pallas_call(functools.partial(pack_kernel, dims), out_shape=(sds((GROU...  1.62 us
    pallas_call x1, Pallas kernels, body(): pl.pallas_call(functools.partial(merge_kernel, dims, len(zkinds)), out_sh...  0.85 us
  transfers between devices with their start and end apart: 7, of which 4 were waited for; matrix products, arithmetic and copies ran while one was open for 0% of the time, Pallas kernels for 17%

profile of v2, /device:TPU:0, one launch (start us, length us, event | category | flops | bytes accessed | tf_op | source)
XLA Modules:
  0.0 24.4 jit_solution(9734991110660638151)
XLA Ops:
  0.6 1.6 %pack.1 = (bf16[4,4,8,16,128]{4,3,2,1,0:T(8,128)(2,1)S(1)}, bf16[52,16,128]{2,1,0:T(8,128)(2,1)S(1)}, bf16[52,16,128]{2,1,0:T(8,128)(2,1)S(1)}, bf16[4,16,128]{2...) custom-call(bf16[3,16,4,8,128]{4,3,2,1,0:T(8,128)(2,1)} %modes_in.1, ...), custom_call_target="tpu_custom_call" | custom-call | tf_op jit(solution)/shard_map/pack/pallas_call | solution.py:773
  2.3 0.5 %collective-permute-start = (bf16[52,16,128]{2,1,0:T(8,128)(2,1)S(1)}, bf16[52,16,128]{2,1,0:T(8,128)(2,1)S(1)}, u32[]{:S(2)}, u32[]{:S(2)}) collective-permute-start(bf16[52,16,128]{2,1,0:T(8,128)(2,1)S(1)} %get-tuple-element.18), channel_id=1, source_target_pairs={{0,8},{1,9},{8,0},{9,1},{16,24},{17,25},{24,16},{25,17},{2,10},{3,... | collective-permute-start | bytes 638984 | tf_op jit(solution)/shard_map/ppermute | solution.py:751
  2.8 2.6 %collective-permute-start.1 = (bf16[52,16,128]{2,1,0:T(8,128)(2,1)S(1)}, bf16[52,16,128]{2,1,0:T(8,128)(2,1)S(1)}, u32[]{:S(2)}, u32[]{:S(2)}) collective-permute-start(bf16[52,16,128]{2,1,0:T(8,128)(2,1)S(1)} %get-tuple-element.19), channel_id=1, source_target_pairs={{0,1},{1,0},{8,16},{9,17},{16,8},{17,9},{24,25},{25,24},{2,3},{3,2... | collective-permute-start | bytes 638984 | tf_op jit(solution)/shard_map/ppermute | solution.py:751
  5.3 0.1 collective-permute-start.2
  5.4 1.4 %collective-permute-start.3 = (bf16[4,16,128]{2,1,0:T(8,128)(2,1)S(1)}, bf16[4,16,128]{2,1,0:T(8,128)(2,1)S(1)}, u32[]{:S(2)}, u32[]{:S(2)}) collective-permute-start(bf16[4,16,128]{2,1,0:T(8,128)(2,1)S(1)} %get-tuple-element.21), channel_id=1, source_target_pairs={{0,9},{1,8},{8,1},{9,0},{16,25},{17,24},{24,17},{25,16},{2,11},{3,... | collective-permute-start | bytes 49160 | tf_op jit(solution)/shard_map/ppermute | solution.py:751
  6.8 1.5 %collective-permute-start.4 = (bf16[4,16,128]{2,1,0:T(8,128)(2,1)S(1)}, bf16[4,16,128]{2,1,0:T(8,128)(2,1)S(1)}, u32[]{:S(2)}, u32[]{:S(2)}) collective-permute-start(bf16[4,16,128]{2,1,0:T(8,128)(2,1)S(1)} %get-tuple-element.22), channel_id=1, source_target_pairs={{0,1},{1,0},{8,17},{9,16},{16,9},{17,8},{24,25},{25,24},{2,3},{3,2... | collective-permute-start | bytes 49160 | tf_op jit(solution)/shard_map/ppermute | solution.py:751
  8.3 1.4 %collective-permute-done.2.refs_3_ = bf16[4,16,128]{2,1,0:T(8,128)(2,1)S(1)} collective-permute-done((bf16[4,16,128]{2,1,0:T(8,128)(2,1)S(1)}, bf16[4,16,128]{2,1,0:T(8,128)(2,1)S(1)}, u32[]{:S(2)}, u32[]{:S(2)}) %collective-permute-start.2) | collective-permute-done | bytes 16416 | tf_op jit(solution)/shard_map/ppermute | solution.py:751
  9.7 0.0 collective-permute-done.3.refs_4_
  9.7 0.9 %collective-permute-done.4.refs_5_ = bf16[4,16,128]{2,1,0:T(8,128)(2,1)S(1)} collective-permute-done((bf16[4,16,128]{2,1,0:T(8,128)(2,1)S(1)}, bf16[4,16,128]{2,1,0:T(8,128)(2,1)S(1)}, u32[]{:S(2)}, u32[]{:S(2)}) %collective-permute-start.4) | collective-permute-done | bytes 16416 | tf_op jit(solution)/shard_map/ppermute | solution.py:751
  10.6 0.0 collective-permute-done.refs_1_.r1
  10.6 0.0 collective-permute-done.1.refs_2_.r2
  10.6 0.0 copy-start
  10.6 0.9 %merge.1 = (f32[4,7,16,128]{3,2,1,0:T(8,128)S(1)}, bf16[49,16,128]{2,1,0:T(8,128)(2,1)S(1)}, bf16[49,16,128]{2,1,0:T(8,128)(2,1)S(1)}) custom-call(bf16[4,4,8,16,128]{4,3,2,1,0:T(8,128)(2,1)S(1)} %get-tuple-element.17.refs_0_.tiles, bf16[52,16,128]{2,1,0:T(8,128)(2,1)S(1)} %collective-permute-done.refs_1_.r1, ...), custom_call_target="tpu_custom_call" | custom-call | tf_op jit(solution)/shard_map/merge/pallas_call | solution.py:805
  11.5 1.6 %collective-permute-start.5 = (bf16[49,16,128]{2,1,0:T(8,128)(2,1)S(1)}, bf16[49,16,128]{2,1,0:T(8,128)(2,1)S(1)}, u32[]{:S(2)}, u32[]{:S(2)}) collective-permute-start(bf16[49,16,128]{2,1,0:T(8,128)(2,1)S(1)} %get-tuple-element.23.y1), channel_id=1, source_target_pairs={{0,2},{1,3},{2,0},{3,1},{4,6},{5,7},{6,4},{7,5},{8,10},{9,11},{10,... | collective-permute-start | bytes 602120 | tf_op jit(solution)/shard_map/ppermute | solution.py:751
  13.1 0.0 copy-start.1
  13.1 0.0 copy-start.2
  13.1 1.7 %collective-permute-start.6 = (bf16[49,16,128]{2,1,0:T(8,128)(2,1)S(1)}, bf16[49,16,128]{2,1,0:T(8,128)(2,1)S(1)}, u32[]{:S(2)}, u32[]{:S(2)}) collective-permute-start(bf16[49,16,128]{2,1,0:T(8,128)(2,1)S(1)} %get-tuple-element.24.y2), channel_id=1, source_target_pairs={{0,1},{1,0},{2,4},{3,5},{4,2},{5,3},{6,7},{7,6},{8,9},{9,8},{10,12... | collective-permute-start | bytes 602120 | tf_op jit(solution)/shard_map/ppermute | solution.py:751
  14.8 0.0 copy-done
  14.8 0.0 copy-done.1
  14.8 0.0 copy-done.2
  14.8 4.1 %inner.1 = (f32[512,128]{1,0:T(8,128)}, f32[6,6,8,128]{3,2,1,0:T(8,128)S(1)}, f32[5,6,8,128]{3,2,1,0:T(8,128)S(1)}, f32[7,4,8,128]{3,2,1,0:T(8,128)S(1)}, f32[4,...) custom-call(bf16[4,4,8,16,128]{4,3,2,1,0:T(8,128)(2,1)S(1)} %get-tuple-element.17.refs_0_.tiles, ...), custom_call_target="tpu_custom_call" | custom-call | flops 20000000 | bytes 12000000 | tf_op jit(solution)/shard_map/inner/pallas_call | solution.py:818
  18.9 0.5 %collective-permute-done.5.r1 = bf16[49,16,128]{2,1,0:T(8,128)(2,1)S(1)} collective-permute-done((bf16[49,16,128]{2,1,0:T(8,128)(2,1)S(1)}, bf16[49,16,128]{2,1,0:T(8,128)(2,1)S(1)}, u32[]{:S(2)}, u32[]{:S(2)}) %collective-permute-start.5) | collective-permute-done | bytes 200736 | tf_op jit(solution)/shard_map/ppermute | solution.py:751
  19.4 1.3 %collective-permute-done.6.r2 = bf16[49,16,128]{2,1,0:T(8,128)(2,1)S(1)} collective-permute-done((bf16[49,16,128]{2,1,0:T(8,128)(2,1)S(1)}, bf16[49,16,128]{2,1,0:T(8,128)(2,1)S(1)}, u32[]{:S(2)}, u32[]{:S(2)}) %collective-permute-start.6) | collective-permute-done | bytes 200736 | tf_op jit(solution)/shard_map/ppermute | solution.py:751
  20.7 3.7 %finish.1 = (f32[16,4,8,128]{3,2,1,0:T(8,128)}, f32[4,8,128]{2,1,0:T(8,128)}) custom-call(bf16[49,16,128]{2,1,0:T(8,128)(2,1)S(1)} %get-tuple-element.23.y1, bf16[49,16,128]{2,1,0:T(8,128)(2,1)S(1)} %get-tuple-element.24.y2, bf16[49,16,128]{2,1,0:T(8,128)(2,1)S(1)} %collective-permute-done.5.r1, ...), custom_call_target="tpu_custom_call", output_to_operand_aliasing={{0}: (10, {})} | custom-call | tf_op jit(solution)/shard_map/finish/pallas_call | solution.py:841
Async XLA Ops:
  2.3 8.3 %collective-permute-start = (bf16[52,16,128]{2,1,0:T(8,128)(2,1)S(1)}, bf16[52,16,128]{2,1,0:T(8,128)(2,1)S(1)}, u32[]{:S(2)}, u32[]{:S(2)}) collective-permute-start(bf16[52,16,128]{2,1,0:T(8,128)(2,1)S(1)} %get-tuple-element.18), channel_id=1, source_target_pairs={{0,8},{1,9},{8,0},{9,1},{16,24},{17,25},{24,16},{25,17},{2,10},{3,... | collective-permute-start | bytes 638984 | tf_op jit(solution)/shard_map/ppermute | solution.py:751
  2.8 7.8 %collective-permute-start.1 = (bf16[52,16,128]{2,1,0:T(8,128)(2,1)S(1)}, bf16[52,16,128]{2,1,0:T(8,128)(2,1)S(1)}, u32[]{:S(2)}, u32[]{:S(2)}) collective-permute-start(bf16[52,16,128]{2,1,0:T(8,128)(2,1)S(1)} %get-tuple-element.19), channel_id=1, source_target_pairs={{0,1},{1,0},{8,16},{9,17},{16,8},{17,9},{24,25},{25,24},{2,3},{3,2... | collective-permute-start | bytes 638984 | tf_op jit(solution)/shard_map/ppermute | solution.py:751
  5.3 4.4 %collective-permute-start.2 = (bf16[4,16,128]{2,1,0:T(8,128)(2,1)S(1)}, bf16[4,16,128]{2,1,0:T(8,128)(2,1)S(1)}, u32[]{:S(2)}, u32[]{:S(2)}) collective-permute-start(bf16[4,16,128]{2,1,0:T(8,128)(2,1)S(1)} %get-tuple-element.20), channel_id=1, source_target_pairs={{0,1},{1,0},{8,9},{9,8},{16,17},{17,16},{24,25},{25,24},{2,3},{3,2... | collective-permute-start | bytes 49160 | tf_op jit(solution)/shard_map/ppermute | solution.py:751
  5.4 4.3 %collective-permute-start.3 = (bf16[4,16,128]{2,1,0:T(8,128)(2,1)S(1)}, bf16[4,16,128]{2,1,0:T(8,128)(2,1)S(1)}, u32[]{:S(2)}, u32[]{:S(2)}) collective-permute-start(bf16[4,16,128]{2,1,0:T(8,128)(2,1)S(1)} %get-tuple-element.21), channel_id=1, source_target_pairs={{0,9},{1,8},{8,1},{9,0},{16,25},{17,24},{24,17},{25,16},{2,11},{3,... | collective-permute-start | bytes 49160 | tf_op jit(solution)/shard_map/ppermute | solution.py:751
  6.8 3.7 %collective-permute-start.4 = (bf16[4,16,128]{2,1,0:T(8,128)(2,1)S(1)}, bf16[4,16,128]{2,1,0:T(8,128)(2,1)S(1)}, u32[]{:S(2)}, u32[]{:S(2)}) collective-permute-start(bf16[4,16,128]{2,1,0:T(8,128)(2,1)S(1)} %get-tuple-element.22), channel_id=1, source_target_pairs={{0,1},{1,0},{8,17},{9,16},{16,9},{17,8},{24,25},{25,24},{2,3},{3,2... | collective-permute-start | bytes 49160 | tf_op jit(solution)/shard_map/ppermute | solution.py:751
  10.6 4.2 %copy-start = (f32[6,4,8,128]{3,2,1,0:T(8,128)S(1)}, f32[6,4,8,128]{3,2,1,0:T(8,128)}, u32[]{:S(2)}) copy-start(f32[6,4,8,128]{3,2,1,0:T(8,128)} %stress.1) | copy-start | bytes 294916
  11.5 7.9 %collective-permute-start.5 = (bf16[49,16,128]{2,1,0:T(8,128)(2,1)S(1)}, bf16[49,16,128]{2,1,0:T(8,128)(2,1)S(1)}, u32[]{:S(2)}, u32[]{:S(2)}) collective-permute-start(bf16[49,16,128]{2,1,0:T(8,128)(2,1)S(1)} %get-tuple-element.23.y1), channel_id=1, source_target_pairs={{0,2},{1,3},{2,0},{3,1},{4,6},{5,7},{6,4},{7,5},{8,10},{9,11},{10,... | collective-permute-start | bytes 602120 | tf_op jit(solution)/shard_map/ppermute | solution.py:751
  13.1 1.7 %copy-start.1 = (f32[16]{0:T(128)S(1)}, f32[16]{0:T(128)}, u32[]{:S(2)}) copy-start(f32[16]{0:T(128)} %eig.1) | copy-start | bytes 196
  13.1 1.7 %copy-start.2 = (f32[16]{0:T(128)S(1)}, f32[16]{0:T(128)}, u32[]{:S(2)}) copy-start(f32[16]{0:T(128)} %weight.1) | copy-start | bytes 196
  13.1 7.6 %collective-permute-start.6 = (bf16[49,16,128]{2,1,0:T(8,128)(2,1)S(1)}, bf16[49,16,128]{2,1,0:T(8,128)(2,1)S(1)}, u32[]{:S(2)}, u32[]{:S(2)}) collective-permute-start(bf16[49,16,128]{2,1,0:T(8,128)(2,1)S(1)} %get-tuple-element.24.y2), channel_id=1, source_target_pairs={{0,1},{1,0},{2,4},{3,5},{4,2},{5,3},{6,7},{7,6},{8,9},{9,8},{10,12... | collective-permute-start | bytes 602120 | tf_op jit(solution)/shard_map/ppermute | solution.py:751

commit v3 on v2

--- a/solution.py
+++ b/solution.py
@@ -45,14 +45,14 @@
 
 
 HALF = 8
-PITCH = 40
+PITCH = 33
 
 
 def pair_up(first, second):
     return jnp.concatenate([first[:HALF].astype(F32), second[:HALF].astype(F32)], 0).astype(BF16)
 
 
-def pack_kernel(dims, modes_in, material_in, fixed_in, disp_in, tiles, x1, x2, edge, ex1, ex2, modes, material, fixed, disp, raw, sems):
+def pack_kernel(dims, modes_in, material_in, fixed_in, disp_in, tiles, x1, x2, edge, ex1, ex2, modes, material, fixed, disp, raw, chosen, sems):
     nx, ny = dims
     copies = [
         pltpu.make_async_copy(src, dst, sems.at[i])
@@ -64,6 +64,12 @@
     for copy in copies:
         copy.start()
     part = nx * ny
+    col = lane_iota((LANES, LANES))
+    kind = lax.rem(col, 3)
+    wanted = jnp.where(row_iota((LANES, LANES)) == jnp.where(kind == 0, LANES - 1, kind - 1), 1.0, 0.0)
+    for y in range(ny):
+        table = jnp.where((col >= 3 * y) & (col < 3 * y + 3), wanted, 0.0)
+        chosen[y * LANES : (y + 1) * LANES, :] = table.astype(BF16)
 
     def store(c, m, value):
         start = (c * MODES + m) * PITCH
@@ -94,15 +100,8 @@
         store(3, m, jnp.zeros((part, LANES), F32))
     spread(3)
 
-    col = lane_iota((LANES, LANES))
-    kind = lax.rem(col, 3)
-    wanted = row_iota((LANES, LANES)) == jnp.where(kind == 0, LANES - 1, kind - 1)
-    ends = None
-    for y in range(ny):
-        chosen = jnp.where(wanted & (col >= 3 * y) & (col < 3 * y + 3), 1.0, 0.0).astype(BF16)
-        block = tiles[:, :, y].reshape(GROUPS * nx * MODES, LANES)
-        term = jnp.dot(block, chosen, preferred_element_type=F32)
-        ends = term if ends is None else ends + term
+    block = jnp.concatenate([tiles[:, :, y].reshape(GROUPS * nx * MODES, LANES) for y in range(ny)], 1)
+    ends = jnp.dot(block, chosen[...], preferred_element_type=F32)
     ends = ends.reshape(GROUPS, nx, MODES, LANES)
     pieces = LANES // nx
     even, _, _ = place("gx")
@@ -137,54 +136,36 @@
     pl.when(jnp.logical_not(upper))(none_upper)
 
 
+def z_partners(zcount):
+    even, lower, upper = place("gz")
+    lower, upper = lower.astype(F32), upper.astype(F32)
+    if zcount == 1:
+        return [(lower, upper)]
+    even = even.astype(F32)
+    return [(lower * (1.0 - even), upper * even), (lower * even, upper * (1.0 - even))]
+
+
 def merge_kernel(dims, zcount, *refs):
     nx, ny = dims
-    tiles, r1, r2 = refs[:3]
-    rz = refs[3 : 3 + zcount]
-    rz1 = refs[3 + zcount : 3 + 2 * zcount]
-    rz2 = refs[3 + 2 * zcount : 3 + 3 * zcount]
-    rim, y1, y2, rows_aux = refs[3 + 3 * zcount :]
+    rz2 = refs[:zcount]
+    rz1 = refs[zcount : 2 * zcount]
+    rz = refs[2 * zcount : 3 * zcount]
+    r2, r1, tiles = refs[3 * zcount : 3 + 3 * zcount]
+    y1, y2, rows_aux, ends_here = refs[3 + 3 * zcount :]
     xe, xlo, xup = place("gx")
-    ze, zlo, zup = place("gz")
     ye, _, _ = place("gy")
     width = nx + 3
     pieces = LANES // nx
-    lane = lane_iota()
-    phase = lax.rem(lane, 3)
-    kept = lane < 3 * ny
-    even_f = ze.astype(F32)
-    low_mask = jnp.where(kept & (phase == 0), zlo.astype(F32), 0.0)
-    high_mask = jnp.where(kept & (phase != 0), zup.astype(F32), 0.0)
-    whole = low_mask + high_mask
-
-    def merged(blocks, slot):
-        turned = [roll(b.astype(F32), LANES - pieces * slot) for b in blocks]
-        if len(turned) == 1:
-            return turned[0] * whole
-        first, second = turned
-        low = second * even_f + first * (1.0 - even_f)
-        high = first * even_f + second * (1.0 - even_f)
-        return low * low_mask + high * high_mask
-
-    for c in range(GROUPS):
-        for x in range(nx):
-            rim[c, x + 1] = merged([r[c] for r in rz], x)
-
-        def rim_lower(refs, c=c):
-            rim[c, 0] = merged([r[c] for r in refs], 0)
-
-        def rim_upper(refs, c=c):
-            for s in range(2):
-                rim[c, nx + 1 + s] = merged([r[c] for r in refs], s)
-
-        def rim_no_lower(c=c):
-            rim[c, 0] = jnp.zeros((MODES, LANES), F32)
-
-        def rim_no_upper(c=c):
-            for s in range(2):
-                rim[c, nx + 1 + s] = jnp.zeros((MODES, LANES), F32)
-
-        pick(xe, xlo, xup, rz1, rz2, rim_lower, rim_upper, rim_no_lower, rim_no_upper)
+    sides = z_partners(zcount)
+    row = row_iota((LANES, LANES))
+    col = lane_iota((LANES, LANES))
+    turn = lax.rem(row, pieces)
+    slot = row // pieces
+    end = lax.rem(col, 16)
+    layer = col // 16
+    usable = (turn < 3 * ny) & (end < 6)
+    low_side = jnp.where(usable & (lax.rem(turn, 3) == 0), 1.0, 0.0)
+    high_side = jnp.where(usable & (lax.rem(turn, 3) != 0), 1.0, 0.0)
 
     blank = jnp.zeros((MODES, LANES), BF16)
     blank_half = jnp.zeros((HALF, LANES), F32)
@@ -233,13 +214,31 @@
         for x in range(0, nx + 2, 2):
             out[base + x // 2] = jnp.concatenate([rows_aux[x], rows_aux[x + 1]], 0).astype(BF16)
         base += (nx + 2) // 2
-        for c in range(GROUPS):
-            ends = jnp.zeros((MODES, LANES), F32)
-            for x in range(width):
-                start = 16 * x
-                turned = roll(rim[c, x], lax.rem(start + LANES - 3 * rows[0], LANES))
-                ends = jnp.where((lane >= start) & (lane < start + 6), turned, ends)
-            out[base + c] = ends.astype(BF16)
+        match = turn == end + 3 * rows[0]
+        tables = [jnp.where(match, low_side * lo + high_side * up, 0.0) for lo, up in sides]
+
+        def chosen(refs, offset, count):
+            total = None
+            for ref, table in zip(refs, tables, strict=True):
+                wanted = jnp.where((layer == slot + offset) & (slot < count), table, 0.0).astype(BF16)
+                block = ref[...].reshape(GROUPS * MODES, LANES)
+                term = jnp.dot(block, wanted, preferred_element_type=F32)
+                total = term if total is None else total + term
+            return total
+
+        ends_here[...] = chosen(rz, 1, nx)
+
+        def add_lower(refs, chosen=chosen):
+            ends_here[...] += chosen(refs, 0, 1)
+
+        def add_upper(refs, chosen=chosen):
+            ends_here[...] += chosen(refs, nx + 1, 2)
+
+        def nothing():
+            pass
+
+        pick(xe, xlo, xup, rz1, rz2, add_lower, add_upper, nothing, nothing)
+        out[base : base + GROUPS] = ends_here[...].reshape(GROUPS, MODES, LANES).astype(BF16)
 
 
 def cross_xy(a, b):
@@ -332,22 +331,27 @@
     return jnp.where(lax.rem(row, 2) == 0, step[0] + roll(step[0], 7, 0), step[1] + roll(step[1], 1, 0))
 
 
-def z_table(kind):
-    row = row_iota((2 * LANES, 2 * LANES))
-    col = lane_iota((2 * LANES, 2 * LANES))
+def z_table():
+    row = row_iota((LANES, 2 * LANES))
+    col = lane_iota((LANES, 2 * LANES))
     z = jnp.where(col < LANES, col, col - LANES)
     own = jnp.where(row == z, jnp.where(col < LANES, 1.0, -1.0), 0.0)
-    after = jnp.where((row == z + 1) & (row < LANES), 1.0, 0.0)
-    rim = jnp.where((z == LANES - 1) & (row == LANES + kind), 1.0, 0.0)
-    return (own + after + rim).astype(BF16)
+    return (own + jnp.where(row == z + 1, 1.0, 0.0)).astype(BF16)
+
+
+def rim_table(kind):
+    row = row_iota((LANES, 2 * LANES))
+    z = lax.rem(lane_iota((LANES, 2 * LANES)), LANES)
+    return jnp.where((z == LANES - 1) & (row == kind), 1.0, 0.0).astype(BF16)
 
 
 def first_column(lane_to):
     return jnp.where((row_iota((LANES, LANES)) == 0) & (lane_iota((LANES, LANES)) == lane_to), 1.0, 0.0).astype(BF16)
 
 
-def rows_along_z(block, rim, kind, sz, dz, at):
-    both = jnp.dot(jnp.concatenate([block, rim], 1), z_table(kind), preferred_element_type=F32)
+def rows_along_z(block, rim, kind, table, sz, dz, at):
+    table[LANES:, :] = rim_table(kind)
+    both = jnp.dot(jnp.concatenate([block, rim], 1), table[...], preferred_element_type=F32)
     sz[at] = both[:, :LANES].reshape(sz.shape[1:])
     dz[at] = both[:, LANES:].reshape(dz.shape[1:])
 
@@ -372,12 +376,52 @@
 FIELDS = 5
 
 
-def inner_kernel(dims, tiles, r1, r2, rim, stress, eig, weight, sens, wmain, field, cell, zr, scale, full, sz, dz, part, aux):
+def inner_kernel(dims, zcount, *refs):
+    rz = refs[:zcount]
+    rz1 = refs[zcount : 2 * zcount]
+    rz2 = refs[2 * zcount : 3 * zcount]
+    tiles, r1, r2, stress, eig, weight = refs[3 * zcount : 3 * zcount + 6]
+    sens, wmain, field, cell, zr, scale, rim, full, sz, dz, part, aux, table = refs[3 * zcount + 6 :]
     nx, ny = dims
     width = nx + 3
     tall = ny + 3
     lane = lane_iota()
     xe, xlo, xup = place("gx")
+    table[0:LANES, :] = z_table()
+
+    pieces = LANES // nx
+    sides = z_partners(zcount)
+    low_lane = (lane < 3 * ny) & (lax.rem(lane, 3) == 0)
+    high_lane = (lane < 3 * ny) & (lax.rem(lane, 3) != 0)
+
+    def merged(blocks, slot):
+        total = None
+        for block, (lo, up) in zip(blocks, sides, strict=True):
+            mask = jnp.where(low_lane, lo, 0.0) + jnp.where(high_lane, up, 0.0)
+            term = roll(block.astype(F32), LANES - pieces * slot) * mask
+            total = term if total is None else total + term
+        return total
+
+    for c in range(GROUPS):
+        for x in range(nx):
+            rim[c, x + 1] = merged([r[c] for r in rz], x)
+
+    def rim_lower(refs):
+        for c in range(GROUPS):
+            rim[c, 0] = merged([r[c] for r in refs], 0)
+
+    def rim_upper(refs):
+        for c in range(GROUPS):
+            for s in range(2):
+                rim[c, nx + 1 + s] = merged([r[c] for r in refs], s)
+
+    def rim_no_lower():
+        rim[:, 0] = jnp.zeros((GROUPS, MODES, LANES), F32)
+
+    def rim_no_upper():
+        rim[:, nx + 1 : nx + 3] = jnp.zeros((GROUPS, 2, MODES, LANES), F32)
+
+    pick(xe, xlo, xup, rz1, rz2, rim_lower, rim_upper, rim_no_lower, rim_no_upper)
 
     full[:, 1 : nx + 1] = tiles[0:3]
     for x in range(nx):
@@ -417,7 +461,7 @@
     column = None
     for y in range(ny):
         block = full[:, :, y].reshape(count, LANES)
-        rows_along_z(block, ends, 3 * y + 1, sz, dz, y)
+        rows_along_z(block, ends, 3 * y + 1, table, sz, dz, y)
         term = jnp.dot(block, first_column(3 * tall + y + 1), preferred_element_type=F32)
         column = term if column is None else column + term
     column = column.reshape(3, width, MODES, LANES)
@@ -487,13 +531,14 @@
         sweep(i * (nx + 1), False)
 
 
-def final_kernel(dims, y1, y2, r1, r2, rim, wmain, field_in, cell, zr, scale, sens_in, sens, adjoint, rows, rows_aux, rows_end, sz, dz, sum_z, w, zt, field, shear, load, stage, last, sems):
-    del sens_in
+def final_kernel(dims, y1, y2, r1, r2, wmain, field_in, cell, zr, scale, sens_in, sens, adjoint, rows, rows_aux, rows_end, sz, dz, sum_z, w, zt, field, shear, load, stage, whole, table, sem):
     nx, ny = dims
     width = nx + 3
     tall = ny + 3
     lane = lane_iota()
     ye, ylo, yup = place("gy")
+    table[0:LANES, :] = z_table()
+    whole[...] = sens_in[...]
 
     def copy_rows(to, ref, slot):
         for i in range(3 * width):
@@ -562,7 +607,7 @@
         zt[c] = stacked.T
     ends = jnp.concatenate(full_rim[:3], 0).astype(BF16)
     for i in range(5):
-        rows_along_z(rows[i].reshape(count, LANES), ends, 3 * at[i] + 1, sz, dz, i)
+        rows_along_z(rows[i].reshape(count, LANES), ends, 3 * at[i] + 1, table, sz, dz, i)
 
     w[:, :, 0:8, 0:LANES] = wmain[...]
 
@@ -577,15 +622,24 @@
                 quad, energy = forms([combos(now[c], after[c]) for c in range(3)], own)
                 if own:
                     fields = [cell[k, x - 1, ny - 1 : ny, :] for k in range(7)]
-                    last[x - 1, pl.ds(8 * h, 8), :] = mode_value(quad, energy, fields, scale[0, 8 * h : 8 * h + 8])
+                    start = 8 * h * nx * ny + x * ny - 1
+                    value = mode_value(quad, energy, fields, scale[0, 8 * h : 8 * h + 8])
+                    whole[pl.ds(start, 8, stride=nx * ny), :] = value
                 for k in range(6):
                     if h == 0:
                         sum_z[k, i] = coef * quad[k]
                     else:
-                        total = jnp.sum(sum_z[k, i] + coef * quad[k], axis=0, keepdims=True)
-                        row = (0, ny, ny + 1)[i]
-                        w[k, x, row : row + 1, 0:LANES] = total
+                        sum_z[k, i] += coef * quad[k]
                 now = after
+        pairs = [(k, i) for k in range(6) for i in range(3)]
+        for start in range(0, len(pairs), 8):
+            some = pairs[start : start + 8]
+            values = [sum_z[k, i] for k, i in some]
+            values += [jnp.zeros((8, LANES), F32)] * (8 - len(some))
+            folded = fold_rows(values)
+            for j, (k, i) in enumerate(some):
+                row = (0, ny, ny + 1)[i]
+                w[k, x, row : row + 1, 0:LANES] = folded[j : j + 1]
 
     @pl.loop(1, nx + 1)
     def _(x):
@@ -595,9 +649,8 @@
     def _(i):
         sweep(i * (nx + 1), False)
 
-    copies = [pltpu.make_async_copy(last.at[x], sens.at[:, x, ny - 1], sems.at[x]) for x in range(nx)]
-    for copy in copies:
-        copy.start()
+    copy = pltpu.make_async_copy(whole, sens, sem)
+    copy.start()
 
     for x in range(nx + 2):
         for k in range(FIELDS):
@@ -627,17 +680,19 @@
     for low, high in ((0, 3), (1, 2)):
         now, after = end_parts(low, high, 0), end_parts(low, high, 1)
         quad, _ = forms([combos(now[c], after[c]) for c in range(3)], False)
-        summed = []
-        for value in quad:
-            value = value * scale[2]
-            for shift in (1, 2, 4, 8):
-                value = value + roll(value, LANES - shift)
-            summed.append(value)
-        sides.append(summed)
+        sides.append([value * scale[2] for value in quad])
+
+    def narrow(first, second, shift):
+        kept = lax.rem(lane, 2 * shift) < shift
+        return jnp.where(kept, first + roll(first, LANES - shift), second + roll(second, shift))
+
+    step = [narrow(sides[0][i], sides[1][i], 1) for i in range(6)]
+    step = [narrow(step[i], step[i + 1], 2) for i in (0, 2, 4)]
+    step = [narrow(step[0], step[1], 4), step[2] + roll(step[2], LANES - 4)]
+    packed = narrow(step[0], step[1], 8)
     for i in range(6):
-        both = jnp.where(lax.rem(lane, 16) == 0, sides[1][i], roll(sides[0][i], LANES - 1))
         for x in range(nx + 2):
-            w[i, x, 0:16, LANES:] = roll(both, LANES - 16 * x)
+            w[i, x, 0:16, LANES:] = roll(packed, LANES - (16 * x + 2 * i + 1))
 
     def end_field(channel, x, first, with_low):
         value = roll(zt[3, pl.ds(3 * first + 1, 16, stride=3), :], LANES - (16 * x + channel))
@@ -727,8 +782,7 @@
         parts = [layer_combos(now[f], after[f]) for f in range(6)]
         adjoint[x] = cell[6, x] * bilinear(parts[:3], parts[3:])
         now = after
-    for copy in copies:
-        copy.wait()
+    copy.wait()
 
 
 def partner(index, size, kind):
@@ -788,6 +842,7 @@
             pltpu.VMEM(fixed_nodes.shape, fixed_nodes.dtype),
             pltpu.VMEM(displacement.shape, F32),
             pltpu.VMEM((GROUPS * MODES * PITCH, LANES), F32),
+            pltpu.VMEM((ny * LANES, LANES), BF16),
             pltpu.SemaphoreType.DMA((6,)),
         ],
         compiler_params=pltpu.CompilerParams(vmem_limit_bytes=8 << 20),
@@ -802,21 +857,21 @@
     rz1 = [swap(ex1, xz, (1, k), True) for k in zkinds]
     rz2 = [swap(ex2, xz, (2, k), True) for k in zkinds]
     count = 6 * width + (nx + 2) // 2 + GROUPS
-    rim, y1, y2 = pl.pallas_call(
+    y1, y2 = pl.pallas_call(
         functools.partial(merge_kernel, dims, len(zkinds)),
-        out_shape=(sds((GROUPS, width) + tile, F32), sds((count,) + tile, BF16), sds((count,) + tile, BF16)),
+        out_shape=(sds((count,) + tile, BF16), sds((count,) + tile, BF16)),
         in_specs=vmem(3 + 3 * len(zkinds)),
-        out_specs=tuple(vmem(3)),
-        scratch_shapes=[pltpu.VMEM((nx + 2, HALF, LANES), F32)],
+        out_specs=tuple(vmem(2)),
+        scratch_shapes=[pltpu.VMEM((nx + 2, HALF, LANES), F32), pltpu.VMEM((GROUPS * MODES, LANES), F32)],
         compiler_params=pltpu.CompilerParams(vmem_limit_bytes=8 << 20),
         name="merge",
-    )(tiles, r1, r2, *rz, *rz1, *rz2)
+    )(*rz2, *rz1, *rz, r2, r1, tiles)
 
     yz = ("gy", "gz")
     ry1 = swap(y1, yz, (1, 0), True)
-    ry2 = swap(y2, yz, (2, 0), True)
+    ry2 = swap(y2, ("gx", "gy"), (0, 2), True)
     sens, wmain, field, cell, zr, scale = pl.pallas_call(
-        functools.partial(inner_kernel, dims),
+        functools.partial(inner_kernel, dims, len(zkinds)),
         out_shape=(
             sds((MODES * nx * ny, LANES), F32),
             sds((6, nx + 2, 8, LANES), F32),
@@ -825,25 +880,26 @@
             sds((GROUPS, width) + tile, F32),
             sds((3,) + tile, F32),
         ),
-        in_specs=vmem(5) + [pl.BlockSpec(memory_space=pltpu.SMEM)] * 2,
+        in_specs=vmem(4 + 3 * len(zkinds)) + [pl.BlockSpec(memory_space=pltpu.SMEM)] * 2,
         out_specs=tuple(vmem(6)),
         scratch_shapes=[
+            pltpu.VMEM((GROUPS, width) + tile, F32),
             pltpu.VMEM((3, width, ny) + tile, BF16),
             pltpu.VMEM((ny, 3, width) + tile, F32),
             pltpu.VMEM((ny, 3, width) + tile, F32),
             pltpu.VMEM((6, ny - 1, 8, LANES), F32),
             pltpu.VMEM(((nx + 2) * ny * HALF, LANES), F32),
+            pltpu.VMEM((2 * LANES, 2 * LANES), BF16),
         ],
         compiler_params=pltpu.CompilerParams(vmem_limit_bytes=24 << 20),
         cost_estimate=pl.CostEstimate(flops=20_000_000, bytes_accessed=12_000_000, transcendentals=0),
         name="inner",
-    )(tiles, r1, r2, rim, stress_field, eigenvalues, mode_weight)
+    )(*rz, *rz1, *rz2, tiles, r1, r2, stress_field, eigenvalues, mode_weight)
     sens, adjoint = pl.pallas_call(
         functools.partial(final_kernel, dims),
-        out_shape=(sds((MODES, nx, ny, LANES), F32), sds((nx, ny, LANES), F32)),
-        in_specs=vmem(10) + anywhere(1),
+        out_shape=(sds((MODES * nx * ny, LANES), F32), sds((nx, ny, LANES), F32)),
+        in_specs=vmem(10),
         out_specs=(pl.BlockSpec(memory_space=pl.ANY), pl.BlockSpec(memory_space=pltpu.VMEM)),
-        input_output_aliases={10: 0},
         scratch_shapes=[
             pltpu.VMEM((5, 3 * width) + tile, BF16),
             pltpu.VMEM((2, (nx + 2) // 2) + tile, F32),
@@ -857,13 +913,14 @@
             pltpu.VMEM((8, 2, 24, LANES), F32),
             pltpu.VMEM((6, nx + 1, 2, 16, LANES), F32),
             pltpu.VMEM((2, 24, LANES), F32),
-            pltpu.VMEM((nx,) + tile, F32),
-            pltpu.SemaphoreType.DMA((nx,)),
+            pltpu.VMEM((MODES * nx * ny, LANES), F32),
+            pltpu.VMEM((2 * LANES, 2 * LANES), BF16),
+            pltpu.SemaphoreType.DMA,
         ],
         compiler_params=pltpu.CompilerParams(vmem_limit_bytes=24 << 20),
         name="finish",
-    )(y1, y2, ry1, ry2, rim, wmain, field, cell, zr, scale, sens.reshape(MODES, nx, ny, nz))
-    return sens, adjoint
+    )(y1, y2, ry1, ry2, wmain, field, cell, zr, scale, sens)
+    return sens.reshape(MODES, nx, ny, nz), adjoint
 
 
 def solution(mesh):

time: 24.6 us -> 22 us (0.89)
  starting transfers between devices: 9.37 us -> 7.51 us
  Pallas kernels: 10.3 us -> 9.55 us
  waiting for transfers between devices: 4.08 us -> 3.83 us
    ppermute x7, starting transfers between devices: 9.37 us -> 7.51 us  [swap(): return lax.ppermute(block, axes, route)]
    ppermute x7, waiting for transfers between devices: 4.08 us -> 3.83 us  [swap(): return lax.ppermute(block, axes, route)]
  transfers between devices with their start and end apart: 7 -> 7, of which waited for: 4 -> 4; matrix products, arithmetic and copies ran while one was open for 0% -> 0% of each run, Pallas kernels for 17% -> 18%
where the time goes in v3:
time: 22 us; the launch traced here: 21.6 us
  Pallas kernels  9.55 us (43%)
  starting transfers between devices  7.51 us (34%)
  waiting for transfers between devices  3.83 us (17%)
  between operations  0.68 us (3%)
    ppermute x7, starting transfers between devices, swap(): return lax.ppermute(block, axes, route)  7.51 us
    pallas_call x1, Pallas kernels, body(): pl.pallas_call(functools.partial(inner_kernel, dims, len(zkinds)), out_sh...  3.86 us
    ppermute x7, waiting for transfers between devices, swap(): return lax.ppermute(block, axes, route)  3.83 us
    pallas_call x1, Pallas kernels, body(): pl.pallas_call(functools.partial(final_kernel, dims), out_shape=(sds((MOD...  3.49 us
    pallas_call x1, Pallas kernels, body(): pl.pallas_call(functools.partial(pack_kernel, dims), out_shape=(sds((GROU...  1.55 us
    pallas_call x1, Pallas kernels, body(): pl.pallas_call(functools.partial(merge_kernel, dims, len(zkinds)), out_sh...  0.65 us
  transfers between devices with their start and end apart: 7, of which 4 were waited for; matrix products, arithmetic and copies ran while one was open for 0% of the time, Pallas kernels for 18%

profile of v3, /device:TPU:0, one launch (start us, length us, event | category | flops | bytes accessed | tf_op | source)
XLA Modules:
  0.0 21.6 jit_solution(4824911111474886191)
XLA Ops:
  0.6 1.5 %pack.1 = (bf16[4,4,8,16,128]{4,3,2,1,0:T(8,128)(2,1)S(1)}, bf16[52,16,128]{2,1,0:T(8,128)(2,1)S(1)}, bf16[52,16,128]{2,1,0:T(8,128)(2,1)S(1)}, bf16[4,16,128]{2...) custom-call(bf16[3,16,4,8,128]{4,3,2,1,0:T(8,128)(2,1)} %modes_in.1, ...), custom_call_target="tpu_custom_call" | custom-call | tf_op jit(solution)/shard_map/pack/pallas_call | solution.py:827
  2.2 3.0 %collective-permute-start.3 = (bf16[52,16,128]{2,1,0:T(8,128)(2,1)S(1)}, bf16[52,16,128]{2,1,0:T(8,128)(2,1)S(1)}, u32[]{:S(2)}, u32[]{:S(2)}) collective-permute-start(bf16[52,16,128]{2,1,0:T(8,128)(2,1)S(1)} %get-tuple-element.21), channel_id=1, source_target_pairs={{0,1},{1,0},{8,16},{9,17},{16,8},{17,9},{24,25},{25,24},{2,3},{3,2... | collective-permute-start | bytes 638984 | tf_op jit(solution)/shard_map/ppermute | solution.py:805
  5.2 0.1 collective-permute-start.4
  5.3 1.5 %collective-permute-start = (bf16[4,16,128]{2,1,0:T(8,128)(2,1)S(1)}, bf16[4,16,128]{2,1,0:T(8,128)(2,1)S(1)}, u32[]{:S(2)}, u32[]{:S(2)}) collective-permute-start(bf16[4,16,128]{2,1,0:T(8,128)(2,1)S(1)} %get-tuple-element.18), channel_id=1, source_target_pairs={{0,1},{1,0},{8,17},{9,16},{16,9},{17,8},{24,25},{25,24},{2,3},{3,2... | collective-permute-start | bytes 49160 | tf_op jit(solution)/shard_map/ppermute | solution.py:805
  6.8 0.6 %collective-permute-start.1 = (bf16[4,16,128]{2,1,0:T(8,128)(2,1)S(1)}, bf16[4,16,128]{2,1,0:T(8,128)(2,1)S(1)}, u32[]{:S(2)}, u32[]{:S(2)}) collective-permute-start(bf16[4,16,128]{2,1,0:T(8,128)(2,1)S(1)} %get-tuple-element.19), channel_id=1, source_target_pairs={{0,9},{1,8},{8,1},{9,0},{16,25},{17,24},{24,17},{25,16},{2,11},{3,... | collective-permute-start | bytes 49160 | tf_op jit(solution)/shard_map/ppermute | solution.py:805
  7.4 0.6 %collective-permute-start.2 = (bf16[4,16,128]{2,1,0:T(8,128)(2,1)S(1)}, bf16[4,16,128]{2,1,0:T(8,128)(2,1)S(1)}, u32[]{:S(2)}, u32[]{:S(2)}) collective-permute-start(bf16[4,16,128]{2,1,0:T(8,128)(2,1)S(1)} %get-tuple-element.20), channel_id=1, source_target_pairs={{0,1},{1,0},{8,9},{9,8},{16,17},{17,16},{24,25},{25,24},{2,3},{3,2... | collective-permute-start | bytes 49160 | tf_op jit(solution)/shard_map/ppermute | solution.py:805
  8.0 1.3 %collective-permute-done.refs_0_.refs_2_ = bf16[4,16,128]{2,1,0:T(8,128)(2,1)S(1)} collective-permute-done((bf16[4,16,128]{2,1,0:T(8,128)(2,1)S(1)}, bf16[4,16,128]{2,1,0:T(8,128)(2,1)S(1)}, u32[]{:S(2)}, u32[]{:S(2)}) %collective-permute-start) | collective-permute-done | bytes 16416 | tf_op jit(solution)/shard_map/ppermute | solution.py:805
  9.4 0.6 %collective-permute-done.1.refs_1_ = bf16[4,16,128]{2,1,0:T(8,128)(2,1)S(1)} collective-permute-done((bf16[4,16,128]{2,1,0:T(8,128)(2,1)S(1)}, bf16[4,16,128]{2,1,0:T(8,128)(2,1)S(1)}, u32[]{:S(2)}, u32[]{:S(2)}) %collective-permute-start.1) | collective-permute-done | bytes 16416 | tf_op jit(solution)/shard_map/ppermute | solution.py:805
  10.0 1.2 %collective-permute-done.2.refs_2_.refs_0_ = bf16[4,16,128]{2,1,0:T(8,128)(2,1)S(1)} collective-permute-done((bf16[4,16,128]{2,1,0:T(8,128)(2,1)S(1)}, bf16[4,16,128]{2,1,0:T(8,128)(2,1)S(1)}, u32[]{:S(2)}, u32[]{:S(2)}) %collective-permute-start.2) | collective-permute-done | bytes 16416 | tf_op jit(solution)/shard_map/ppermute | solution.py:805
  11.2 0.0 collective-permute-done.3.refs_3_.refs_5_
  11.2 0.0 collective-permute-done.4.refs_4_
  11.2 0.0 copy-start
  11.2 0.6 %merge.1 = (bf16[49,16,128]{2,1,0:T(8,128)(2,1)S(1)}, bf16[49,16,128]{2,1,0:T(8,128)(2,1)S(1)}) custom-call(bf16[4,16,128]{2,1,0:T(8,128)(2,1)S(1)} %collective-permute-done.refs_0_.refs_2_, bf16[4,16,128]{2,1,0:T(8,128)(2,1)S(1)} %collective-permute-done.1.refs_1_, bf16[4,16,128]{2,1,0:T(8,128)(2,1)S(1)} %collective-permute-done.2.refs_2_.refs_0_, ...), custom_call_target="tpu_custom_call" | custom-call | tf_op jit(solution)/shard_map/merge/pallas_call | solution.py:860
  11.8 0.0 copy-start.1
  11.9 0.0 copy-start.2
  11.9 1.6 %collective-permute-start.5 = (bf16[49,16,128]{2,1,0:T(8,128)(2,1)S(1)}, bf16[49,16,128]{2,1,0:T(8,128)(2,1)S(1)}, u32[]{:S(2)}, u32[]{:S(2)}) collective-permute-start(bf16[49,16,128]{2,1,0:T(8,128)(2,1)S(1)} %get-tuple-element.24.y1), channel_id=1, source_target_pairs={{0,2},{1,3},{2,0},{3,1},{4,6},{5,7},{6,4},{7,5},{8,10},{9,11},{10,... | collective-permute-start | bytes 602120 | tf_op jit(solution)/shard_map/ppermute | solution.py:805
  13.5 0.0 collective-permute-start.6
  13.5 0.0 copy-done
  13.5 0.0 copy-done.1
  13.5 0.0 copy-done.2
  13.5 3.9 %inner.1 = (f32[512,128]{1,0:T(8,128)S(1)}, f32[6,6,8,128]{3,2,1,0:T(8,128)S(1)}, f32[5,6,8,128]{3,2,1,0:T(8,128)S(1)}, f32[7,4,8,128]{3,2,1,0:T(8,128)S(1)}, f3...) custom-call(bf16[4,16,128]{2,1,0:T(8,128)(2,1)S(1)} %collective-permute-done.2.refs_2_.refs_0_, ...), custom_call_target="tpu_custom_call" | custom-call | flops 20000000 | bytes 12000000 | tf_op jit(solution)/shard_map/inner/pallas_call | solution.py:873
  17.4 0.7 %collective-permute-done.5.r1 = bf16[49,16,128]{2,1,0:T(8,128)(2,1)S(1)} collective-permute-done((bf16[49,16,128]{2,1,0:T(8,128)(2,1)S(1)}, bf16[49,16,128]{2,1,0:T(8,128)(2,1)S(1)}, u32[]{:S(2)}, u32[]{:S(2)}) %collective-permute-start.5) | collective-permute-done | bytes 200736 | tf_op jit(solution)/shard_map/ppermute | solution.py:805
  18.1 0.0 collective-permute-done.6.r2
  18.1 3.5 %finish.1 = (f32[512,128]{1,0:T(8,128)}, f32[4,8,128]{2,1,0:T(8,128)}) custom-call(bf16[49,16,128]{2,1,0:T(8,128)(2,1)S(1)} %get-tuple-element.24.y1, bf16[49,16,128]{2,1,0:T(8,128)(2,1)S(1)} %get-tuple-element.25.y2, bf16[49,16,128]{2,1,0:T(8,128)(2,1)S(1)} %collective-permute-done.5.r1, bf16[49,16,128]{2,1,0:T(8,128)(2,1)S(1)} %collective-permute-done.6.r2, ...), custom_call_target="tpu_custom_call" | custom-call | tf_op jit(solution)/shard_map/finish/pallas_call | solution.py:898
Async XLA Ops:
  2.2 9.0 %collective-permute-start.3 = (bf16[52,16,128]{2,1,0:T(8,128)(2,1)S(1)}, bf16[52,16,128]{2,1,0:T(8,128)(2,1)S(1)}, u32[]{:S(2)}, u32[]{:S(2)}) collective-permute-start(bf16[52,16,128]{2,1,0:T(8,128)(2,1)S(1)} %get-tuple-element.21), channel_id=1, source_target_pairs={{0,1},{1,0},{8,16},{9,17},{16,8},{17,9},{24,25},{25,24},{2,3},{3,2... | collective-permute-start | bytes 638984 | tf_op jit(solution)/shard_map/ppermute | solution.py:805
  5.2 6.0 %collective-permute-start.4 = (bf16[52,16,128]{2,1,0:T(8,128)(2,1)S(1)}, bf16[52,16,128]{2,1,0:T(8,128)(2,1)S(1)}, u32[]{:S(2)}, u32[]{:S(2)}) collective-permute-start(bf16[52,16,128]{2,1,0:T(8,128)(2,1)S(1)} %get-tuple-element.22), channel_id=1, source_target_pairs={{0,8},{1,9},{8,0},{9,1},{16,24},{17,25},{24,16},{25,17},{2,10},{3,... | collective-permute-start | bytes 638984 | tf_op jit(solution)/shard_map/ppermute | solution.py:805
  5.3 4.0 %collective-permute-start = (bf16[4,16,128]{2,1,0:T(8,128)(2,1)S(1)}, bf16[4,16,128]{2,1,0:T(8,128)(2,1)S(1)}, u32[]{:S(2)}, u32[]{:S(2)}) collective-permute-start(bf16[4,16,128]{2,1,0:T(8,128)(2,1)S(1)} %get-tuple-element.18), channel_id=1, source_target_pairs={{0,1},{1,0},{8,17},{9,16},{16,9},{17,8},{24,25},{25,24},{2,3},{3,2... | collective-permute-start | bytes 49160 | tf_op jit(solution)/shard_map/ppermute | solution.py:805
  6.8 3.2 %collective-permute-start.1 = (bf16[4,16,128]{2,1,0:T(8,128)(2,1)S(1)}, bf16[4,16,128]{2,1,0:T(8,128)(2,1)S(1)}, u32[]{:S(2)}, u32[]{:S(2)}) collective-permute-start(bf16[4,16,128]{2,1,0:T(8,128)(2,1)S(1)} %get-tuple-element.19), channel_id=1, source_target_pairs={{0,9},{1,8},{8,1},{9,0},{16,25},{17,24},{24,17},{25,16},{2,11},{3,... | collective-permute-start | bytes 49160 | tf_op jit(solution)/shard_map/ppermute | solution.py:805
  7.4 3.7 %collective-permute-start.2 = (bf16[4,16,128]{2,1,0:T(8,128)(2,1)S(1)}, bf16[4,16,128]{2,1,0:T(8,128)(2,1)S(1)}, u32[]{:S(2)}, u32[]{:S(2)}) collective-permute-start(bf16[4,16,128]{2,1,0:T(8,128)(2,1)S(1)} %get-tuple-element.20), channel_id=1, source_target_pairs={{0,1},{1,0},{8,9},{9,8},{16,17},{17,16},{24,25},{25,24},{2,3},{3,2... | collective-permute-start | bytes 49160 | tf_op jit(solution)/shard_map/ppermute | solution.py:805
  11.2 2.3 %copy-start = (f32[6,4,8,128]{3,2,1,0:T(8,128)S(1)}, f32[6,4,8,128]{3,2,1,0:T(8,128)}, u32[]{:S(2)}) copy-start(f32[6,4,8,128]{3,2,1,0:T(8,128)} %refs_6_.1) | copy-start | bytes 294916
  11.8 1.7 %copy-start.1 = (f32[16]{0:T(128)S(1)}, f32[16]{0:T(128)}, u32[]{:S(2)}) copy-start(f32[16]{0:T(128)} %refs_7_.1) | copy-start | bytes 196
  11.9 1.7 %copy-start.2 = (f32[16]{0:T(128)S(1)}, f32[16]{0:T(128)}, u32[]{:S(2)}) copy-start(f32[16]{0:T(128)} %refs_8_.1) | copy-start | bytes 196
  11.9 6.2 %collective-permute-start.5 = (bf16[49,16,128]{2,1,0:T(8,128)(2,1)S(1)}, bf16[49,16,128]{2,1,0:T(8,128)(2,1)S(1)}, u32[]{:S(2)}, u32[]{:S(2)}) collective-permute-start(bf16[49,16,128]{2,1,0:T(8,128)(2,1)S(1)} %get-tuple-element.24.y1), channel_id=1, source_target_pairs={{0,2},{1,3},{2,0},{3,1},{4,6},{5,7},{6,4},{7,5},{8,10},{9,11},{10,... | collective-permute-start | bytes 602120 | tf_op jit(solution)/shard_map/ppermute | solution.py:805
  13.5 4.6 %collective-permute-start.6 = (bf16[49,16,128]{2,1,0:T(8,128)(2,1)S(1)}, bf16[49,16,128]{2,1,0:T(8,128)(2,1)S(1)}, u32[]{:S(2)}, u32[]{:S(2)}) collective-permute-start(bf16[49,16,128]{2,1,0:T(8,128)(2,1)S(1)} %get-tuple-element.25.y2), channel_id=1, source_target_pairs={{0,8},{2,4},{4,2},{6,14},{8,0},{10,12},{12,10},{14,6},{16,24},{18,... | collective-permute-start | bytes 602120 | tf_op jit(solution)/shard_map/ppermute | solution.py:805

commit v4 on v3

--- a/solution.py
+++ b/solution.py
@@ -52,7 +52,7 @@
     return jnp.concatenate([first[:HALF].astype(F32), second[:HALF].astype(F32)], 0).astype(BF16)
 
 
-def pack_kernel(dims, modes_in, material_in, fixed_in, disp_in, tiles, x1, x2, edge, ex1, ex2, modes, material, fixed, disp, raw, chosen, sems):
+def pack_kernel(dims, zcount, modes_in, material_in, fixed_in, disp_in, tiles, x1, x2, edge, ex1, ex2, tables, modes, material, fixed, disp, raw, chosen, sems):
     nx, ny = dims
     copies = [
         pltpu.make_async_copy(src, dst, sems.at[i])
@@ -70,6 +70,11 @@
     for y in range(ny):
         table = jnp.where((col >= 3 * y) & (col < 3 * y + 3), wanted, 0.0)
         chosen[y * LANES : (y + 1) * LANES, :] = table.astype(BF16)
+
+    def store_table(index, table):
+        tables[index * LANES : (index + 1) * LANES, :] = table
+
+    rim_tables(dims, zcount, store_table)
 
     def store(c, m, value):
         start = (c * MODES + m) * PITCH
@@ -145,28 +150,54 @@
     return [(lower * (1.0 - even), upper * even), (lower * even, upper * (1.0 - even))]
 
 
-def merge_kernel(dims, zcount, *refs):
+def z_partners(zcount):
+    even, lower, upper = place("gz")
+    lower, upper = lower.astype(F32), upper.astype(F32)
+    if zcount == 1:
+        return [(lower, upper)]
+    even = even.astype(F32)
+    return [(lower * (1.0 - even), upper * even), (lower * even, upper * (1.0 - even))]
+
+
+def rim_tables(dims, zcount, store):
     nx, ny = dims
-    rz2 = refs[:zcount]
-    rz1 = refs[zcount : 2 * zcount]
-    rz = refs[2 * zcount : 3 * zcount]
-    r2, r1, tiles = refs[3 * zcount : 3 + 3 * zcount]
-    y1, y2, rows_aux, ends_here = refs[3 + 3 * zcount :]
+    pieces = LANES // nx
     xe, xlo, xup = place("gx")
     ye, _, _ = place("gy")
-    width = nx + 3
-    pieces = LANES // nx
-    sides = z_partners(zcount)
-    row = row_iota((LANES, LANES))
-    col = lane_iota((LANES, LANES))
+    xe, xlo, xup = xe.astype(F32), xlo.astype(F32), xup.astype(F32)
+    row = row_iota((LANES, 2 * LANES))
+    col = lane_iota((LANES, 2 * LANES))
+    second = col >= LANES
+    col = lax.rem(col, LANES)
     turn = lax.rem(row, pieces)
     slot = row // pieces
     end = lax.rem(col, 16)
     layer = col // 16
-    usable = (turn < 3 * ny) & (end < 6)
-    low_side = jnp.where(usable & (lax.rem(turn, 3) == 0), 1.0, 0.0)
-    high_side = jnp.where(usable & (lax.rem(turn, 3) != 0), 1.0, 0.0)
-
+    last = jnp.where(ye, 3 * ny - 3, 0)
+    first_row = jnp.where(second, 3 * ny - 3 - last, last)
+    fits = (turn == end + first_row) & (turn < 3 * ny) & (end < 6)
+    low = lax.rem(turn, 3) == 0
+    own = jnp.where(layer == slot + 1, 1.0, 0.0)
+    below = jnp.where((layer == 0) & (slot == 0), xlo, 0.0)
+    above = jnp.where((layer == slot + nx + 1) & (slot < 2), xup, 0.0)
+    by_kind = (below * xe + above * (1.0 - xe), above * xe + below * (1.0 - xe), own)
+    for z, (lower, upper) in enumerate(z_partners(zcount)):
+        valid = jnp.where(fits, jnp.where(low, lower, upper), 0.0)
+        for k, kind in enumerate(by_kind):
+            store(k * zcount + z, (valid * kind).astype(BF16))
+
+
+def merge_kernel(dims, zcount, *refs):
+    nx, ny = dims
+    zblocks = refs[: 3 * zcount]
+    r2, r1, tiles, tables, y1, y2, rows_aux = refs[3 * zcount :]
+    xe, xlo, xup = place("gx")
+    ye, _, _ = place("gy")
+    width = nx + 3
+    side = jnp.concatenate([ref[...].reshape(GROUPS * MODES, LANES) for ref in zblocks], 1)
+    ends = jnp.dot(side, tables[...], preferred_element_type=F32)
+    rows = [[jnp.where(up, ny - 1, s) for s in range(2)] for up in (ye, jnp.logical_not(ye))]
+    outs = (y1, y2)
     blank = jnp.zeros((MODES, LANES), BF16)
     blank_half = jnp.zeros((HALF, LANES), F32)
 
@@ -175,70 +206,48 @@
         odd = lax.rem(row, 2).astype(F32)
         return pairs[:HALF] * (1.0 - odd) + pairs[HALF:] * odd
 
-    for out, upward in ((y1, ye), (y2, jnp.logical_not(ye))):
-        rows = [jnp.where(upward, ny - 1, s) for s in range(2)]
+    def lower(ref):
+        for k in range(2):
+            for c in range(3):
+                for s in range(2):
+                    outs[k][c * width * 2 + s] = ref[c * 2 * ny + rows[k][s]]
+            rows_aux[k, 0] = half_of(ref, rows[k][0])
+
+    def upper(ref):
+        for k in range(2):
+            for c in range(3):
+                for t in range(2):
+                    for s in range(2):
+                        outs[k][(c * width + nx + 1 + t) * 2 + s] = ref[(c * 2 + t) * ny + rows[k][s]]
+            rows_aux[k, nx + 1] = half_of(ref, rows[k][0])
+
+    def no_lower():
+        for k in range(2):
+            for c in range(3):
+                for s in range(2):
+                    outs[k][c * width * 2 + s] = blank
+            rows_aux[k, 0] = blank_half
+
+    def no_upper():
+        for k in range(2):
+            for c in range(3):
+                for i in range(4):
+                    outs[k][(c * width + nx + 1) * 2 + i] = blank
+            rows_aux[k, nx + 1] = blank_half
+
+    pick(xe, xlo, xup, r1, r2, lower, upper, no_lower, no_upper)
+    base = 6 * width
+    for k, out in enumerate(outs):
         for c in range(3):
             for s in range(2):
                 for x in range(nx):
-                    out[(c * width + x + 1) * 2 + s] = tiles[c, x, rows[s]]
+                    out[(c * width + x + 1) * 2 + s] = tiles[c, x, rows[k][s]]
         for x in range(nx):
-            rows_aux[x + 1] = tiles[3, x, rows[0]][:HALF].astype(F32)
-
-        def lower(ref, out=out, rows=rows):
-            for c in range(3):
-                for s in range(2):
-                    out[c * width * 2 + s] = ref[c * 2 * ny + rows[s]]
-            rows_aux[0] = half_of(ref, rows[0])
-
-        def upper(ref, out=out, rows=rows):
-            for c in range(3):
-                for t in range(2):
-                    for s in range(2):
-                        out[(c * width + nx + 1 + t) * 2 + s] = ref[(c * 2 + t) * ny + rows[s]]
-            rows_aux[nx + 1] = half_of(ref, rows[0])
-
-        def no_lower(out=out):
-            for c in range(3):
-                for s in range(2):
-                    out[c * width * 2 + s] = blank
-            rows_aux[0] = blank_half
-
-        def no_upper(out=out):
-            for c in range(3):
-                for i in range(4):
-                    out[(c * width + nx + 1) * 2 + i] = blank
-            rows_aux[nx + 1] = blank_half
-
-        pick(xe, xlo, xup, r1, r2, lower, upper, no_lower, no_upper)
-        base = 6 * width
+            rows_aux[k, x + 1] = tiles[3, x, rows[k][0]][:HALF].astype(F32)
         for x in range(0, nx + 2, 2):
-            out[base + x // 2] = jnp.concatenate([rows_aux[x], rows_aux[x + 1]], 0).astype(BF16)
-        base += (nx + 2) // 2
-        match = turn == end + 3 * rows[0]
-        tables = [jnp.where(match, low_side * lo + high_side * up, 0.0) for lo, up in sides]
-
-        def chosen(refs, offset, count):
-            total = None
-            for ref, table in zip(refs, tables, strict=True):
-                wanted = jnp.where((layer == slot + offset) & (slot < count), table, 0.0).astype(BF16)
-                block = ref[...].reshape(GROUPS * MODES, LANES)
-                term = jnp.dot(block, wanted, preferred_element_type=F32)
-                total = term if total is None else total + term
-            return total
-
-        ends_here[...] = chosen(rz, 1, nx)
-
-        def add_lower(refs, chosen=chosen):
-            ends_here[...] += chosen(refs, 0, 1)
-
-        def add_upper(refs, chosen=chosen):
-            ends_here[...] += chosen(refs, nx + 1, 2)
-
-        def nothing():
-            pass
-
-        pick(xe, xlo, xup, rz1, rz2, add_lower, add_upper, nothing, nothing)
-        out[base : base + GROUPS] = ends_here[...].reshape(GROUPS, MODES, LANES).astype(BF16)
+            out[base + x // 2] = pair_up(rows_aux[k, x], rows_aux[k, x + 1])
+        block = ends[:, k * LANES : (k + 1) * LANES].reshape(GROUPS, MODES, LANES)
+        out[base + (nx + 2) // 2 :] = block.astype(BF16)
 
 
 def cross_xy(a, b):
@@ -514,21 +523,18 @@
                     sens[pl.ds(start, 8, stride=nx * ny), :] = mode_value(quad, energy, fields, eig_half)
                 for i in range(6):
                     if h == 0:
-                        part[i, y] = coef * quad[i]
+                        part[x, i, y] = coef * quad[i]
                     else:
-                        part[i, y] += coef * quad[i]
+                        part[x, i, y] += coef * quad[i]
                 now = after
         blank = jnp.zeros((8, LANES), F32)
         for i in range(6):
-            wmain[i, x] = fold_rows([blank] + [part[i, y] for y in range(ny - 1)])
-
-    @pl.loop(1, nx + 1)
-    def _(x):
+            wmain[i, x] = fold_rows([blank] + [part[x, i, y] for y in range(ny - 1)])
+
+    for x in range(1, nx + 1):
         sweep(x, True)
-
-    @pl.loop(0, 2)
-    def _(i):
-        sweep(i * (nx + 1), False)
+    for x in (0, nx + 1):
+        sweep(x, False)
 
 
 def final_kernel(dims, y1, y2, r1, r2, wmain, field_in, cell, zr, scale, sens_in, sens, adjoint, rows, rows_aux, rows_end, sz, dz, sum_z, w, zt, field, shear, load, stage, whole, table, sem):
@@ -641,13 +647,10 @@
                 row = (0, ny, ny + 1)[i]
                 w[k, x, row : row + 1, 0:LANES] = folded[j : j + 1]
 
-    @pl.loop(1, nx + 1)
-    def _(x):
+    for x in range(1, nx + 1):
         sweep(x, True)
-
-    @pl.loop(0, 2)
-    def _(i):
-        sweep(i * (nx + 1), False)
+    for x in (0, nx + 1):
+        sweep(x, False)
 
     copy = pltpu.make_async_copy(whole, sens, sem)
     copy.start()
@@ -824,8 +827,10 @@
     sds = jax.ShapeDtypeStruct
     tile = (MODES, LANES)
     layer = 6 * ny + ny // 2
-    tiles, x1, x2, edge, ex1, ex2 = pl.pallas_call(
-        functools.partial(pack_kernel, dims),
+    zkinds = (1,) if lax.axis_size("gz") == 2 else (1, 2)
+    zcount = len(zkinds)
+    tiles, x1, x2, edge, ex1, ex2, tables = pl.pallas_call(
+        functools.partial(pack_kernel, dims, zcount),
         out_shape=(
             sds((GROUPS, nx, ny) + tile, BF16),
             sds((layer,) + tile, BF16),
@@ -833,9 +838,10 @@
             sds((GROUPS,) + tile, BF16),
             sds((GROUPS,) + tile, BF16),
             sds((GROUPS,) + tile, BF16),
+            sds((3 * zcount * LANES, 2 * LANES), BF16),
         ),
         in_specs=anywhere(4),
-        out_specs=tuple(vmem(6)),
+        out_specs=tuple(vmem(7)),
         scratch_shapes=[
             pltpu.VMEM(mode_shapes.shape, BF16),
             pltpu.VMEM(material.shape, material.dtype),
@@ -850,7 +856,6 @@
     )(*(pltpu.with_memory_space_constraint(a, pltpu.HBM) for a in (mode_shapes, material, fixed_nodes, displacement)))
 
     xz = ("gx", "gz")
-    zkinds = (1,) if lax.axis_size("gz") == 2 else (1, 2)
     r2 = swap(x2, xz, (2, 0), True)
     r1 = swap(x1, xz, (1, 0), True)
     rz = [swap(edge, xz, (0, k), True) for k in zkinds]
@@ -858,20 +863,20 @@
     rz2 = [swap(ex2, xz, (2, k), True) for k in zkinds]
     count = 6 * width + (nx + 2) // 2 + GROUPS
     y1, y2 = pl.pallas_call(
-        functools.partial(merge_kernel, dims, len(zkinds)),
+        functools.partial(merge_kernel, dims, zcount),
         out_shape=(sds((count,) + tile, BF16), sds((count,) + tile, BF16)),
-        in_specs=vmem(3 + 3 * len(zkinds)),
+        in_specs=vmem(4 + 3 * zcount),
         out_specs=tuple(vmem(2)),
-        scratch_shapes=[pltpu.VMEM((nx + 2, HALF, LANES), F32), pltpu.VMEM((GROUPS * MODES, LANES), F32)],
+        scratch_shapes=[pltpu.VMEM((2, nx + 2, HALF, LANES), F32)],
         compiler_params=pltpu.CompilerParams(vmem_limit_bytes=8 << 20),
         name="merge",
-    )(*rz2, *rz1, *rz, r2, r1, tiles)
+    )(*rz2, *rz1, *rz, r2, r1, tiles, tables)
 
     yz = ("gy", "gz")
     ry1 = swap(y1, yz, (1, 0), True)
     ry2 = swap(y2, ("gx", "gy"), (0, 2), True)
     sens, wmain, field, cell, zr, scale = pl.pallas_call(
-        functools.partial(inner_kernel, dims, len(zkinds)),
+        functools.partial(inner_kernel, dims, zcount),
         out_shape=(
             sds((MODES * nx * ny, LANES), F32),
             sds((6, nx + 2, 8, LANES), F32),
@@ -880,14 +885,14 @@
             sds((GROUPS, width) + tile, F32),
             sds((3,) + tile, F32),
         ),
-        in_specs=vmem(4 + 3 * len(zkinds)) + [pl.BlockSpec(memory_space=pltpu.SMEM)] * 2,
+        in_specs=vmem(4 + 3 * zcount) + [pl.BlockSpec(memory_space=pltpu.SMEM)] * 2,
         out_specs=tuple(vmem(6)),
         scratch_shapes=[
             pltpu.VMEM((GROUPS, width) + tile, F32),
             pltpu.VMEM((3, width, ny) + tile, BF16),
             pltpu.VMEM((ny, 3, width) + tile, F32),
             pltpu.VMEM((ny, 3, width) + tile, F32),
-            pltpu.VMEM((6, ny - 1, 8, LANES), F32),
+            pltpu.VMEM((nx + 2, 6, ny - 1, 8, LANES), F32),
             pltpu.VMEM(((nx + 2) * ny * HALF, LANES), F32),
             pltpu.VMEM((2 * LANES, 2 * LANES), BF16),
         ],

time: 22 us -> 20.9 us (0.950)
  Pallas kernels: 9.55 us -> 8.36 us
    pallas_call x3, Pallas kernels: 6.05 us -> 5.25 us  [the longest x1 3.47 us: body(): pl.pallas_call(functools.partial(inner_kernel, dims, zcount), out_shape=(...]
    pallas_call x1, Pallas kernels: 3.49 us -> 3.11 us  [body(): pl.pallas_call(functools.partial(final_kernel, dims), out_shape=(sds((MOD...]
  transfers between devices with their start and end apart: 7 -> 7, of which waited for: 4 -> 4; matrix products, arithmetic and copies ran while one was open for 0% -> 0% of each run, Pallas kernels for 18% -> 17%
where the time goes in v4:
time: 20.9 us; the launch traced here: 20.5 us
  Pallas kernels  8.36 us (40%)
  starting transfers between devices  7.51 us (36%)
  waiting for transfers between devices  3.98 us (19%)
  between operations  0.69 us (3%)
    ppermute x7, starting transfers between devices, swap(): return lax.ppermute(block, axes, route)  7.51 us
    ppermute x7, waiting for transfers between devices, swap(): return lax.ppermute(block, axes, route)  3.98 us
    pallas_call x1, Pallas kernels, body(): pl.pallas_call(functools.partial(inner_kernel, dims, zcount), out_shape=(...  3.47 us
    pallas_call x1, Pallas kernels, body(): pl.pallas_call(functools.partial(final_kernel, dims), out_shape=(sds((MOD...  3.11 us
    pallas_call x1, Pallas kernels, body(): pl.pallas_call(functools.partial(pack_kernel, dims, zcount), out_shape=(s...  1.55 us
  transfers between devices with their start and end apart: 7, of which 4 were waited for; matrix products, arithmetic and copies ran while one was open for 0% of the time, Pallas kernels for 17%

profile of v4, /device:TPU:0, one launch (start us, length us, event | category | flops | bytes accessed | tf_op | source)
XLA Modules:
  0.0 20.5 jit_solution(17763049028012529305)
XLA Ops:
  0.6 1.5 %pack.1 = (bf16[4,4,8,16,128]{4,3,2,1,0:T(8,128)(2,1)S(1)}, bf16[52,16,128]{2,1,0:T(8,128)(2,1)S(1)}, bf16[52,16,128]{2,1,0:T(8,128)(2,1)S(1)}, bf16[4,16,128]{2...) custom-call(bf16[3,16,4,8,128]{4,3,2,1,0:T(8,128)(2,1)} %modes_in.1,, ...), custom_call_target="tpu_custom_call" | custom-call | tf_op jit(solution)/shard_map/pack/pallas_call | solution.py:832
  2.2 3.0 %collective-permute-start.3 = (bf16[52,16,128]{2,1,0:T(8,128)(2,1)S(1)}, bf16[52,16,128]{2,1,0:T(8,128)(2,1)S(1)}, u32[]{:S(2)}, u32[]{:S(2)}) collective-permute-start(bf16[52,16,128]{2,1,0:T(8,128)(2,1)S(1)} %get-tuple-element.22), channel_id=1, source_target_pairs={{0,1},{1,0},{8,16},{9,17},{16,8},{17,9},{24,25},{25,24},{2,3},{3,2... | collective-permute-start | bytes 638984 | tf_op jit(solution)/shard_map/ppermute | solution.py:808
  5.2 0.1 collective-permute-start.4
  5.3 1.5 %collective-permute-start = (bf16[4,16,128]{2,1,0:T(8,128)(2,1)S(1)}, bf16[4,16,128]{2,1,0:T(8,128)(2,1)S(1)}, u32[]{:S(2)}, u32[]{:S(2)}) collective-permute-start(bf16[4,16,128]{2,1,0:T(8,128)(2,1)S(1)} %get-tuple-element.19), channel_id=1, source_target_pairs={{0,1},{1,0},{8,17},{9,16},{16,9},{17,8},{24,25},{25,24},{2,3},{3,2... | collective-permute-start | bytes 49160 | tf_op jit(solution)/shard_map/ppermute | solution.py:808
  6.8 0.6 %collective-permute-start.1 = (bf16[4,16,128]{2,1,0:T(8,128)(2,1)S(1)}, bf16[4,16,128]{2,1,0:T(8,128)(2,1)S(1)}, u32[]{:S(2)}, u32[]{:S(2)}) collective-permute-start(bf16[4,16,128]{2,1,0:T(8,128)(2,1)S(1)} %get-tuple-element.20), channel_id=1, source_target_pairs={{0,9},{1,8},{8,1},{9,0},{16,25},{17,24},{24,17},{25,16},{2,11},{3,... | collective-permute-start | bytes 49160 | tf_op jit(solution)/shard_map/ppermute | solution.py:808
  7.4 0.6 %collective-permute-start.2 = (bf16[4,16,128]{2,1,0:T(8,128)(2,1)S(1)}, bf16[4,16,128]{2,1,0:T(8,128)(2,1)S(1)}, u32[]{:S(2)}, u32[]{:S(2)}) collective-permute-start(bf16[4,16,128]{2,1,0:T(8,128)(2,1)S(1)} %get-tuple-element.21), channel_id=1, source_target_pairs={{0,1},{1,0},{8,9},{9,8},{16,17},{17,16},{24,25},{25,24},{2,3},{3,2... | collective-permute-start | bytes 49160 | tf_op jit(solution)/shard_map/ppermute | solution.py:808
  8.0 1.3 %collective-permute-done.refs_0_.refs_2_ = bf16[4,16,128]{2,1,0:T(8,128)(2,1)S(1)} collective-permute-done((bf16[4,16,128]{2,1,0:T(8,128)(2,1)S(1)}, bf16[4,16,128]{2,1,0:T(8,128)(2,1)S(1)}, u32[]{:S(2)}, u32[]{:S(2)}) %collective-permute-start) | collective-permute-done | bytes 16416 | tf_op jit(solution)/shard_map/ppermute | solution.py:808
  9.4 0.6 %collective-permute-done.1.refs_1_ = bf16[4,16,128]{2,1,0:T(8,128)(2,1)S(1)} collective-permute-done((bf16[4,16,128]{2,1,0:T(8,128)(2,1)S(1)}, bf16[4,16,128]{2,1,0:T(8,128)(2,1)S(1)}, u32[]{:S(2)}, u32[]{:S(2)}) %collective-permute-start.1) | collective-permute-done | bytes 16416 | tf_op jit(solution)/shard_map/ppermute | solution.py:808
  10.0 1.2 %collective-permute-done.2.refs_2_.refs_0_ = bf16[4,16,128]{2,1,0:T(8,128)(2,1)S(1)} collective-permute-done((bf16[4,16,128]{2,1,0:T(8,128)(2,1)S(1)}, bf16[4,16,128]{2,1,0:T(8,128)(2,1)S(1)}, u32[]{:S(2)}, u32[]{:S(2)}) %collective-permute-start.2) | collective-permute-done | bytes 16416 | tf_op jit(solution)/shard_map/ppermute | solution.py:808
  11.2 0.0 collective-permute-done.3.refs_3_.refs_5_
  11.2 0.0 collective-permute-done.4.refs_4_
  11.2 0.0 copy-start
  11.2 0.2 %merge.1 = (bf16[49,16,128]{2,1,0:T(8,128)(2,1)S(1)}, bf16[49,16,128]{2,1,0:T(8,128)(2,1)S(1)}) custom-call(bf16[4,16,128]{2,1,0:T(8,128)(2,1)S(1)} %collective-permute-done.refs_0_.refs_2_, bf16[4,16,128]{2,1,0:T(8,128)(2,1)S(1)} %collective-permute-done.1.refs_1_, bf16[4,16,128]{2,1,0:T(8,128)(2,1)S(1)} %collective-permute-done.2.refs_2_.refs_0_, ...), custom_call_target="tpu_custom_call" | custom-call | tf_op jit(solution)/shard_map/merge/pallas_call | solution.py:865
  11.4 0.0 copy-start.1
  11.4 0.0 copy-start.2
  11.5 1.6 %collective-permute-start.5 = (bf16[49,16,128]{2,1,0:T(8,128)(2,1)S(1)}, bf16[49,16,128]{2,1,0:T(8,128)(2,1)S(1)}, u32[]{:S(2)}, u32[]{:S(2)}) collective-permute-start(bf16[49,16,128]{2,1,0:T(8,128)(2,1)S(1)} %get-tuple-element.26.y1), channel_id=1, source_target_pairs={{0,2},{1,3},{2,0},{3,1},{4,6},{5,7},{6,4},{7,5},{8,10},{9,11},{10,... | collective-permute-start | bytes 602120 | tf_op jit(solution)/shard_map/ppermute | solution.py:808
  13.1 0.0 collective-permute-start.6
  13.1 0.0 copy-done
  13.1 0.0 copy-done.1
  13.1 0.0 copy-done.2
  13.1 3.5 %inner.1 = (f32[512,128]{1,0:T(8,128)S(1)}, f32[6,6,8,128]{3,2,1,0:T(8,128)S(1)}, f32[5,6,8,128]{3,2,1,0:T(8,128)S(1)}, f32[7,4,8,128]{3,2,1,0:T(8,128)S(1)}, f3...) custom-call(bf16[4,16,128]{2,1,0:T(8,128)(2,1)S(1)} %collective-permute-done.2.refs_2_.refs_0_, ...), custom_call_target="tpu_custom_call" | custom-call | flops 20000000 | bytes 12000000 | tf_op jit(solution)/shard_map/inner/pallas_call | solution.py:878
  16.6 0.8 %collective-permute-done.5.r1 = bf16[49,16,128]{2,1,0:T(8,128)(2,1)S(1)} collective-permute-done((bf16[49,16,128]{2,1,0:T(8,128)(2,1)S(1)}, bf16[49,16,128]{2,1,0:T(8,128)(2,1)S(1)}, u32[]{:S(2)}, u32[]{:S(2)}) %collective-permute-start.5) | collective-permute-done | bytes 200736 | tf_op jit(solution)/shard_map/ppermute | solution.py:808
  17.4 0.0 collective-permute-done.6.r2
  17.4 3.1 %finish.1 = (f32[512,128]{1,0:T(8,128)}, f32[4,8,128]{2,1,0:T(8,128)}) custom-call(bf16[49,16,128]{2,1,0:T(8,128)(2,1)S(1)} %get-tuple-element.26.y1, bf16[49,16,128]{2,1,0:T(8,128)(2,1)S(1)} %get-tuple-element.27.y2, bf16[49,16,128]{2,1,0:T(8,128)(2,1)S(1)} %collective-permute-done.5.r1, bf16[49,16,128]{2,1,0:T(8,128)(2,1)S(1)} %collective-permute-done.6.r2, ...), custom_call_target="tpu_custom_call" | custom-call | tf_op jit(solution)/shard_map/finish/pallas_call | solution.py:903
Async XLA Ops:
  2.2 9.0 %collective-permute-start.3 = (bf16[52,16,128]{2,1,0:T(8,128)(2,1)S(1)}, bf16[52,16,128]{2,1,0:T(8,128)(2,1)S(1)}, u32[]{:S(2)}, u32[]{:S(2)}) collective-permute-start(bf16[52,16,128]{2,1,0:T(8,128)(2,1)S(1)} %get-tuple-element.22), channel_id=1, source_target_pairs={{0,1},{1,0},{8,16},{9,17},{16,8},{17,9},{24,25},{25,24},{2,3},{3,2... | collective-permute-start | bytes 638984 | tf_op jit(solution)/shard_map/ppermute | solution.py:808
  5.2 6.0 %collective-permute-start.4 = (bf16[52,16,128]{2,1,0:T(8,128)(2,1)S(1)}, bf16[52,16,128]{2,1,0:T(8,128)(2,1)S(1)}, u32[]{:S(2)}, u32[]{:S(2)}) collective-permute-start(bf16[52,16,128]{2,1,0:T(8,128)(2,1)S(1)} %get-tuple-element.23), channel_id=1, source_target_pairs={{0,8},{1,9},{8,0},{9,1},{16,24},{17,25},{24,16},{25,17},{2,10},{3,... | collective-permute-start | bytes 638984 | tf_op jit(solution)/shard_map/ppermute | solution.py:808
  5.3 4.0 %collective-permute-start = (bf16[4,16,128]{2,1,0:T(8,128)(2,1)S(1)}, bf16[4,16,128]{2,1,0:T(8,128)(2,1)S(1)}, u32[]{:S(2)}, u32[]{:S(2)}) collective-permute-start(bf16[4,16,128]{2,1,0:T(8,128)(2,1)S(1)} %get-tuple-element.19), channel_id=1, source_target_pairs={{0,1},{1,0},{8,17},{9,16},{16,9},{17,8},{24,25},{25,24},{2,3},{3,2... | collective-permute-start | bytes 49160 | tf_op jit(solution)/shard_map/ppermute | solution.py:808
  6.8 3.2 %collective-permute-start.1 = (bf16[4,16,128]{2,1,0:T(8,128)(2,1)S(1)}, bf16[4,16,128]{2,1,0:T(8,128)(2,1)S(1)}, u32[]{:S(2)}, u32[]{:S(2)}) collective-permute-start(bf16[4,16,128]{2,1,0:T(8,128)(2,1)S(1)} %get-tuple-element.20), channel_id=1, source_target_pairs={{0,9},{1,8},{8,1},{9,0},{16,25},{17,24},{24,17},{25,16},{2,11},{3,... | collective-permute-start | bytes 49160 | tf_op jit(solution)/shard_map/ppermute | solution.py:808
  7.4 3.7 %collective-permute-start.2 = (bf16[4,16,128]{2,1,0:T(8,128)(2,1)S(1)}, bf16[4,16,128]{2,1,0:T(8,128)(2,1)S(1)}, u32[]{:S(2)}, u32[]{:S(2)}) collective-permute-start(bf16[4,16,128]{2,1,0:T(8,128)(2,1)S(1)} %get-tuple-element.21), channel_id=1, source_target_pairs={{0,1},{1,0},{8,9},{9,8},{16,17},{17,16},{24,25},{25,24},{2,3},{3,2... | collective-permute-start | bytes 49160 | tf_op jit(solution)/shard_map/ppermute | solution.py:808
  11.2 1.9 %copy-start = (f32[6,4,8,128]{3,2,1,0:T(8,128)S(1)}, f32[6,4,8,128]{3,2,1,0:T(8,128)}, u32[]{:S(2)}) copy-start(f32[6,4,8,128]{3,2,1,0:T(8,128)} %refs_6_.1) | copy-start | bytes 294916
  11.4 1.7 %copy-start.1 = (f32[16]{0:T(128)S(1)}, f32[16]{0:T(128)}, u32[]{:S(2)}) copy-start(f32[16]{0:T(128)} %refs_7_.1) | copy-start | bytes 196
  11.4 1.7 %copy-start.2 = (f32[16]{0:T(128)S(1)}, f32[16]{0:T(128)}, u32[]{:S(2)}) copy-start(f32[16]{0:T(128)} %refs_8_.1) | copy-start | bytes 196
  11.5 6.0 %collective-permute-start.5 = (bf16[49,16,128]{2,1,0:T(8,128)(2,1)S(1)}, bf16[49,16,128]{2,1,0:T(8,128)(2,1)S(1)}, u32[]{:S(2)}, u32[]{:S(2)}) collective-permute-start(bf16[49,16,128]{2,1,0:T(8,128)(2,1)S(1)} %get-tuple-element.26.y1), channel_id=1, source_target_pairs={{0,2},{1,3},{2,0},{3,1},{4,6},{5,7},{6,4},{7,5},{8,10},{9,11},{10,... | collective-permute-start | bytes 602120 | tf_op jit(solution)/shard_map/ppermute | solution.py:808
  13.1 4.3 %collective-permute-start.6 = (bf16[49,16,128]{2,1,0:T(8,128)(2,1)S(1)}, bf16[49,16,128]{2,1,0:T(8,128)(2,1)S(1)}, u32[]{:S(2)}, u32[]{:S(2)}) collective-permute-start(bf16[49,16,128]{2,1,0:T(8,128)(2,1)S(1)} %get-tuple-element.27.y2), channel_id=1, source_target_pairs={{0,8},{2,4},{4,2},{6,14},{8,0},{10,12},{12,10},{14,6},{16,24},{18,... | collective-permute-start | bytes 602120 | tf_op jit(solution)/shard_map/ppermute | solution.py:808

commit v5 on v4

--- a/solution.py
+++ b/solution.py
@@ -52,13 +52,13 @@
     return jnp.concatenate([first[:HALF].astype(F32), second[:HALF].astype(F32)], 0).astype(BF16)
 
 
-def pack_kernel(dims, zcount, modes_in, material_in, fixed_in, disp_in, tiles, x1, x2, edge, ex1, ex2, tables, modes, material, fixed, disp, raw, chosen, sems):
+def pack_kernel(dims, zcount, modes_in, material_in, fixed_in, disp_in, eig_in, weight_in, tiles, x1, x2, edge, ex1, ex2, tables, scale, modes, material, fixed, disp, eig, weight, raw, chosen, sems):
     nx, ny = dims
     copies = [
         pltpu.make_async_copy(src, dst, sems.at[i])
         for i, (src, dst) in enumerate(
             [(modes_in.at[c], modes.at[c]) for c in range(3)]
-            + [(material_in, material), (fixed_in, fixed), (disp_in, disp)]
+            + [(material_in, material), (fixed_in, fixed), (disp_in, disp), (eig_in, eig), (weight_in, weight)]
         )
     ]
     for copy in copies:
@@ -103,6 +103,18 @@
         store(3, 5 + c, value - first)
     for m in range(HALF, MODES):
         store(3, m, jnp.zeros((part, LANES), F32))
+
+    mode_row = row_iota((MODES, LANES))
+    mode_lane = lax.rem(lane_iota(), MODES)
+    eig_rows = jnp.zeros((MODES, LANES), F32)
+    coef_rows = jnp.zeros((MODES, LANES), F32)
+    coef_lanes = jnp.zeros((MODES, LANES), F32)
+    for m in range(MODES):
+        product = eig[m] * weight[m]
+        eig_rows = jnp.where(mode_row == m, eig[m], eig_rows)
+        coef_rows = jnp.where(mode_row == m, product, coef_rows)
+        coef_lanes = jnp.where(mode_lane == m, product, coef_lanes)
+    scale[0], scale[1], scale[2] = eig_rows, coef_rows, coef_lanes
     spread(3)
 
     block = jnp.concatenate([tiles[:, :, y].reshape(GROUPS * nx * MODES, LANES) for y in range(ny)], 1)
@@ -185,69 +197,6 @@
         valid = jnp.where(fits, jnp.where(low, lower, upper), 0.0)
         for k, kind in enumerate(by_kind):
             store(k * zcount + z, (valid * kind).astype(BF16))
-
-
-def merge_kernel(dims, zcount, *refs):
-    nx, ny = dims
-    zblocks = refs[: 3 * zcount]
-    r2, r1, tiles, tables, y1, y2, rows_aux = refs[3 * zcount :]
-    xe, xlo, xup = place("gx")
-    ye, _, _ = place("gy")
-    width = nx + 3
-    side = jnp.concatenate([ref[...].reshape(GROUPS * MODES, LANES) for ref in zblocks], 1)
-    ends = jnp.dot(side, tables[...], preferred_element_type=F32)
-    rows = [[jnp.where(up, ny - 1, s) for s in range(2)] for up in (ye, jnp.logical_not(ye))]
-    outs = (y1, y2)
-    blank = jnp.zeros((MODES, LANES), BF16)
-    blank_half = jnp.zeros((HALF, LANES), F32)
-
-    def half_of(ref, row):
-        pairs = ref[6 * ny + row // 2].astype(F32)
-        odd = lax.rem(row, 2).astype(F32)
-        return pairs[:HALF] * (1.0 - odd) + pairs[HALF:] * odd
-
-    def lower(ref):
-        for k in range(2):
-            for c in range(3):
-                for s in range(2):
-                    outs[k][c * width * 2 + s] = ref[c * 2 * ny + rows[k][s]]
-            rows_aux[k, 0] = half_of(ref, rows[k][0])
-
-    def upper(ref):
-        for k in range(2):
-            for c in range(3):
-                for t in range(2):
-                    for s in range(2):
-                        outs[k][(c * width + nx + 1 + t) * 2 + s] = ref[(c * 2 + t) * ny + rows[k][s]]
-            rows_aux[k, nx + 1] = half_of(ref, rows[k][0])
-
-    def no_lower():
-        for k in range(2):
-            for c in range(3):
-                for s in range(2):
-                    outs[k][c * width * 2 + s] = blank
-            rows_aux[k, 0] = blank_half
-
-    def no_upper():
-        for k in range(2):
-            for c in range(3):
-                for i in range(4):
-                    outs[k][(c * width + nx + 1) * 2 + i] = blank
-            rows_aux[k, nx + 1] = blank_half
-
-    pick(xe, xlo, xup, r1, r2, lower, upper, no_lower, no_upper)
-    base = 6 * width
-    for k, out in enumerate(outs):
-        for c in range(3):
-            for s in range(2):
-                for x in range(nx):
-                    out[(c * width + x + 1) * 2 + s] = tiles[c, x, rows[k][s]]
-        for x in range(nx):
-            rows_aux[k, x + 1] = tiles[3, x, rows[k][0]][:HALF].astype(F32)
-        for x in range(0, nx + 2, 2):
-            out[base + x // 2] = pair_up(rows_aux[k, x], rows_aux[k, x + 1])
-        block = ends[:, k * LANES : (k + 1) * LANES].reshape(GROUPS, MODES, LANES)
-        out[base + (nx + 2) // 2 :] = block.astype(BF16)
 
 
 def cross_xy(a, b):
@@ -382,6 +331,112 @@
     return fields[6] * energy + eig_rows * total
 
 
+W_ROWS = 40
+
+
+def merge_kernel(dims, zcount, *refs):
+    nx, ny = dims
+    zblocks = refs[: 3 * zcount]
+    r2, r1, tiles, tables, scale, y1, y2, rows, rows_aux, ends, sz, dz, part = refs[3 * zcount :]
+    xe, xlo, xup = place("gx")
+    ye, _, _ = place("gy")
+    width = nx + 3
+    lane = lane_iota()
+    outs = (y1, y2)
+    blank = jnp.zeros((MODES, LANES), BF16)
+    blank_half = jnp.zeros((HALF, LANES), F32)
+    kinds = (0, 1, ny - 1)
+
+    def half_of(ref, row):
+        start = row % 2 * HALF
+        return ref[6 * ny + row // 2].astype(F32)[start : start + HALF]
+
+    def lower(ref):
+        for i, row in enumerate(kinds):
+            for c in range(3):
+                rows[i, c * width] = ref[c * 2 * ny + row]
+            rows_aux[i, 0] = half_of(ref, row)
+
+    def upper(ref):
+        for i, row in enumerate(kinds):
+            for c in range(3):
+                for t in range(2):
+                    rows[i, c * width + nx + 1 + t] = ref[(c * 2 + t) * ny + row]
+            rows_aux[i, nx + 1] = half_of(ref, row)
+
+    def no_lower():
+        for i in range(3):
+            for c in range(3):
+                rows[i, c * width] = blank
+            rows_aux[i, 0] = blank_half
+
+    def no_upper():
+        for i in range(3):
+            for c in range(3):
+                for t in range(2):
+                    rows[i, c * width + nx + 1 + t] = blank
+            rows_aux[i, nx + 1] = blank_half
+
+    pick(xe, xlo, xup, r1, r2, lower, upper, no_lower, no_upper)
+    for i, row in enumerate(kinds):
+        for x in range(nx):
+            for c in range(3):
+                rows[i, c * width + x + 1] = tiles[c, x, row]
+            rows_aux[i, x + 1] = tiles[3, x, row][:HALF].astype(F32)
+
+    side = jnp.concatenate([ref[...].reshape(GROUPS * MODES, LANES) for ref in zblocks], 1)
+    found = jnp.dot(side, tables[...], preferred_element_type=F32)
+    for k in range(2):
+        ends[k] = found[:, k * LANES : (k + 1) * LANES].reshape(GROUPS, MODES, LANES)
+    down = jnp.where(ye, 1, 0)
+
+    count = 3 * width * MODES
+    table = z_table()
+    beyond = [ends[down, c] for c in range(3)]
+    for i in range(2):
+        both = jnp.dot(rows[i].reshape(count, LANES), table, preferred_element_type=F32)
+        both = both.reshape(3, width, MODES, 2 * LANES)
+        for c in range(3):
+            for x in range(width):
+                more = roll(beyond[c], LANES - 1 - (16 * x + 3 * i + 1))
+                more = jnp.where(lane == LANES - 1, more, 0.0)
+                sz[i, c, x] = both[c, x, :, :LANES] + more
+                dz[i, c, x] = both[c, x, :, LANES:] + more
+    for c in range(3):
+        value = beyond[c]
+        for x in range(width):
+            value = jnp.where(lane == 16 * x + 6, roll(rows[1, c * width + x].astype(F32), 16 * x + 6), value)
+        ends[down, c] = value
+
+    values = []
+    for x in range(nx + 2):
+        for h in range(2):
+            coef = scale[1, 8 * h : 8 * h + 8]
+            now, after = x_parts(sz, dz, 0, x, h), x_parts(sz, dz, 1, x, h)
+            quad, _ = forms([combos(now[c], after[c]) for c in range(3)], False)
+            for i in range(6):
+                if h == 0:
+                    part[x, i] = coef * quad[i]
+                else:
+                    part[x, i] += coef * quad[i]
+        values += [part[x, i] for i in range(6)]
+    values += [jnp.zeros((8, LANES), F32)] * (W_ROWS - len(values))
+    summed = jnp.concatenate([fold_rows(values[i : i + 8]) for i in range(0, W_ROWS, 8)], 0)
+    first = summed.astype(BF16).astype(F32)
+    sent = jnp.concatenate([first, summed - first], 0).astype(BF16).reshape(2 * W_ROWS // MODES, MODES, LANES)
+
+    base = 3 * width
+    for k, out in enumerate(outs):
+        kind = jnp.where(ye, 2 if k == 0 else 0, 0 if k == 0 else 2)
+        for i in range(base):
+            out[i] = rows[kind, i]
+        for x in range(0, nx + 2, 2):
+            out[base + x // 2] = pair_up(rows_aux[kind, x], rows_aux[kind, x + 1])
+        at = base + (nx + 2) // 2
+        out[at : at + GROUPS] = ends[k].astype(BF16)
+        out[at + GROUPS :] = sent
+
+
 FIELDS = 5
 
 
@@ -389,8 +444,8 @@
     rz = refs[:zcount]
     rz1 = refs[zcount : 2 * zcount]
     rz2 = refs[2 * zcount : 3 * zcount]
-    tiles, r1, r2, stress, eig, weight = refs[3 * zcount : 3 * zcount + 6]
-    sens, wmain, field, cell, zr, scale, rim, full, sz, dz, part, aux, table = refs[3 * zcount + 6 :]
+    tiles, r1, r2, stress, scale = refs[3 * zcount : 3 * zcount + 5]
+    sens, wmain, field, cell, zr, rim, full, sz, dz, part, aux, table = refs[3 * zcount + 5 :]
     nx, ny = dims
     width = nx + 3
     tall = ny + 3
@@ -487,18 +542,6 @@
         field[1, x] = channel(1)
         for c in range(3):
             field[2 + c, x] = channel(2 + c) + channel(5 + c)
-
-    mode_row = row_iota((MODES, LANES))
-    mode_lane = lax.rem(lane, MODES)
-    eig_rows = jnp.zeros((MODES, LANES), F32)
-    coef_rows = jnp.zeros((MODES, LANES), F32)
-    coef_lanes = jnp.zeros((MODES, LANES), F32)
-    for m in range(MODES):
-        product = eig[m] * weight[m]
-        eig_rows = jnp.where(mode_row == m, eig[m], eig_rows)
-        coef_rows = jnp.where(mode_row == m, product, coef_rows)
-        coef_lanes = jnp.where(mode_lane == m, product, coef_lanes)
-    scale[0], scale[1], scale[2] = eig_rows, coef_rows, coef_lanes
 
     for x in range(nx):
         density = field[0, x + 1] * (1.0 / LEVELS)
@@ -537,7 +580,7 @@
         sweep(x, False)
 
 
-def final_kernel(dims, y1, y2, r1, r2, wmain, field_in, cell, zr, scale, sens_in, sens, adjoint, rows, rows_aux, rows_end, sz, dz, sum_z, w, zt, field, shear, load, stage, whole, table, sem):
+def final_kernel(dims, y1, y2, r1, r2, wmain, field_in, cell, zr, scale, sens_in, sens, adjoint, rows, rows_aux, rows_end, far_w, sz, dz, sum_z, w, zt, field, shear, load, stage, whole, table, sem):
     nx, ny = dims
     width = nx + 3
     tall = ny + 3
@@ -546,11 +589,11 @@
     table[0:LANES, :] = z_table()
     whole[...] = sens_in[...]
 
-    def copy_rows(to, ref, slot):
+    def copy_rows(to, ref):
         for i in range(3 * width):
-            rows[to, i] = ref[2 * i + slot]
-
-    aux_base = 6 * width
+            rows[to, i] = ref[i]
+
+    aux_base = 3 * width
     end_base = aux_base + (nx + 2) // 2
 
     def copy_aux(to, ref):
@@ -560,13 +603,14 @@
             rows_end[to, c] = ref[end_base + c].astype(F32)
 
     def lower(ref):
-        copy_rows(0, ref, 0)
+        copy_rows(0, ref)
         copy_aux(0, ref)
 
     def upper(ref):
-        copy_rows(3, ref, 0)
-        copy_rows(4, ref, 1)
+        copy_rows(3, ref)
         copy_aux(1, ref)
+        sent = ref[end_base + GROUPS :].astype(F32).reshape(2 * W_ROWS, LANES)
+        far_w[...] = sent[:W_ROWS] + sent[W_ROWS:]
 
     def no_lower():
         rows[0] = jnp.zeros_like(rows[0])
@@ -574,27 +618,28 @@
         rows_end[0] = jnp.zeros_like(rows_end[0])
 
     def no_upper():
-        rows[3:5] = jnp.zeros_like(rows[3:5])
+        rows[3] = jnp.zeros_like(rows[3])
         rows_aux[1] = jnp.zeros_like(rows_aux[1])
         rows_end[1] = jnp.zeros_like(rows_end[1])
+        far_w[...] = jnp.zeros_like(far_w)
 
     pick(ye, ylo, yup, r1, r2, lower, upper, no_lower, no_upper)
 
     @pl.when(ye)
     def _():
-        copy_rows(2, y1, 0)
-        copy_rows(1, y2, 0)
+        copy_rows(2, y1)
+        copy_rows(1, y2)
 
     @pl.when(jnp.logical_not(ye))
     def _():
-        copy_rows(2, y2, 0)
-        copy_rows(1, y1, 0)
+        copy_rows(2, y2)
+        copy_rows(1, y1)
 
     far = 3 * (ny + 1)
     count = 3 * width * MODES
-    at = (0, 1, ny, ny + 1, ny + 2)
+    at = (0, 1, ny, ny + 1)
     column = None
-    for i in (0, 3, 4):
+    for i in (0, 3):
         term = jnp.dot(rows[i].reshape(count, LANES), first_column(3 * tall + at[i]), preferred_element_type=F32)
         column = term if column is None else column + term
     column = column.reshape(3, width, MODES, LANES)
@@ -606,24 +651,27 @@
             ends = jnp.where((lane >= far) & (lane < far + 6), roll(rows_end[1, c], far - 16 * x), ends)
             if c < 3:
                 ends = ends + column[c, x]
+                corner = 3 * tall + ny + 2
+                ends = jnp.where(lane == corner, roll(rows_end[1, c], corner - 6 - 16 * x), ends)
             layers.append(ends)
         layers.append(jnp.zeros((LANES - width * MODES, LANES), F32))
         stacked = jnp.concatenate(layers, 0)
         full_rim.append(stacked[: width * MODES])
         zt[c] = stacked.T
     ends = jnp.concatenate(full_rim[:3], 0).astype(BF16)
-    for i in range(5):
+    for i in range(4):
         rows_along_z(rows[i].reshape(count, LANES), ends, 3 * at[i] + 1, table, sz, dz, i)
 
     w[:, :, 0:8, 0:LANES] = wmain[...]
+    for x in range(nx + 2):
+        for k in range(6):
+            w[k, x, ny + 1 : ny + 2, 0:LANES] = far_w[6 * x + k : 6 * x + k + 1, :]
 
     def sweep(x, inside):
         for h in range(2):
             coef = scale[1, 8 * h : 8 * h + 8]
-            now = None
-            for i, (first, own) in enumerate(((0, False), (2, inside), (3, False))):
-                if i < 2:
-                    now = x_parts(sz, dz, first, x, h)
+            for i, (first, own) in enumerate(((0, False), (2, inside))):
+                now = x_parts(sz, dz, first, x, h)
                 after = x_parts(sz, dz, first + 1, x, h)
                 quad, energy = forms([combos(now[c], after[c]) for c in range(3)], own)
                 if own:
@@ -636,15 +684,14 @@
                         sum_z[k, i] = coef * quad[k]
                     else:
                         sum_z[k, i] += coef * quad[k]
-                now = after
-        pairs = [(k, i) for k in range(6) for i in range(3)]
+        pairs = [(k, i) for k in range(6) for i in range(2)]
         for start in range(0, len(pairs), 8):
             some = pairs[start : start + 8]
             values = [sum_z[k, i] for k, i in some]
             values += [jnp.zeros((8, LANES), F32)] * (8 - len(some))
             folded = fold_rows(values)
             for j, (k, i) in enumerate(some):
-                row = (0, ny, ny + 1)[i]
+                row = (0, ny)[i]
                 w[k, x, row : row + 1, 0:LANES] = folded[j : j + 1]
 
     for x in range(1, nx + 1):
@@ -829,7 +876,7 @@
     layer = 6 * ny + ny // 2
     zkinds = (1,) if lax.axis_size("gz") == 2 else (1, 2)
     zcount = len(zkinds)
-    tiles, x1, x2, edge, ex1, ex2, tables = pl.pallas_call(
+    tiles, x1, x2, edge, ex1, ex2, tables, scale = pl.pallas_call(
         functools.partial(pack_kernel, dims, zcount),
         out_shape=(
             sds((GROUPS, nx, ny) + tile, BF16),
@@ -839,21 +886,29 @@
             sds((GROUPS,) + tile, BF16),
             sds((GROUPS,) + tile, BF16),
             sds((3 * zcount * LANES, 2 * LANES), BF16),
+            sds((3,) + tile, F32),
         ),
-        in_specs=anywhere(4),
-        out_specs=tuple(vmem(7)),
+        in_specs=anywhere(6),
+        out_specs=tuple(vmem(8)),
         scratch_shapes=[
             pltpu.VMEM(mode_shapes.shape, BF16),
             pltpu.VMEM(material.shape, material.dtype),
             pltpu.VMEM(fixed_nodes.shape, fixed_nodes.dtype),
             pltpu.VMEM(displacement.shape, F32),
+            pltpu.SMEM(eigenvalues.shape, F32),
+            pltpu.SMEM(mode_weight.shape, F32),
             pltpu.VMEM((GROUPS * MODES * PITCH, LANES), F32),
             pltpu.VMEM((ny * LANES, LANES), BF16),
-            pltpu.SemaphoreType.DMA((6,)),
+            pltpu.SemaphoreType.DMA((8,)),
         ],
         compiler_params=pltpu.CompilerParams(vmem_limit_bytes=8 << 20),
         name="pack",
-    )(*(pltpu.with_memory_space_constraint(a, pltpu.HBM) for a in (mode_shapes, material, fixed_nodes, displacement)))
+    )(
+        *(
+            pltpu.with_memory_space_constraint(a, pltpu.HBM)
+            for a in (mode_shapes, material, fixed_nodes, displacement, eigenvalues, mode_weight)
+        )
+    )
 
     xz = ("gx", "gz")
     r2 = swap(x2, xz, (2, 0), True)
@@ -861,21 +916,28 @@
     rz = [swap(edge, xz, (0, k), True) for k in zkinds]
     rz1 = [swap(ex1, xz, (1, k), True) for k in zkinds]
     rz2 = [swap(ex2, xz, (2, k), True) for k in zkinds]
-    count = 6 * width + (nx + 2) // 2 + GROUPS
+    count = 3 * width + (nx + 2) // 2 + GROUPS + 2 * W_ROWS // MODES
     y1, y2 = pl.pallas_call(
         functools.partial(merge_kernel, dims, zcount),
         out_shape=(sds((count,) + tile, BF16), sds((count,) + tile, BF16)),
-        in_specs=vmem(4 + 3 * zcount),
+        in_specs=vmem(5 + 3 * zcount),
         out_specs=tuple(vmem(2)),
-        scratch_shapes=[pltpu.VMEM((2, nx + 2, HALF, LANES), F32)],
+        scratch_shapes=[
+            pltpu.VMEM((3, 3 * width) + tile, BF16),
+            pltpu.VMEM((3, nx + 2, HALF, LANES), F32),
+            pltpu.VMEM((2, GROUPS) + tile, F32),
+            pltpu.VMEM((2, 3, width) + tile, F32),
+            pltpu.VMEM((2, 3, width) + tile, F32),
+            pltpu.VMEM((nx + 2, 6, 8, LANES), F32),
+        ],
         compiler_params=pltpu.CompilerParams(vmem_limit_bytes=8 << 20),
         name="merge",
-    )(*rz2, *rz1, *rz, r2, r1, tiles, tables)
+    )(*rz2, *rz1, *rz, r2, r1, tiles, tables, scale)
 
     yz = ("gy", "gz")
     ry1 = swap(y1, yz, (1, 0), True)
     ry2 = swap(y2, ("gx", "gy"), (0, 2), True)
-    sens, wmain, field, cell, zr, scale = pl.pallas_call(
+    sens, wmain, field, cell, zr = pl.pallas_call(
         functools.partial(inner_kernel, dims, zcount),
         out_shape=(
             sds((MODES * nx * ny, LANES), F32),
@@ -883,10 +945,9 @@
             sds((FIELDS, nx + 2, ny, LANES), F32),
             sds((7, nx, ny, LANES), F32),
             sds((GROUPS, width) + tile, F32),
-            sds((3,) + tile, F32),
         ),
-        in_specs=vmem(4 + 3 * zcount) + [pl.BlockSpec(memory_space=pltpu.SMEM)] * 2,
-        out_specs=tuple(vmem(6)),
+        in_specs=vmem(5 + 3 * zcount),
+        out_specs=tuple(vmem(5)),
         scratch_shapes=[
             pltpu.VMEM((GROUPS, width) + tile, F32),
             pltpu.VMEM((3, width, ny) + tile, BF16),
@@ -899,19 +960,20 @@
         compiler_params=pltpu.CompilerParams(vmem_limit_bytes=24 << 20),
         cost_estimate=pl.CostEstimate(flops=20_000_000, bytes_accessed=12_000_000, transcendentals=0),
         name="inner",
-    )(*rz, *rz1, *rz2, tiles, r1, r2, stress_field, eigenvalues, mode_weight)
+    )(*rz, *rz1, *rz2, tiles, r1, r2, stress_field, scale)
     sens, adjoint = pl.pallas_call(
         functools.partial(final_kernel, dims),
         out_shape=(sds((MODES * nx * ny, LANES), F32), sds((nx, ny, LANES), F32)),
         in_specs=vmem(10),
         out_specs=(pl.BlockSpec(memory_space=pl.ANY), pl.BlockSpec(memory_space=pltpu.VMEM)),
         scratch_shapes=[
-            pltpu.VMEM((5, 3 * width) + tile, BF16),
+            pltpu.VMEM((4, 3 * width) + tile, BF16),
             pltpu.VMEM((2, (nx + 2) // 2) + tile, F32),
             pltpu.VMEM((2, GROUPS) + tile, F32),
-            pltpu.VMEM((5, 3, width) + tile, F32),
-            pltpu.VMEM((5, 3, width) + tile, F32),
-            pltpu.VMEM((6, 3, 8, LANES), F32),
+            pltpu.VMEM((W_ROWS, LANES), F32),
+            pltpu.VMEM((4, 3, width) + tile, F32),
+            pltpu.VMEM((4, 3, width) + tile, F32),
+            pltpu.VMEM((6, 2, 8, LANES), F32),
             pltpu.VMEM((6, nx + 2, 16, 2 * LANES), F32),
             pltpu.VMEM((GROUPS, LANES, LANES), F32),
             pltpu.VMEM((FIELDS, nx + 2, 24, LANES), F32),

time: 20.9 us -> 20.1 us (0.962)
  Pallas kernels: 8.36 us -> 7.98 us
  waiting for transfers between devices: 3.98 us -> 3.64 us
    pallas_call x1, Pallas kernels: 3.47 us -> 2.92 us  [body(): pl.pallas_call(functools.partial(inner_kernel, dims, zcount), out_shape=(...]
    pallas_call x1, Pallas kernels: 0.24 us -> 0.64 us  [body(): pl.pallas_call(functools.partial(merge_kernel, dims, zcount), out_shape=(...]
    ppermute x7, waiting for transfers between devices: 3.98 us -> 3.64 us  [swap(): return lax.ppermute(block, axes, route)]
    pallas_call x1, Pallas kernels: 3.11 us -> 2.84 us  [body(): pl.pallas_call(functools.partial(final_kernel, dims), out_shape=(sds((MOD...]
  transfers between devices with their start and end apart: 7 -> 7, of which waited for: 4 -> 4; matrix products, arithmetic and copies ran while one was open for 0% -> 0% of each run, Pallas kernels for 17% -> 15%
where the time goes in v5:
time: 20.1 us; the launch traced here: 19.8 us
  Pallas kernels  7.98 us (40%)
  starting transfers between devices  7.51 us (37%)
  waiting for transfers between devices  3.64 us (18%)
  between operations  0.66 us (3%)
    ppermute x7, starting transfers between devices, swap(): return lax.ppermute(block, axes, route)  7.51 us
    ppermute x7, waiting for transfers between devices, swap(): return lax.ppermute(block, axes, route)  3.64 us
    pallas_call x1, Pallas kernels, body(): pl.pallas_call(functools.partial(inner_kernel, dims, zcount), out_shape=(...  2.92 us
    pallas_call x1, Pallas kernels, body(): pl.pallas_call(functools.partial(final_kernel, dims), out_shape=(sds((MOD...  2.84 us
    pallas_call x1, Pallas kernels, body(): pl.pallas_call(functools.partial(pack_kernel, dims, zcount), out_shape=(s...  1.58 us
    pallas_call x1, Pallas kernels, body(): pl.pallas_call(functools.partial(merge_kernel, dims, zcount), out_shape=(...  0.64 us
  transfers between devices with their start and end apart: 7, of which 4 were waited for; matrix products, arithmetic and copies ran while one was open for 0% of the time, Pallas kernels for 15%

profile of v5, /device:TPU:0, one launch (start us, length us, event | category | flops | bytes accessed | tf_op | source)
XLA Modules:
  0.0 19.8 jit_solution(5847314602806744873)
XLA Ops:
  0.6 1.6 %pack.1 = (bf16[4,4,8,16,128]{4,3,2,1,0:T(8,128)(2,1)S(1)}, bf16[52,16,128]{2,1,0:T(8,128)(2,1)S(1)}, bf16[52,16,128]{2,1,0:T(8,128)(2,1)S(1)}, bf16[4,16,128]{2...) custom-call(bf16[3,16,4,8,128]{4,3,2,1,0:T(8,128)(2,1)} %modes_in.1,, ...), custom_call_target="tpu_custom_call" | custom-call | tf_op jit(solution)/shard_map/pack/pallas_call | solution.py:879
  2.2 3.0 %collective-permute-start.3 = (bf16[52,16,128]{2,1,0:T(8,128)(2,1)S(1)}, bf16[52,16,128]{2,1,0:T(8,128)(2,1)S(1)}, u32[]{:S(2)}, u32[]{:S(2)}) collective-permute-start(bf16[52,16,128]{2,1,0:T(8,128)(2,1)S(1)} %get-tuple-element.22), channel_id=1, source_target_pairs={{0,1},{1,0},{8,16},{9,17},{16,8},{17,9},{24,25},{25,24},{2,3},{3,2... | collective-permute-start | bytes 638984 | tf_op jit(solution)/shard_map/ppermute | solution.py:855
  5.2 0.1 collective-permute-start.4
  5.4 1.5 %collective-permute-start = (bf16[4,16,128]{2,1,0:T(8,128)(2,1)S(1)}, bf16[4,16,128]{2,1,0:T(8,128)(2,1)S(1)}, u32[]{:S(2)}, u32[]{:S(2)}) collective-permute-start(bf16[4,16,128]{2,1,0:T(8,128)(2,1)S(1)} %get-tuple-element.19), channel_id=1, source_target_pairs={{0,1},{1,0},{8,17},{9,16},{16,9},{17,8},{24,25},{25,24},{2,3},{3,2... | collective-permute-start | bytes 49160 | tf_op jit(solution)/shard_map/ppermute | solution.py:855
  6.9 0.6 %collective-permute-start.1 = (bf16[4,16,128]{2,1,0:T(8,128)(2,1)S(1)}, bf16[4,16,128]{2,1,0:T(8,128)(2,1)S(1)}, u32[]{:S(2)}, u32[]{:S(2)}) collective-permute-start(bf16[4,16,128]{2,1,0:T(8,128)(2,1)S(1)} %get-tuple-element.20), channel_id=1, source_target_pairs={{0,9},{1,8},{8,1},{9,0},{16,25},{17,24},{24,17},{25,16},{2,11},{3,... | collective-permute-start | bytes 49160 | tf_op jit(solution)/shard_map/ppermute | solution.py:855
  7.5 0.6 %collective-permute-start.2 = (bf16[4,16,128]{2,1,0:T(8,128)(2,1)S(1)}, bf16[4,16,128]{2,1,0:T(8,128)(2,1)S(1)}, u32[]{:S(2)}, u32[]{:S(2)}) collective-permute-start(bf16[4,16,128]{2,1,0:T(8,128)(2,1)S(1)} %get-tuple-element.21), channel_id=1, source_target_pairs={{0,1},{1,0},{8,9},{9,8},{16,17},{17,16},{24,25},{25,24},{2,3},{3,2... | collective-permute-start | bytes 49160 | tf_op jit(solution)/shard_map/ppermute | solution.py:855
  8.1 1.3 %collective-permute-done.refs_0_.refs_2_ = bf16[4,16,128]{2,1,0:T(8,128)(2,1)S(1)} collective-permute-done((bf16[4,16,128]{2,1,0:T(8,128)(2,1)S(1)}, bf16[4,16,128]{2,1,0:T(8,128)(2,1)S(1)}, u32[]{:S(2)}, u32[]{:S(2)}) %collective-permute-start) | collective-permute-done | bytes 16416 | tf_op jit(solution)/shard_map/ppermute | solution.py:855
  9.4 0.6 %collective-permute-done.1.refs_1_ = bf16[4,16,128]{2,1,0:T(8,128)(2,1)S(1)} collective-permute-done((bf16[4,16,128]{2,1,0:T(8,128)(2,1)S(1)}, bf16[4,16,128]{2,1,0:T(8,128)(2,1)S(1)}, u32[]{:S(2)}, u32[]{:S(2)}) %collective-permute-start.1) | collective-permute-done | bytes 16416 | tf_op jit(solution)/shard_map/ppermute | solution.py:855
  10.0 1.2 %collective-permute-done.2.refs_2_.refs_0_ = bf16[4,16,128]{2,1,0:T(8,128)(2,1)S(1)} collective-permute-done((bf16[4,16,128]{2,1,0:T(8,128)(2,1)S(1)}, bf16[4,16,128]{2,1,0:T(8,128)(2,1)S(1)}, u32[]{:S(2)}, u32[]{:S(2)}) %collective-permute-start.2) | collective-permute-done | bytes 16416 | tf_op jit(solution)/shard_map/ppermute | solution.py:855
  11.2 0.0 collective-permute-done.3.refs_3_.refs_5_
  11.2 0.0 collective-permute-done.4.refs_4_
  11.2 0.0 copy-start
  11.2 0.6 %merge.1 = (bf16[33,16,128]{2,1,0:T(8,128)(2,1)S(1)}, bf16[33,16,128]{2,1,0:T(8,128)(2,1)S(1)}) custom-call(bf16[4,16,128]{2,1,0:T(8,128)(2,1)S(1)} %collective-permute-done.refs_0_.refs_2_, bf16[4,16,128]{2,1,0:T(8,128)(2,1)S(1)} %collective-permute-done.1.refs_1_, bf16[4,16,128]{2,1,0:T(8,128)(2,1)S(1)} %collective-permute-done.2.refs_2_.refs_0_, ...), custom_call_target="tpu_custom_call" | custom-call | tf_op jit(solution)/shard_map/merge/pallas_call | solution.py:920
  11.9 1.6 %collective-permute-start.5 = (bf16[33,16,128]{2,1,0:T(8,128)(2,1)S(1)}, bf16[33,16,128]{2,1,0:T(8,128)(2,1)S(1)}, u32[]{:S(2)}, u32[]{:S(2)}) collective-permute-start(bf16[33,16,128]{2,1,0:T(8,128)(2,1)S(1)} %get-tuple-element.27.y1), channel_id=1, source_target_pairs={{0,2},{1,3},{2,0},{3,1},{4,6},{5,7},{6,4},{7,5},{8,10},{9,11},{10,... | collective-permute-start | bytes 405512 | tf_op jit(solution)/shard_map/ppermute | solution.py:855
  13.5 0.0 collective-permute-start.6
  13.5 0.0 copy-done
  13.5 2.9 %inner.1 = (f32[512,128]{1,0:T(8,128)S(1)}, f32[6,6,8,128]{3,2,1,0:T(8,128)S(1)}, f32[5,6,8,128]{3,2,1,0:T(8,128)S(1)}, f32[7,4,8,128]{3,2,1,0:T(8,128)S(1)}, f32[4,7,16,128]{3,2,1,0:T(8,128)S(1)}) custom-call(bf16[4,16,128]{2,1,0:T(8,128)(2,1)S(1)} %collective-permute-done.2.refs_2_.refs_0_, bf16[4,16,128]{2,1,0:T(8,128)(2,1)S(1)} %collective-permute-done.1.refs_1_, ...), custom_call_target="tpu_custom_call" | custom-call | flops 20000000 | bytes 12000000 | tf_op jit(solution)/shard_map/inner/pallas_call | solution.py:940
  16.5 0.5 %collective-permute-done.5.r1 = bf16[33,16,128]{2,1,0:T(8,128)(2,1)S(1)} collective-permute-done((bf16[33,16,128]{2,1,0:T(8,128)(2,1)S(1)}, bf16[33,16,128]{2,1,0:T(8,128)(2,1)S(1)}, u32[]{:S(2)}, u32[]{:S(2)}) %collective-permute-start.5) | collective-permute-done | bytes 135200 | tf_op jit(solution)/shard_map/ppermute | solution.py:855
  17.0 0.0 collective-permute-done.6.r2
  17.0 2.8 %finish.1 = (f32[512,128]{1,0:T(8,128)}, f32[4,8,128]{2,1,0:T(8,128)}) custom-call(bf16[33,16,128]{2,1,0:T(8,128)(2,1)S(1)} %get-tuple-element.27.y1, bf16[33,16,128]{2,1,0:T(8,128)(2,1)S(1)} %get-tuple-element.28.y2, bf16[33,16,128]{2,1,0:T(8,128)(2,1)S(1)} %collective-permute-done.5.r1, bf16[33,16,128]{2,1,0:T(8,128)(2,1)S(1)} %collective-permute-done.6.r2, ...), custom_call_target="tpu_custom_call" | custom-call | tf_op jit(solution)/shard_map/finish/pallas_call | solution.py:964
Async XLA Ops:
  2.2 9.0 %collective-permute-start.3 = (bf16[52,16,128]{2,1,0:T(8,128)(2,1)S(1)}, bf16[52,16,128]{2,1,0:T(8,128)(2,1)S(1)}, u32[]{:S(2)}, u32[]{:S(2)}) collective-permute-start(bf16[52,16,128]{2,1,0:T(8,128)(2,1)S(1)} %get-tuple-element.22), channel_id=1, source_target_pairs={{0,1},{1,0},{8,16},{9,17},{16,8},{17,9},{24,25},{25,24},{2,3},{3,2... | collective-permute-start | bytes 638984 | tf_op jit(solution)/shard_map/ppermute | solution.py:855
  5.2 6.0 %collective-permute-start.4 = (bf16[52,16,128]{2,1,0:T(8,128)(2,1)S(1)}, bf16[52,16,128]{2,1,0:T(8,128)(2,1)S(1)}, u32[]{:S(2)}, u32[]{:S(2)}) collective-permute-start(bf16[52,16,128]{2,1,0:T(8,128)(2,1)S(1)} %get-tuple-element.23), channel_id=1, source_target_pairs={{0,8},{1,9},{8,0},{9,1},{16,24},{17,25},{24,16},{25,17},{2,10},{3,... | collective-permute-start | bytes 638984 | tf_op jit(solution)/shard_map/ppermute | solution.py:855
  5.4 4.0 %collective-permute-start = (bf16[4,16,128]{2,1,0:T(8,128)(2,1)S(1)}, bf16[4,16,128]{2,1,0:T(8,128)(2,1)S(1)}, u32[]{:S(2)}, u32[]{:S(2)}) collective-permute-start(bf16[4,16,128]{2,1,0:T(8,128)(2,1)S(1)} %get-tuple-element.19), channel_id=1, source_target_pairs={{0,1},{1,0},{8,17},{9,16},{16,9},{17,8},{24,25},{25,24},{2,3},{3,2... | collective-permute-start | bytes 49160 | tf_op jit(solution)/shard_map/ppermute | solution.py:855
  6.9 3.2 %collective-permute-start.1 = (bf16[4,16,128]{2,1,0:T(8,128)(2,1)S(1)}, bf16[4,16,128]{2,1,0:T(8,128)(2,1)S(1)}, u32[]{:S(2)}, u32[]{:S(2)}) collective-permute-start(bf16[4,16,128]{2,1,0:T(8,128)(2,1)S(1)} %get-tuple-element.20), channel_id=1, source_target_pairs={{0,9},{1,8},{8,1},{9,0},{16,25},{17,24},{24,17},{25,16},{2,11},{3,... | collective-permute-start | bytes 49160 | tf_op jit(solution)/shard_map/ppermute | solution.py:855
  7.5 3.7 %collective-permute-start.2 = (bf16[4,16,128]{2,1,0:T(8,128)(2,1)S(1)}, bf16[4,16,128]{2,1,0:T(8,128)(2,1)S(1)}, u32[]{:S(2)}, u32[]{:S(2)}) collective-permute-start(bf16[4,16,128]{2,1,0:T(8,128)(2,1)S(1)} %get-tuple-element.21), channel_id=1, source_target_pairs={{0,1},{1,0},{8,9},{9,8},{16,17},{17,16},{24,25},{25,24},{2,3},{3,2... | collective-permute-start | bytes 49160 | tf_op jit(solution)/shard_map/ppermute | solution.py:855
  11.2 2.3 %copy-start = (f32[6,4,8,128]{3,2,1,0:T(8,128)S(1)}, f32[6,4,8,128]{3,2,1,0:T(8,128)}, u32[]{:S(2)}) copy-start(f32[6,4,8,128]{3,2,1,0:T(8,128)} %refs_6_.1) | copy-start | bytes 294916
  11.9 5.1 %collective-permute-start.5 = (bf16[33,16,128]{2,1,0:T(8,128)(2,1)S(1)}, bf16[33,16,128]{2,1,0:T(8,128)(2,1)S(1)}, u32[]{:S(2)}, u32[]{:S(2)}) collective-permute-start(bf16[33,16,128]{2,1,0:T(8,128)(2,1)S(1)} %get-tuple-element.27.y1), channel_id=1, source_target_pairs={{0,2},{1,3},{2,0},{3,1},{4,6},{5,7},{6,4},{7,5},{8,10},{9,11},{10,... | collective-permute-start | bytes 405512 | tf_op jit(solution)/shard_map/ppermute | solution.py:855
  13.5 3.4 %collective-permute-start.6 = (bf16[33,16,128]{2,1,0:T(8,128)(2,1)S(1)}, bf16[33,16,128]{2,1,0:T(8,128)(2,1)S(1)}, u32[]{:S(2)}, u32[]{:S(2)}) collective-permute-start(bf16[33,16,128]{2,1,0:T(8,128)(2,1)S(1)} %get-tuple-element.28.y2), channel_id=1, source_target_pairs={{0,8},{2,4},{4,2},{6,14},{8,0},{10,12},{12,10},{14,6},{16,24},{18,... | collective-permute-start | bytes 405512 | tf_op jit(solution)/shard_map/ppermute | solution.py:855
